TPU v7x, 32 devices: a whole 2x2x4 slice. The times are simulated.
32 devices in a mesh: dom: 2 (over y), col: 4 (over z), row: 2 (over x), sub: 2 (over core).
Axes of the slice: x: 2, y: 2, z: 4, core: 2. Of those that a mesh axis runs over, the one named last changes fastest.
Arguments:
- blocks: float32 [8, 4, 16, 256, 256], P(('dom', 'row', 'sub'), 'col'), parts along dimension 0, may hold values from -6 to 6
- block_slot: int32 [8, 4, 16], P(('dom', 'row', 'sub'), 'col'), parts along dimension 0, may hold values from 0 to 31, as said below
- basis_in: float32 [16, 16384], P(None, ('dom', 'col', 'row', 'sub')), parts along dimension 1, may hold values from -6 to 6
Outputs:
- basis_out: float32 [16, 16384], P(None, ('dom', 'col', 'row', 'sub')), parts along dimension 1
- factor: float32 [32, 16], P('dom'), parts along dimension 0
There are 2 independent parts, one for each index of `dom`. A program takes and returns all parts, laid end to end along the dimension named above; each array names one. Nothing has to cross between parts.
Inputs may be any that keep to these rules, and one draw needn't show every extreme that they name: `block_slot`: within one device's 16 entries all slots differ; every device holds slot 0 and slot 31.
All inputs are finite; a program needn't handle non-finite values.
Results may differ from a plain program's by a relative error of at most 0.0003.
Values sent between devices are 32-bit elements; how exact they have to be, the bound alone decides.
No kernel may reach another device: no remote copies, remote signals or barrier semaphores. Data moves between devices by JAX's collectives and lax.ppermute only.
A program may use at most 64 MiB of HBM per device.

v0:
```python
import jax
import jax.numpy as jnp
from jax import lax
from jax.sharding import PartitionSpec as P

RBL = 4


PRECISION_LEVEL = lax.Precision.HIGHEST


def one_hots(slot, row_count, column_count):
    rowb = slot // column_count
    colb = slot % column_count
    row_hot = (rowb[:, None] == jnp.arange(row_count, dtype=jnp.int32)[None, :]).astype(jnp.float32)
    column_onehot = (colb[:, None] == jnp.arange(column_count, dtype=jnp.int32)[None, :]).astype(
        jnp.float32
    )
    return (row_hot, column_onehot)


def body(blocks, block_slot, basis_in):
    basis_vectors = basis_in.shape[0]
    block_width = blocks.shape[-1]
    nblk = blocks.shape[2]
    stored_block = blocks.reshape(nblk, block_width, block_width)
    slot = block_slot.reshape(nblk)
    whole_matrix = lax.all_gather(basis_in, ("row", "sub"), axis=1, tiled=True)
    column_count = whole_matrix.shape[1] // block_width
    row_count = RBL
    row_hot, column_onehot = one_hots(slot, row_count, column_count)
    vector_select = jnp.einsum(
        "fte,rt->fre",
        whole_matrix.reshape(basis_vectors, column_count, block_width),
        column_onehot,
        precision=PRECISION_LEVEL,
    )
    block_product = jnp.einsum(
        "dvc,vyc->dvy", vector_select, stored_block, precision=PRECISION_LEVEL
    )
    ypart = jnp.einsum("kbi,br->kri", block_product, row_hot, precision=PRECISION_LEVEL).reshape(
        basis_vectors, row_count * block_width
    )
    yrow = lax.psum(ypart, "col")
    ysel = jnp.einsum(
        "kri,br->kbi",
        yrow.reshape(basis_vectors, row_count, block_width),
        row_hot,
        precision=PRECISION_LEVEL,
    )
    back = jnp.einsum("kbi,bij->kbj", ysel, stored_block, precision=PRECISION_LEVEL)
    zpart = jnp.einsum("kbj,bc->kcj", back, column_onehot, precision=PRECISION_LEVEL).reshape(
        basis_vectors, column_count * block_width
    )
    totals = lax.psum(zpart, ("row", "sub"))
    gram = lax.psum(jnp.dot(totals, totals.T, precision=PRECISION_LEVEL), "col")
    share = totals.shape[1] // lax.axis_size(("row", "sub"))
    owned = lax.dynamic_slice_in_dim(totals, lax.axis_index(("row", "sub")) * share, share, 1)
    lower = jnp.linalg.cholesky(gram)
    total_cols = owned.shape[1] * lax.axis_size(("col", "row", "sub"))
    solved = lax.linalg.triangular_solve(lower, owned, left_side=True, lower=True)
    basis_out = solved * jnp.sqrt(jnp.float32(total_cols))
    return (basis_out, lower.T)


def solution(mesh):
    in_specs = (
        P(("dom", "row", "sub"), "col", None, None, None),
        P(("dom", "row", "sub"), "col", None),
        P(None, ("dom", "col", "row", "sub")),
    )
    out_specs = (P(None, ("dom", "col", "row", "sub")), P("dom", None))
    return jax.shard_map(body, mesh=mesh, in_specs=in_specs, out_specs=out_specs, check_vma=False)
```

profile of v0, /device:TPU:0, one launch (start us, length us, event | category | flops | bytes accessed | tf_op | source)
XLA Modules:
  0.0 121.8 jit_solution(8953731324654902076)
XLA Ops:
  7.2 0.0 all-reduce.3.cloned.1.call-start
  7.2 0.7 and_select_fusion
  7.9 6.7 %all_gather.3 = f32[16,2048]{1,0:T(8,128)S(1)} all-gather(f32[16,512]{1,0:T(8,128)} %param.5), channel_id=1, replica_groups=mesh['dom'=2,'col'=4,'row'=2,'sub'=2] {'row','sub'}, dimensions={1}, use_global_device_ids=true | all-gather | bytes 163840 | tf_op jit(solution)/shard_map/all_gather | solution.py:28
  14.6 0.3 fusion.29
  14.9 5.8 %fusion.4 = f32[16,16,256]{2,0,1:T(8,128)S(1)} fusion(f32[1,1,16,256,256]{4,3,2,1,0:T(8,128)} %param.3, f32[16,16,256]{2,0,1:T(8,128)S(1)} %fusion.29), kind=kOutput, calls=%fused_computation.4 | convolution fusion | flops 201326592 | bytes 4718592 | tf_op jit(solution)/shard_map/dvc,vyc->dvy/dot_general | solution.py:38
  20.7 0.4 fusion.13
  21.2 0.6 copy.34
  21.8 0.0 all-reduce.3.cloned.1.call-update
  21.8 0.0 all-reduce.5.cloned.1.call-start
  21.9 35.8 %all-reduce.3.cloned.1.call-done = f32[16,4,256]{2,0,1:T(8,128)} async-done(((f32[16,4,256]{2,0,1:T(8,128)}), f32[16,4,256]{2,0,1:T(8,128)}) %all-reduce.3.cloned.1.call-update) | async-done | bytes 65552 | tf_op jit(solution)/shard_map/psum | solution.py:44
  57.6 1.1 fusion.16
  58.8 4.4 %fusion = f32[16,16,256]{2,1,0:T(8,128)S(1)} fusion(f32[1,1,16,256,256]{4,3,2,1,0:T(8,128)} %param.3, f32[16,16,256]{2,0,1:T(8,128)S(1)} %fusion.16), kind=kOutput, calls=%fused_computation | convolution fusion | flops 201326592 | bytes 4718592 | tf_op jit(solution)/shard_map/kbi,bij->kbj/dot_general | solution.py:51
  63.2 0.4 fusion.7
  63.6 0.7 copy.16
  64.3 0.0 all-reduce.5.cloned.1.call-update
  64.3 31.2 %all-reduce.5.cloned.1.call-done = f32[16,2048]{1,0:T(8,128)} async-done(((f32[16,2048]{1,0:T(8,128)}), f32[16,2048]{1,0:T(8,128)}) %all-reduce.5.cloned.1.call-update) | async-done | bytes 131088 | tf_op jit(solution)/shard_map/psum | solution.py:55
  95.5 1.2 fusion.34
  96.7 11.9 %psum.23 = f32[16,16]{0,1:T(8,128)S(1)} all-reduce(f32[16,16]{0,1:T(8,128)S(1)} %fusion.34), channel_id=1, replica_groups=mesh['dom'=2,'col'=4,'row'=2,'sub'=2] {'col'}, use_global_device_ids=true, to_apply=%region_2.3 | all-reduce | flops 256 | bytes 2048 | tf_op jit(solution)/shard_map/psum | solution.py:56
  108.6 0.1 copy.6
  108.7 1.5 %cholesky.16 = f32[16,16]{1,0:T(8,128)S(1)} custom-call(f32[16,16]{1,0:T(8,128)S(1)} %fusion.20), custom_call_target="Cholesky" | custom-call | tf_op jit(solution)/shard_map/jit(cholesky)/cholesky | solution.py:59
  110.2 0.6 compare_reduce_fusion
  110.8 0.6 fusion.24
  111.5 1.2 %custom-call.6 = f32[1,16,16]{1,2,0:T(8,128)S(1)} custom-call(f32[1,16,16]{2,1,0:T(8,128)S(1)} %get-tuple-element.5), custom_call_target="InvertDiagBlocksLowerTriangular" | custom-call | tf_op jit(solution)/shard_map/triangular_solve | solution.py:61
  112.7 0.7 copy.7
  113.4 1.6 %convolution_multiply_fusion = f32[16,512]{1,0:T(8,128)} fusion(f32[16,2048]{1,0:T(8,128)} %all-reduce.5.cloned.1.call-done, s32[]{:T(128)S(6)} %select_n.30, f32[1,16,16]{1,2,0:T(8,128)S(1)} %custom-call.6), kind=kOutput, calls=%fused_computation.5 | convolution fusion | flops 1581056 | bytes 66564 | tf_op jit(solution)/shard_map/triangular_solve | solution.py:61
  (3 shorter events, 0.1 us)
Async XLA Ops:
  7.2 50.5 %all-reduce.3.cloned.1.call-start = ((), (), s32[]{:S(2)}) async-start(), calls=%async_computation | async-start | bytes 131072 | tf_op jit(solution)/shard_map/psum | solution.py:44
  21.8 73.7 %all-reduce.5.cloned.1.call-start = ((), (), s32[]{:S(2)}) async-start(), calls=%async_computation.1 | async-start | bytes 262144 | tf_op jit(solution)/shard_map/psum | solution.py:55
Sparse Core Ops, SparseCore 0:
  21.9 35.6 all-reduce.2
  64.4 31.0 all-reduce.4
where the time goes:
time: 122 us
  waiting for transfers between devices  67 us (55%)
  blocking collectives  18.6 us (15%)
  matrix products  15.3 us (13%)
  between operations  14.1 us (12%)
  other arithmetic  4.68 us (4%)
  local copies, waits for them, and re-layouts  2.12 us (2%)
    psum x1, waiting for transfers between devices, body(): yrow = lax.psum(ypart, 'col')  35.8 us
    psum x1, waiting for transfers between devices, body(): totals = lax.psum(zpart, ('row', 'sub'))  31.2 us
    psum x1, blocking collectives, body(): gram = lax.psum(jnp.dot(totals, totals.T, precision=PRECISION_LEVEL), 'col')  11.9 us
    all_gather x1, blocking collectives, body(): whole_matrix = lax.all_gather(basis_in, ('row', 'sub'), axis=1, tiled=True)  6.68 us
    dot_general x1, matrix products, body(): jnp.einsum('dvc,vyc->dvy', vector_select, stored_block, precision=PRECISI...  5.8 us
    dot_general x1, matrix products, body(): jnp.einsum('kbi,bij->kbj', ysel, stored_block, precision=PRECISION_LEVEL)  4.43 us
  transfers between devices with their start and end apart: 2, of which 2 were waited for; matrix products, arithmetic and copies ran while one was open for 0% of the time, Pallas kernels for 0%

commit v1 on v0

v1 whole, which is shorter than its diff:
```python
import math

import jax
import jax.numpy as jnp
from jax import lax
from jax.experimental import pallas as pl
from jax.experimental.pallas import tpu as pltpu
from jax.sharding import PartitionSpec as P

RBL = 4
GROUP = ("row", "sub")
VMEM_LIMIT = 24 * 1024 * 1024

NT = (((1,), (1,)), ((), ()))
NN = (((1,), (0,)), ((), ()))


def params():
    return pltpu.CompilerParams(vmem_limit_bytes=VMEM_LIMIT)


def vmem():
    return pl.BlockSpec(memory_space=pltpu.VMEM)


def smem():
    return pl.BlockSpec(memory_space=pltpu.SMEM)


def halves(x):
    high = x.astype(jnp.bfloat16)
    low = (x - high.astype(jnp.float32)).astype(jnp.bfloat16)
    return high, low


def split_kernel(blocks_ref, high_ref, low_ref):
    for i in range(blocks_ref.shape[0]):
        high_ref[i], low_ref[i] = halves(blocks_ref[i])


def split_blocks(blocks):
    n, rows, cols = blocks.shape
    return pl.pallas_call(
        split_kernel,
        out_shape=(
            pltpu.VMEM(blocks.shape, jnp.bfloat16),
            pltpu.VMEM(blocks.shape, jnp.bfloat16),
        ),
        in_specs=[vmem()],
        out_specs=(vmem(), vmem()),
        compiler_params=params(),
        cost_estimate=pl.CostEstimate(flops=3 * n * rows * cols, bytes_accessed=8 * n * rows * cols, transcendentals=0),
    )(blocks)


def store_halves(ref, index, x):
    count = x.shape[0]
    high, low = halves(x)
    ref[index, pl.ds(0, count)] = high
    ref[index, pl.ds(count, count)] = low


def product(pair, high, low, dims):
    count = pair.shape[0] // 2
    first = lax.dot_general(pair, high, dims, preferred_element_type=jnp.float32)
    second = lax.dot_general(pair[:count], low, dims, preferred_element_type=jnp.float32)
    return first[:count] + first[count:] + second


def rows_kernel(slot_ref, high_ref, low_ref, *refs):
    pieces, out_ref, pair_ref = refs[:-2], refs[-2], refs[-1]
    nblk, edge = high_ref.shape[0], high_ref.shape[1]
    per_piece = pieces[0].shape[1] // edge
    column_count = per_piece * len(pieces)
    me = lax.axis_index(GROUP)
    for k, piece in enumerate(pieces):
        for h in range(per_piece):
            store_halves(pair_ref, (me ^ k) * per_piece + h, piece[:, h * edge:(h + 1) * edge])
    out_ref[...] = jnp.zeros_like(out_ref)
    for b in range(nblk):
        slot = slot_ref[b]
        r, c = slot // column_count, slot % column_count
        out_ref[r] += product(pair_ref[c], high_ref[b], low_ref[b], NT)


def rows_product(slot, high, low, pieces):
    count = pieces[0].shape[0]
    nblk, edge = high.shape[0], high.shape[1]
    column_count = len(pieces) * pieces[0].shape[1] // edge
    return pl.pallas_call(
        rows_kernel,
        out_shape=jax.ShapeDtypeStruct((RBL, count, edge), jnp.float32),
        in_specs=[smem()] + [vmem()] * (2 + len(pieces)),
        out_specs=vmem(),
        scratch_shapes=[pltpu.VMEM((column_count, 2 * count, edge), jnp.bfloat16)],
        compiler_params=params(),
    )(slot, high, low, *pieces)


def cols_kernel(column_count, slot_ref, high_ref, low_ref, *refs):
    pieces, out_ref, pair_ref = refs[:-2], refs[-2], refs[-1]
    nblk = high_ref.shape[0]
    for r in range(RBL):
        total = pieces[0][r]
        for piece in pieces[1:]:
            total = total + piece[r]
        store_halves(pair_ref, r, total)
    out_ref[...] = jnp.zeros_like(out_ref)
    for b in range(nblk):
        slot = slot_ref[b]
        r, c = slot // column_count, slot % column_count
        out_ref[c] += product(pair_ref[r], high_ref[b], low_ref[b], NN)


def cols_product(slot, high, low, pieces, column_count):
    _, count, edge = pieces[0].shape
    return pl.pallas_call(
        lambda *refs: cols_kernel(column_count, *refs),
        out_shape=jax.ShapeDtypeStruct((column_count, count, edge), jnp.float32),
        in_specs=[smem()] + [vmem()] * (2 + len(pieces)),
        out_specs=vmem(),
        scratch_shapes=[pltpu.VMEM((RBL, 2 * count, edge), jnp.bfloat16)],
        compiler_params=params(),
    )(slot, high, low, *pieces)


def gram_kernel(a_ref, b_ref, z_ref, gram_ref):
    total = None
    for c in range(a_ref.shape[0]):
        z = a_ref[c] + b_ref[c]
        z_ref[c] = z
        g = lax.dot_general(z, z, NT, precision=lax.Precision.HIGHEST, preferred_element_type=jnp.float32)
        total = g if total is None else total + g
    gram_ref[...] = total


def gram_of(a, b):
    count = a.shape[1]
    return pl.pallas_call(
        gram_kernel,
        out_shape=(
            jax.ShapeDtypeStruct(a.shape, jnp.float32),
            jax.ShapeDtypeStruct((count, count), jnp.float32),
        ),
        in_specs=[vmem(), vmem()],
        out_specs=(vmem(), vmem()),
        compiler_params=params(),
    )(a, b)


def solve_kernel(scale, z_ref, *refs):
    grams, out_ref, factor_ref = refs[:-2], refs[-2], refs[-1]
    count = factor_ref.shape[0]
    per_share = out_ref.shape[1] // z_ref.shape[2]
    first = lax.axis_index(GROUP) * per_share
    g = grams[0][...]
    for piece in grams[1:]:
        g = g + piece[...]
    z = [z_ref[first + h] * scale for h in range(per_share)]
    row_id = lax.broadcasted_iota(jnp.int32, (count, count), 0)
    col_id = lax.broadcasted_iota(jnp.int32, (count, count), 1)
    factor = jnp.zeros((count, count), jnp.float32)
    edge = z_ref.shape[2]
    row_wide = lax.broadcasted_iota(jnp.int32, (count, edge), 0)
    done = [jnp.zeros_like(x) for x in z]
    for j in range(count):
        inverse = lax.rsqrt(g[j:j + 1, j:j + 1])
        row = g[j:j + 1, :] * inverse
        column = g[:, j:j + 1] * inverse
        factor = jnp.where((row_id == j) & (col_id >= j), row, factor)
        rows = [x[j:j + 1, :] * inverse for x in z]
        done = [jnp.where(row_wide == j, x, d) for x, d in zip(rows, done)]
        if j + 1 < count:
            g = g - column * row
            z = [x - column * y for x, y in zip(z, rows)]
    for h in range(per_share):
        out_ref[:, h * edge:(h + 1) * edge] = done[h]
    factor_ref[...] = factor


def solve(z, grams, share, scale):
    count = z.shape[1]
    return pl.pallas_call(
        lambda *refs: solve_kernel(scale, *refs),
        out_shape=(
            jax.ShapeDtypeStruct((count, share), jnp.float32),
            jax.ShapeDtypeStruct((count, count), jnp.float32),
        ),
        in_specs=[vmem()] * (1 + len(grams)),
        out_specs=(vmem(), vmem()),
        compiler_params=params(),
    )(z, *grams)


def partner(x, axes, k):
    n = lax.axis_size(axes)
    return lax.ppermute(x, axes, [(i, i ^ k) for i in range(n)])


def is_power(n):
    return n & (n - 1) == 0


def gather(x, axes):
    n = lax.axis_size(axes)
    return [x] + [partner(x, axes, k) for k in range(1, n)]


def to_sum(x, axis):
    n = lax.axis_size(axis)
    if n <= 4 and is_power(n):
        return gather(x, axis)
    return [lax.psum(x, axis)]


def body(blocks, block_slot, basis_in):
    edge = blocks.shape[-1]
    nblk = blocks.shape[2]
    share = basis_in.shape[1]
    column_count = share * lax.axis_size(GROUP) // edge
    slot = block_slot.reshape(nblk)
    high, low = split_blocks(blocks.reshape(nblk, edge, edge))
    high = pltpu.with_memory_space_constraint(high, pltpu.VMEM)
    low = pltpu.with_memory_space_constraint(low, pltpu.VMEM)
    ypart = rows_product(slot, high, low, gather(basis_in, GROUP))
    zpart = cols_product(slot, high, low, to_sum(ypart, "col"), column_count)
    rounds = [(axis, 1 << i) for axis in reversed(GROUP) for i in range(int(math.log2(lax.axis_size(axis))))]
    for axis, k in rounds[:-1]:
        zpart = zpart + partner(zpart, axis, k)
    z, gram = gram_of(zpart, partner(zpart, *rounds[-1]))
    scale = math.sqrt(share * lax.axis_size(("col",) + GROUP))
    return solve(z, to_sum(gram, "col"), share, scale)


def solution(mesh):
    in_specs = (
        P(("dom", "row", "sub"), "col", None, None, None),
        P(("dom", "row", "sub"), "col", None),
        P(None, ("dom", "col", "row", "sub")),
    )
    out_specs = (P(None, ("dom", "col", "row", "sub")), P("dom", None))
    return jax.shard_map(body, mesh=mesh, in_specs=in_specs, out_specs=out_specs, check_vma=False)
```

time: 122 us -> 36.4 us (0.30)
  waiting for transfers between devices: 67 us -> 14.2 us
  blocking collectives: 18.6 us -> 0 us
  matrix products: 15.3 us -> 0 us
  between operations: 14.1 us -> 0.67 us
  starting transfers between devices: 0.08 us -> 13.3 us
  Pallas kernels: 0 us -> 5.84 us
  other arithmetic: 4.68 us -> 0.02 us
    psum x2 -> x0, waiting for transfers between devices: 67 us -> none  [the longest x1 35.8 us: body(): yrow = lax.psum(ypart, 'col')]
    ppermute x0 -> x11, waiting for transfers between devices: none -> 14.2 us  [partner(): return lax.ppermute(x, axes, [(i, i ^ k) for i in range(n)])]
    dot_general x7 -> x0, matrix products: 13.7 us -> none  [the longest x1 5.8 us: body(): jnp.einsum('dvc,vyc->dvy', vector_select, stored_block, precision=PRECISI...]
    ppermute x0 -> x11, starting transfers between devices: none -> 13.3 us  [partner(): return lax.ppermute(x, axes, [(i, i ^ k) for i in range(n)])]
    psum x1 -> x0, blocking collectives: 11.9 us -> none  [body(): gram = lax.psum(jnp.dot(totals, totals.T, precision=PRECISION_LEVEL), 'col')]
    all_gather x1 -> x0, blocking collectives: 6.68 us -> none  [body(): whole_matrix = lax.all_gather(basis_in, ('row', 'sub'), axis=1, tiled=True)]
    pallas_call x0 -> x5, Pallas kernels: none -> 5.84 us  [the longest x1 1.86 us: solve(): pl.pallas_call(lambda *refs: solve_kernel(scale, *refs), out_shape=(jax.S...]
    another operation x4 -> x0, other arithmetic: 3.36 us -> none  [the longest x3 2.13 us: body(): lower = jnp.linalg.cholesky(gram)]
  transfers between devices with their start and end apart: 2 -> 11, of which waited for: 2 -> 7; matrix products, arithmetic and copies ran while one was open for 0% -> 0% of each run, Pallas kernels for 0% -> 2%
where the time goes in v1:
time: 36.4 us; the launch traced here: 36.2 us
  waiting for transfers between devices  14.2 us (39%)
  starting transfers between devices  13.3 us (37%)
  Pallas kernels  5.84 us (16%)
  local copies, waits for them, and re-layouts  2.19 us (6%)
  between operations  0.67 us (2%)
    ppermute x11, waiting for transfers between devices, partner(): return lax.ppermute(x, axes, [(i, i ^ k) for i in range(n)])  14.2 us
    ppermute x11, starting transfers between devices, partner(): return lax.ppermute(x, axes, [(i, i ^ k) for i in range(n)])  13.3 us
    unnamed x6, local copies, waits for them, and re-layouts  2.19 us
    pallas_call x1, Pallas kernels, solve(): pl.pallas_call(lambda *refs: solve_kernel(scale, *refs), out_shape=(jax.S...  1.86 us
    pallas_call x1, Pallas kernels, rows_product(): pl.pallas_call(rows_kernel, out_shape=jax.ShapeDtypeStruct((RBL, count, e...  1.78 us
    pallas_call x1, Pallas kernels, cols_product(): pl.pallas_call(lambda *refs: cols_kernel(column_count, *refs), out_shape=...  1.27 us
  transfers between devices with their start and end apart: 11, of which 7 were waited for; matrix products, arithmetic and copies ran while one was open for 0% of the time, Pallas kernels for 2%

profile of v1, /device:TPU:0, one launch (start us, length us, event | category | flops | bytes accessed | tf_op | source)
XLA Modules:
  0.0 36.2 jit_solution(11325414039009318497)
XLA Ops:
  0.6 3.0 %collective-permute-start.1 = (f32[16,512]{1,0:T(8,128)}, f32[16,512]{1,0:T(8,128)S(1)}, u32[]{:S(2)}, u32[]{:S(2)}) collective-permute-start(f32[16,512]{1,0:T(8,128)} %refs_0_.1), channel_id=1, source_target_pairs={{0,2},{1,3},{2,0},{3,1},{4,6},{5,7},{6,4},{7,5},{8,10},{9,11},{10,... | collective-permute-start | bytes 98312 | tf_op jit(solution)/shard_map/ppermute | solution.py:197
  3.6 0.0 collective-permute-start
  3.6 0.2 collective-permute-start.2
  3.8 0.0 copy-start
  3.8 2.2 %copy-done = f32[1,1,16,256,256]{4,3,2,1,0:T(8,128)S(1)} copy-done((f32[1,1,16,256,256]{4,3,2,1,0:T(8,128)S(1)}, f32[1,1,16,256,256]{4,3,2,1,0:T(8,128)}, u32[]{:S(2)}) %copy-start) | copy-done | bytes 4194328
  6.0 0.0 copy-start.1
  6.0 0.0 copy-start.2
  6.0 0.6 %shard_map.50 = (bf16[16,256,256]{2,1,0:T(8,128)(2,1)S(1)}, bf16[16,256,256]{2,1,0:T(8,128)(2,1)S(1)}) custom-call(f32[16,256,256]{2,1,0:T(8,128)S(1)} %bitcast.2), custom_call_target="tpu_custom_call" | custom-call | flops 3145728 | bytes 8388608 | tf_op jit(solution)/shard_map/pallas_call | solution.py:43
  6.7 0.0 collective-permute-done.1.refs_2_
  6.7 0.0 collective-permute-done.refs_1_
  6.7 0.5 %collective-permute-done.2.refs_3_ = f32[16,512]{1,0:T(8,128)S(1)} collective-permute-done((f32[16,512]{1,0:T(8,128)}, f32[16,512]{1,0:T(8,128)S(1)}, u32[]{:S(2)}, u32[]{:S(2)}) %collective-permute-start.2) | collective-permute-done | bytes 32800 | tf_op jit(solution)/shard_map/ppermute | solution.py:197
  7.2 0.0 copy-done.1
  7.2 0.0 copy-done.2
  7.2 1.8 %shard_map.51.refs_3_ = f32[4,16,256]{2,1,0:T(8,128)S(1)} custom-call(s32[16]{0:T(128)S(1)} %bitcast.3, bf16[16,256,256]{2,1,0:T(8,128)(2,1)S(1)} %get-tuple-element.6.high_ref.refs_1_, bf16[16,256,256]{2,1,0:T(8,128)(2,1)S(1)} %get-tuple-element.7.low_ref.refs_2_, f32[16,512]{1,0:T(8,128)S(1)} %copy-done.1, f32[16,512]{1,0:T(8,128)S(1)} %collective-permute-done.refs_1_, ...), custom_call_target="tpu_custom_call" | custom-call | tf_op jit(solution)/shard_map/pallas_call | solution.py:90
  9.0 3.7 %collective-permute-start.5 = (f32[4,16,256]{2,1,0:T(8,128)S(1)}, f32[4,16,256]{2,1,0:T(8,128)S(1)}, u32[]{:S(2)}, u32[]{:S(2)}) collective-permute-start(f32[4,16,256]{2,1,0:T(8,128)S(1)} %shard_map.51.refs_3_), channel_id=1, source_target_pairs={{0,12},{4,8},{8,4},{12,0},{1,13},{5,9},{9,5},{13,1},{2,14},{6,10},... | collective-permute-start | bytes 196616 | tf_op jit(solution)/shard_map/ppermute | solution.py:197
  12.6 0.0 collective-permute-start.4
  12.6 0.7 %collective-permute-start.3 = (f32[4,16,256]{2,1,0:T(8,128)S(1)}, f32[4,16,256]{2,1,0:T(8,128)S(1)}, u32[]{:S(2)}, u32[]{:S(2)}) collective-permute-start(f32[4,16,256]{2,1,0:T(8,128)S(1)} %shard_map.51.refs_3_), channel_id=1, source_target_pairs={{0,4},{4,0},{8,12},{12,8},{1,5},{5,1},{9,13},{13,9},{2,6},{6,2},{1... | collective-permute-start | bytes 196616 | tf_op jit(solution)/shard_map/ppermute | solution.py:197
  13.4 2.2 %collective-permute-done.5.refs_6_ = f32[4,16,256]{2,1,0:T(8,128)S(1)} collective-permute-done((f32[4,16,256]{2,1,0:T(8,128)S(1)}, f32[4,16,256]{2,1,0:T(8,128)S(1)}, u32[]{:S(2)}, u32[]{:S(2)}) %collective-permute-start.5) | collective-permute-done | bytes 65568 | tf_op jit(solution)/shard_map/ppermute | solution.py:197
  15.6 3.2 %collective-permute-done.4.refs_5_ = f32[4,16,256]{2,1,0:T(8,128)S(1)} collective-permute-done((f32[4,16,256]{2,1,0:T(8,128)S(1)}, f32[4,16,256]{2,1,0:T(8,128)S(1)}, u32[]{:S(2)}, u32[]{:S(2)}) %collective-permute-start.4) | collective-permute-done | bytes 65568 | tf_op jit(solution)/shard_map/ppermute | solution.py:197
  18.7 0.0 collective-permute-done.3.refs_4_
  18.7 1.3 %shard_map.52 = f32[8,16,256]{2,1,0:T(8,128)S(1)} custom-call(s32[16]{0:T(128)S(1)} %bitcast.4, bf16[16,256,256]{2,1,0:T(8,128)(2,1)S(1)} %get-tuple-element.6.high_ref.refs_1_, bf16[16,256,256]{2,1,0:T(8,128)(2,1)S(1)} %get-tuple-element.7.low_ref.refs_2_, f32[4,16,256]{2,1,0:T(8,128)S(1)} %shard_map.51.refs_3_, ...), custom_call_target="tpu_custom_call" | custom-call | tf_op jit(solution)/shard_map/pallas_call | solution.py:117
  20.0 0.0 collective-permute-start.6
  20.0 1.3 %collective-permute-done.6 = f32[8,16,256]{2,1,0:T(8,128)S(1)} collective-permute-done((f32[8,16,256]{2,1,0:T(8,128)S(1)}, f32[8,16,256]{2,1,0:T(8,128)S(1)}, u32[]{:S(2)}, u32[]{:S(2)}) %collective-permute-start.6) | collective-permute-done | bytes 131104 | tf_op jit(solution)/shard_map/ppermute | solution.py:197
  21.4 1.2 %collective-permute-start.7 = (f32[8,16,256]{2,1,0:T(8,128)S(1)}, f32[8,16,256]{2,1,0:T(8,128)S(1)}, u32[]{:S(2)}, u32[]{:S(2)}) collective-permute-start(f32[8,16,256]{2,1,0:T(8,128)S(1)} %add.3.a_ref), channel_id=1, source_target_pairs={{0,2},{2,0},{1,3},{3,1},{4,6},{6,4},{5,7},{7,5},{8,10},{10,8},{9,1... | collective-permute-start | bytes 393224 | tf_op jit(solution)/shard_map/ppermute | solution.py:197
  22.6 4.4 %collective-permute-done.7.b_ref = f32[8,16,256]{2,1,0:T(8,128)S(1)} collective-permute-done((f32[8,16,256]{2,1,0:T(8,128)S(1)}, f32[8,16,256]{2,1,0:T(8,128)S(1)}, u32[]{:S(2)}, u32[]{:S(2)}) %collective-permute-start.7) | collective-permute-done | bytes 131104 | tf_op jit(solution)/shard_map/ppermute | solution.py:197
  27.0 0.3 shard_map.53
  27.3 2.5 %collective-permute-start.10 = (f32[16,16]{1,0:T(8,128)S(1)}, f32[16,16]{1,0:T(8,128)S(1)}, u32[]{:S(2)}, u32[]{:S(2)}) collective-permute-start(f32[16,16]{1,0:T(8,128)S(1)} %get-tuple-element.9.refs_1_), channel_id=1, source_target_pairs={{0,12},{4,8},{8,4},{12,0},{1,13},{5,9},{9,5},{13,1},{2,14},{6,10},... | collective-permute-start | bytes 3080 | tf_op jit(solution)/shard_map/ppermute | solution.py:197
  29.8 0.2 collective-permute-start.9
  30.0 1.7 %collective-permute-start.8 = (f32[16,16]{1,0:T(8,128)S(1)}, f32[16,16]{1,0:T(8,128)S(1)}, u32[]{:S(2)}, u32[]{:S(2)}) collective-permute-start(f32[16,16]{1,0:T(8,128)S(1)} %get-tuple-element.9.refs_1_), channel_id=1, source_target_pairs={{0,4},{4,0},{8,12},{12,8},{1,5},{5,1},{9,13},{13,9},{2,6},{6,2},{1... | collective-permute-start | bytes 3080 | tf_op jit(solution)/shard_map/ppermute | solution.py:197
  31.7 1.1 %collective-permute-done.10.refs_4_ = f32[16,16]{1,0:T(8,128)S(1)} collective-permute-done((f32[16,16]{1,0:T(8,128)S(1)}, f32[16,16]{1,0:T(8,128)S(1)}, u32[]{:S(2)}, u32[]{:S(2)}) %collective-permute-start.10) | collective-permute-done | bytes 1056 | tf_op jit(solution)/shard_map/ppermute | solution.py:197
  32.7 1.6 %collective-permute-done.9.refs_3_ = f32[16,16]{1,0:T(8,128)S(1)} collective-permute-done((f32[16,16]{1,0:T(8,128)S(1)}, f32[16,16]{1,0:T(8,128)S(1)}, u32[]{:S(2)}, u32[]{:S(2)}) %collective-permute-start.9) | collective-permute-done | bytes 1056 | tf_op jit(solution)/shard_map/ppermute | solution.py:197
  34.3 0.0 collective-permute-done.8.refs_2_
  34.3 1.9 %shard_map.54 = (f32[16,512]{1,0:T(8,128)}, f32[16,16]{1,0:T(8,128)}) custom-call(f32[8,16,256]{2,1,0:T(8,128)S(1)} %get-tuple-element.8.refs_0_, f32[16,16]{1,0:T(8,128)S(1)} %get-tuple-element.9.refs_1_, f32[16,16]{1,0:T(8,128)S(1)} %collective-permute-done.8.refs_2_, f32[16,16]{1,0:T(8,128)S(1)} %collective-permute-done.9.refs_3_, ...), custom_call_target="tpu_custom_call" | custom-call | tf_op jit(solution)/shard_map/pallas_call | solution.py:183
  (1 shorter events, 0.0 us)
Async XLA Ops:
  0.6 6.1 %collective-permute-start.1 = (f32[16,512]{1,0:T(8,128)}, f32[16,512]{1,0:T(8,128)S(1)}, u32[]{:S(2)}, u32[]{:S(2)}) collective-permute-start(f32[16,512]{1,0:T(8,128)} %refs_0_.1), channel_id=1, source_target_pairs={{0,2},{1,3},{2,0},{3,1},{4,6},{5,7},{6,4},{7,5},{8,10},{9,11},{10,... | collective-permute-start | bytes 98312 | tf_op jit(solution)/shard_map/ppermute | solution.py:197
  3.6 3.1 %collective-permute-start = (f32[16,512]{1,0:T(8,128)}, f32[16,512]{1,0:T(8,128)S(1)}, u32[]{:S(2)}, u32[]{:S(2)}) collective-permute-start(f32[16,512]{1,0:T(8,128)} %refs_0_.1), channel_id=1, source_target_pairs={{0,1},{1,0},{2,3},{3,2},{4,5},{5,4},{6,7},{7,6},{8,9},{9,8},{10,11... | collective-permute-start | bytes 98312 | tf_op jit(solution)/shard_map/ppermute | solution.py:197
  3.6 3.6 %collective-permute-start.2 = (f32[16,512]{1,0:T(8,128)}, f32[16,512]{1,0:T(8,128)S(1)}, u32[]{:S(2)}, u32[]{:S(2)}) collective-permute-start(f32[16,512]{1,0:T(8,128)} %refs_0_.1), channel_id=1, source_target_pairs={{0,3},{1,2},{2,1},{3,0},{4,7},{5,6},{6,5},{7,4},{8,11},{9,10},{10,... | collective-permute-start | bytes 98312 | tf_op jit(solution)/shard_map/ppermute | solution.py:197
  3.8 2.2 %copy-start = (f32[1,1,16,256,256]{4,3,2,1,0:T(8,128)S(1)}, f32[1,1,16,256,256]{4,3,2,1,0:T(8,128)}, u32[]{:S(2)}) copy-start(f32[1,1,16,256,256]{4,3,2,1,0:T(8,128)} %param.3) | copy-start | bytes 12582916
  6.0 1.2 %copy-start.1 = (f32[16,512]{1,0:T(8,128)S(1)}, f32[16,512]{1,0:T(8,128)}, u32[]{:S(2)}) copy-start(f32[16,512]{1,0:T(8,128)} %refs_0_.1) | copy-start | bytes 98308
  6.0 1.2 %copy-start.2 = (s32[1,1,16]{2,1,0:T(1,128)S(1)}, s32[1,1,16]{2,1,0:T(1,128)}, u32[]{:S(2)}) copy-start(s32[1,1,16]{2,1,0:T(1,128)} %param.4) | copy-start | bytes 196
  9.0 6.6 %collective-permute-start.5 = (f32[4,16,256]{2,1,0:T(8,128)S(1)}, f32[4,16,256]{2,1,0:T(8,128)S(1)}, u32[]{:S(2)}, u32[]{:S(2)}) collective-permute-start(f32[4,16,256]{2,1,0:T(8,128)S(1)} %shard_map.51.refs_3_), channel_id=1, source_target_pairs={{0,12},{4,8},{8,4},{12,0},{1,13},{5,9},{9,5},{13,1},{2,14},{6,10},... | collective-permute-start | bytes 196616 | tf_op jit(solution)/shard_map/ppermute | solution.py:197
  12.6 6.1 %collective-permute-start.4 = (f32[4,16,256]{2,1,0:T(8,128)S(1)}, f32[4,16,256]{2,1,0:T(8,128)S(1)}, u32[]{:S(2)}, u32[]{:S(2)}) collective-permute-start(f32[4,16,256]{2,1,0:T(8,128)S(1)} %shard_map.51.refs_3_), channel_id=1, source_target_pairs={{0,8},{4,12},{8,0},{12,4},{1,9},{5,13},{9,1},{13,5},{2,10},{6,14},... | collective-permute-start | bytes 196616 | tf_op jit(solution)/shard_map/ppermute | solution.py:197
  12.6 6.1 %collective-permute-start.3 = (f32[4,16,256]{2,1,0:T(8,128)S(1)}, f32[4,16,256]{2,1,0:T(8,128)S(1)}, u32[]{:S(2)}, u32[]{:S(2)}) collective-permute-start(f32[4,16,256]{2,1,0:T(8,128)S(1)} %shard_map.51.refs_3_), channel_id=1, source_target_pairs={{0,4},{4,0},{8,12},{12,8},{1,5},{5,1},{9,13},{13,9},{2,6},{6,2},{1... | collective-permute-start | bytes 196616 | tf_op jit(solution)/shard_map/ppermute | solution.py:197
  20.0 1.4 %collective-permute-start.6 = (f32[8,16,256]{2,1,0:T(8,128)S(1)}, f32[8,16,256]{2,1,0:T(8,128)S(1)}, u32[]{:S(2)}, u32[]{:S(2)}) collective-permute-start(f32[8,16,256]{2,1,0:T(8,128)S(1)} %shard_map.52), channel_id=1, source_target_pairs={{0,1},{1,0},{2,3},{3,2},{4,5},{5,4},{6,7},{7,6},{8,9},{9,8},{10,11... | collective-permute-start | bytes 393224 | tf_op jit(solution)/shard_map/ppermute | solution.py:197
  21.4 5.6 %collective-permute-start.7 = (f32[8,16,256]{2,1,0:T(8,128)S(1)}, f32[8,16,256]{2,1,0:T(8,128)S(1)}, u32[]{:S(2)}, u32[]{:S(2)}) collective-permute-start(f32[8,16,256]{2,1,0:T(8,128)S(1)} %add.3.a_ref), channel_id=1, source_target_pairs={{0,2},{2,0},{1,3},{3,1},{4,6},{6,4},{5,7},{7,5},{8,10},{10,8},{9,1... | collective-permute-start | bytes 393224 | tf_op jit(solution)/shard_map/ppermute | solution.py:197
  27.3 5.5 %collective-permute-start.10 = (f32[16,16]{1,0:T(8,128)S(1)}, f32[16,16]{1,0:T(8,128)S(1)}, u32[]{:S(2)}, u32[]{:S(2)}) collective-permute-start(f32[16,16]{1,0:T(8,128)S(1)} %get-tuple-element.9.refs_1_), channel_id=1, source_target_pairs={{0,12},{4,8},{8,4},{12,0},{1,13},{5,9},{9,5},{13,1},{2,14},{6,10},... | collective-permute-start | bytes 3080 | tf_op jit(solution)/shard_map/ppermute | solution.py:197
  29.8 4.5 %collective-permute-start.9 = (f32[16,16]{1,0:T(8,128)S(1)}, f32[16,16]{1,0:T(8,128)S(1)}, u32[]{:S(2)}, u32[]{:S(2)}) collective-permute-start(f32[16,16]{1,0:T(8,128)S(1)} %get-tuple-element.9.refs_1_), channel_id=1, source_target_pairs={{0,8},{4,12},{8,0},{12,4},{1,9},{5,13},{9,1},{13,5},{2,10},{6,14},... | collective-permute-start | bytes 3080 | tf_op jit(solution)/shard_map/ppermute | solution.py:197
  30.0 4.4 %collective-permute-start.8 = (f32[16,16]{1,0:T(8,128)S(1)}, f32[16,16]{1,0:T(8,128)S(1)}, u32[]{:S(2)}, u32[]{:S(2)}) collective-permute-start(f32[16,16]{1,0:T(8,128)S(1)} %get-tuple-element.9.refs_1_), channel_id=1, source_target_pairs={{0,4},{4,0},{8,12},{12,8},{1,5},{5,1},{9,13},{13,9},{2,6},{6,2},{1... | collective-permute-start | bytes 3080 | tf_op jit(solution)/shard_map/ppermute | solution.py:197

commit v2 on v1

--- a/solution.py
+++ b/solution.py
@@ -8,6 +8,7 @@
 from jax.sharding import PartitionSpec as P
 
 RBL = 4
+LANES = 128
 GROUP = ("row", "sub")
 VMEM_LIMIT = 24 * 1024 * 1024
 
@@ -33,9 +34,14 @@
     return high, low
 
 
-def split_kernel(blocks_ref, high_ref, low_ref):
-    for i in range(blocks_ref.shape[0]):
-        high_ref[i], low_ref[i] = halves(blocks_ref[i])
+def split_kernel(blocks_ref, high_ref, low_ref, held_ref, sems):
+    count = blocks_ref.shape[0]
+    copies = [pltpu.make_async_copy(blocks_ref.at[i], held_ref.at[i], sems.at[i]) for i in range(count)]
+    for copy in copies:
+        copy.start()
+    for i, copy in enumerate(copies):
+        copy.wait()
+        high_ref[i], low_ref[i] = halves(held_ref[i])
 
 
 def split_blocks(blocks):
@@ -46,11 +52,12 @@
             pltpu.VMEM(blocks.shape, jnp.bfloat16),
             pltpu.VMEM(blocks.shape, jnp.bfloat16),
         ),
-        in_specs=[vmem()],
+        in_specs=[pl.BlockSpec(memory_space=pltpu.HBM)],
         out_specs=(vmem(), vmem()),
+        scratch_shapes=[pltpu.VMEM(blocks.shape, jnp.float32), pltpu.SemaphoreType.DMA((n,))],
         compiler_params=params(),
         cost_estimate=pl.CostEstimate(flops=3 * n * rows * cols, bytes_accessed=8 * n * rows * cols, transcendentals=0),
-    )(blocks)
+    )(pltpu.with_memory_space_constraint(blocks, pltpu.HBM))
 
 
 def store_halves(ref, index, x):
@@ -150,32 +157,35 @@
 
 def solve_kernel(scale, z_ref, *refs):
     grams, out_ref, factor_ref = refs[:-2], refs[-2], refs[-1]
-    count = factor_ref.shape[0]
-    per_share = out_ref.shape[1] // z_ref.shape[2]
+    count, edge = factor_ref.shape[0], z_ref.shape[2]
+    per_share = out_ref.shape[1] // edge
     first = lax.axis_index(GROUP) * per_share
     g = grams[0][...]
     for piece in grams[1:]:
         g = g + piece[...]
-    z = [z_ref[first + h] * scale for h in range(per_share)]
-    row_id = lax.broadcasted_iota(jnp.int32, (count, count), 0)
-    col_id = lax.broadcasted_iota(jnp.int32, (count, count), 1)
-    factor = jnp.zeros((count, count), jnp.float32)
-    edge = z_ref.shape[2]
-    row_wide = lax.broadcasted_iota(jnp.int32, (count, edge), 0)
-    done = [jnp.zeros_like(x) for x in z]
+    z = [z_ref[first + h] for h in range(per_share)]
+    row_id = lax.broadcasted_iota(jnp.int32, (count, LANES), 0)
+    lane_id = lax.broadcasted_iota(jnp.int32, (count, LANES), 1)
+    columns = [jnp.broadcast_to(g[:, k:k + 1], (count, LANES)) for k in range(count)]
+    lower = jnp.zeros((count, LANES), jnp.float32)
+    scales = jnp.zeros((count, LANES), jnp.float32)
     for j in range(count):
-        inverse = lax.rsqrt(g[j:j + 1, j:j + 1])
-        row = g[j:j + 1, :] * inverse
-        column = g[:, j:j + 1] * inverse
-        factor = jnp.where((row_id == j) & (col_id >= j), row, factor)
-        rows = [x[j:j + 1, :] * inverse for x in z]
-        done = [jnp.where(row_wide == j, x, d) for x, d in zip(rows, done)]
+        column = columns[j]
+        root = lax.rsqrt(column[j:j + 1, :])
+        inverse = root * root
+        lower = jnp.where((lane_id == j) & (row_id >= j), column * root, lower)
+        scales = jnp.where(row_id == j, root, scales)
+        below = jnp.where(row_id > j, column, 0.0)
+        for k in range(j + 1, count):
+            columns[k] = columns[k] - below * (column[k:k + 1, :] * inverse)
         if j + 1 < count:
-            g = g - column * row
-            z = [x - column * y for x, y in zip(z, rows)]
+            wide = jnp.concatenate([below] * (edge // LANES), 1)
+            wide_inverse = jnp.concatenate([inverse] * (edge // LANES), 1)
+            z = [x - wide * (x[j:j + 1, :] * wide_inverse) for x in z]
+    scales = jnp.concatenate([scales * scale] * (edge // LANES), 1)
     for h in range(per_share):
-        out_ref[:, h * edge:(h + 1) * edge] = done[h]
-    factor_ref[...] = factor
+        out_ref[:, h * edge:(h + 1) * edge] = z[h] * scales
+    factor_ref[...] = lower[:, :count].T
 
 
 def solve(z, grams, share, scale):
@@ -209,7 +219,7 @@
 def to_sum(x, axis):
     n = lax.axis_size(axis)
     if n <= 4 and is_power(n):
-        return gather(x, axis)
+        return [x] + [partner(x, axis, k) for k in (3, 1, 2)]
     return [lax.psum(x, axis)]
 
 
@@ -229,7 +239,7 @@
         zpart = zpart + partner(zpart, axis, k)
     z, gram = gram_of(zpart, partner(zpart, *rounds[-1]))
     scale = math.sqrt(share * lax.axis_size(("col",) + GROUP))
-    return solve(z, to_sum(gram, "col"), share, scale)
+    return solve(z, gather(gram, "col"), share, scale)
 
 
 def solution(mesh):

time: 36.4 us -> 35 us (0.962)
  local copies, waits for them, and re-layouts: 2.19 us -> 0.01 us
  Pallas kernels: 5.84 us -> 6.58 us
    unnamed x6 -> x4, local copies, waits for them, and re-layouts: 2.19 us -> 0.01 us
    pallas_call x1, Pallas kernels: 0.65 us -> 2.31 us  [split_blocks(): pl.pallas_call(split_kernel, out_shape=(pltpu.VMEM(blocks.shape, jnp.bflo...]
    pallas_call x1, Pallas kernels: 1.86 us -> 0.94 us  [solve(): pl.pallas_call(lambda *refs: solve_kernel(scale, *refs), out_shape=(jax.S...]
  transfers between devices with their start and end apart: 11 -> 11, of which waited for: 7 -> 8; matrix products, arithmetic and copies ran while one was open for 0% -> 0% of each run, Pallas kernels for 2% -> 7%
where the time goes in v2:
time: 35 us; the launch traced here: 34.9 us
  waiting for transfers between devices  14.5 us (41%)
  starting transfers between devices  13.1 us (37%)
  Pallas kernels  6.58 us (19%)
  between operations  0.68 us (2%)
    ppermute x11, waiting for transfers between devices, partner(): return lax.ppermute(x, axes, [(i, i ^ k) for i in range(n)])  14.5 us
    ppermute x11, starting transfers between devices, partner(): return lax.ppermute(x, axes, [(i, i ^ k) for i in range(n)])  13.1 us
    pallas_call x1, Pallas kernels, split_blocks(): pl.pallas_call(split_kernel, out_shape=(pltpu.VMEM(blocks.shape, jnp.bflo...  2.31 us
    pallas_call x1, Pallas kernels, rows_product(): pl.pallas_call(rows_kernel, out_shape=jax.ShapeDtypeStruct((RBL, count, e...  1.78 us
    pallas_call x1, Pallas kernels, cols_product(): pl.pallas_call(lambda *refs: cols_kernel(column_count, *refs), out_shape=...  1.27 us
    pallas_call x1, Pallas kernels, solve(): pl.pallas_call(lambda *refs: solve_kernel(scale, *refs), out_shape=(jax.S...  0.94 us
  transfers between devices with their start and end apart: 11, of which 8 were waited for; matrix products, arithmetic and copies ran while one was open for 0% of the time, Pallas kernels for 7%

profile of v2, /device:TPU:0, one launch (start us, length us, event | category | flops | bytes accessed | tf_op | source)
XLA Modules:
  0.0 34.9 jit_solution(10259445034801288300)
XLA Ops:
  0.6 3.0 %collective-permute-start.1 = (f32[16,512]{1,0:T(8,128)}, f32[16,512]{1,0:T(8,128)S(1)}, u32[]{:S(2)}, u32[]{:S(2)}) collective-permute-start(f32[16,512]{1,0:T(8,128)} %refs_0_.1), channel_id=1, source_target_pairs={{0,2},{1,3},{2,0},{3,1},{4,6},{5,7},{6,4},{7,5},{8,10},{9,11},{10,... | collective-permute-start | bytes 98312 | tf_op jit(solution)/shard_map/ppermute | solution.py:207
  3.6 0.0 collective-permute-start
  3.6 0.2 collective-permute-start.2
  3.8 0.0 copy-start
  3.8 0.0 copy-start.1
  3.8 2.3 %shard_map.50 = (bf16[16,256,256]{2,1,0:T(8,128)(2,1)S(1)}, bf16[16,256,256]{2,1,0:T(8,128)(2,1)S(1)}) custom-call(f32[16,256,256]{2,1,0:T(8,128)} %bitcast.4), custom_call_target="tpu_custom_call" | custom-call | flops 3145728 | bytes 8388608 | tf_op jit(solution)/shard_map/pallas_call | solution.py:49
  6.2 0.0 collective-permute-done.1.refs_2_
  6.2 0.0 collective-permute-done.refs_1_
  6.2 1.0 %collective-permute-done.2.refs_3_ = f32[16,512]{1,0:T(8,128)S(1)} collective-permute-done((f32[16,512]{1,0:T(8,128)}, f32[16,512]{1,0:T(8,128)S(1)}, u32[]{:S(2)}, u32[]{:S(2)}) %collective-permute-start.2) | collective-permute-done | bytes 32800 | tf_op jit(solution)/shard_map/ppermute | solution.py:207
  7.2 0.0 copy-done
  7.2 0.0 copy-done.1
  7.2 1.8 %shard_map.51.refs_3_ = f32[4,16,256]{2,1,0:T(8,128)S(1)} custom-call(s32[16]{0:T(128)S(1)} %bitcast.2, bf16[16,256,256]{2,1,0:T(8,128)(2,1)S(1)} %get-tuple-element.6.high_ref.refs_1_, bf16[16,256,256]{2,1,0:T(8,128)(2,1)S(1)} %get-tuple-element.7.low_ref.refs_2_, f32[16,512]{1,0:T(8,128)S(1)} %copy-done, f32[16,512]{1,0:T(8,128)S(1)} %collective-permute-done.refs_1_, ...), custom_call_target="tpu_custom_call" | custom-call | tf_op jit(solution)/shard_map/pallas_call | solution.py:97
  9.0 2.6 %collective-permute-start.5 = (f32[4,16,256]{2,1,0:T(8,128)S(1)}, f32[4,16,256]{2,1,0:T(8,128)S(1)}, u32[]{:S(2)}, u32[]{:S(2)}) collective-permute-start(f32[4,16,256]{2,1,0:T(8,128)S(1)} %shard_map.51.refs_3_), channel_id=1, source_target_pairs={{0,8},{4,12},{8,0},{12,4},{1,9},{5,13},{9,1},{13,5},{2,10},{6,14},... | collective-permute-start | bytes 196616 | tf_op jit(solution)/shard_map/ppermute | solution.py:207
  11.6 1.6 %collective-permute-start.4 = (f32[4,16,256]{2,1,0:T(8,128)S(1)}, f32[4,16,256]{2,1,0:T(8,128)S(1)}, u32[]{:S(2)}, u32[]{:S(2)}) collective-permute-start(f32[4,16,256]{2,1,0:T(8,128)S(1)} %shard_map.51.refs_3_), channel_id=1, source_target_pairs={{0,4},{4,0},{8,12},{12,8},{1,5},{5,1},{9,13},{13,9},{2,6},{6,2},{1... | collective-permute-start | bytes 196616 | tf_op jit(solution)/shard_map/ppermute | solution.py:207
  13.2 0.2 collective-permute-start.3
  13.4 2.4 %collective-permute-done.5.refs_6_ = f32[4,16,256]{2,1,0:T(8,128)S(1)} collective-permute-done((f32[4,16,256]{2,1,0:T(8,128)S(1)}, f32[4,16,256]{2,1,0:T(8,128)S(1)}, u32[]{:S(2)}, u32[]{:S(2)}) %collective-permute-start.5) | collective-permute-done | bytes 65568 | tf_op jit(solution)/shard_map/ppermute | solution.py:207
  15.8 0.3 collective-permute-done.4.refs_5_
  16.1 3.1 %collective-permute-done.3.refs_4_ = f32[4,16,256]{2,1,0:T(8,128)S(1)} collective-permute-done((f32[4,16,256]{2,1,0:T(8,128)S(1)}, f32[4,16,256]{2,1,0:T(8,128)S(1)}, u32[]{:S(2)}, u32[]{:S(2)}) %collective-permute-start.3) | collective-permute-done | bytes 65568 | tf_op jit(solution)/shard_map/ppermute | solution.py:207
  19.2 1.3 %shard_map.52 = f32[8,16,256]{2,1,0:T(8,128)S(1)} custom-call(s32[16]{0:T(128)S(1)} %bitcast.3, bf16[16,256,256]{2,1,0:T(8,128)(2,1)S(1)} %get-tuple-element.6.high_ref.refs_1_, bf16[16,256,256]{2,1,0:T(8,128)(2,1)S(1)} %get-tuple-element.7.low_ref.refs_2_, f32[4,16,256]{2,1,0:T(8,128)S(1)} %shard_map.51.refs_3_, ...), custom_call_target="tpu_custom_call" | custom-call | tf_op jit(solution)/shard_map/pallas_call | solution.py:124
  20.5 0.0 collective-permute-start.6
  20.5 1.3 %collective-permute-done.6 = f32[8,16,256]{2,1,0:T(8,128)S(1)} collective-permute-done((f32[8,16,256]{2,1,0:T(8,128)S(1)}, f32[8,16,256]{2,1,0:T(8,128)S(1)}, u32[]{:S(2)}, u32[]{:S(2)}) %collective-permute-start.6) | collective-permute-done | bytes 131104 | tf_op jit(solution)/shard_map/ppermute | solution.py:207
  21.9 1.0 %collective-permute-start.7 = (f32[8,16,256]{2,1,0:T(8,128)S(1)}, f32[8,16,256]{2,1,0:T(8,128)S(1)}, u32[]{:S(2)}, u32[]{:S(2)}) collective-permute-start(f32[8,16,256]{2,1,0:T(8,128)S(1)} %add.3.a_ref), channel_id=1, source_target_pairs={{0,2},{2,0},{1,3},{3,1},{4,6},{6,4},{5,7},{7,5},{8,10},{10,8},{9,1... | collective-permute-start | bytes 393224 | tf_op jit(solution)/shard_map/ppermute | solution.py:207
  22.9 4.6 %collective-permute-done.7.b_ref = f32[8,16,256]{2,1,0:T(8,128)S(1)} collective-permute-done((f32[8,16,256]{2,1,0:T(8,128)S(1)}, f32[8,16,256]{2,1,0:T(8,128)S(1)}, u32[]{:S(2)}, u32[]{:S(2)}) %collective-permute-start.7) | collective-permute-done | bytes 131104 | tf_op jit(solution)/shard_map/ppermute | solution.py:207
  27.5 0.3 shard_map.53
  27.8 1.6 %collective-permute-start.10 = (f32[16,16]{1,0:T(8,128)S(1)}, f32[16,16]{1,0:T(8,128)S(1)}, u32[]{:S(2)}, u32[]{:S(2)}) collective-permute-start(f32[16,16]{1,0:T(8,128)S(1)} %get-tuple-element.9.refs_1_), channel_id=1, source_target_pairs={{0,12},{4,8},{8,4},{12,0},{1,13},{5,9},{9,5},{13,1},{2,14},{6,10},... | collective-permute-start | bytes 3080 | tf_op jit(solution)/shard_map/ppermute | solution.py:207
  29.4 0.4 %collective-permute-start.9 = (f32[16,16]{1,0:T(8,128)S(1)}, f32[16,16]{1,0:T(8,128)S(1)}, u32[]{:S(2)}, u32[]{:S(2)}) collective-permute-start(f32[16,16]{1,0:T(8,128)S(1)} %get-tuple-element.9.refs_1_), channel_id=1, source_target_pairs={{0,8},{4,12},{8,0},{12,4},{1,9},{5,13},{9,1},{13,5},{2,10},{6,14},... | collective-permute-start | bytes 3080 | tf_op jit(solution)/shard_map/ppermute | solution.py:207
  29.8 2.4 %collective-permute-start.8 = (f32[16,16]{1,0:T(8,128)S(1)}, f32[16,16]{1,0:T(8,128)S(1)}, u32[]{:S(2)}, u32[]{:S(2)}) collective-permute-start(f32[16,16]{1,0:T(8,128)S(1)} %get-tuple-element.9.refs_1_), channel_id=1, source_target_pairs={{0,4},{4,0},{8,12},{12,8},{1,5},{5,1},{9,13},{13,9},{2,6},{6,2},{1... | collective-permute-start | bytes 3080 | tf_op jit(solution)/shard_map/ppermute | solution.py:207
  32.2 1.1 %collective-permute-done.10.refs_4_ = f32[16,16]{1,0:T(8,128)S(1)} collective-permute-done((f32[16,16]{1,0:T(8,128)S(1)}, f32[16,16]{1,0:T(8,128)S(1)}, u32[]{:S(2)}, u32[]{:S(2)}) %collective-permute-start.10) | collective-permute-done | bytes 1056 | tf_op jit(solution)/shard_map/ppermute | solution.py:207
  33.3 0.7 %collective-permute-done.9.refs_3_ = f32[16,16]{1,0:T(8,128)S(1)} collective-permute-done((f32[16,16]{1,0:T(8,128)S(1)}, f32[16,16]{1,0:T(8,128)S(1)}, u32[]{:S(2)}, u32[]{:S(2)}) %collective-permute-start.9) | collective-permute-done | bytes 1056 | tf_op jit(solution)/shard_map/ppermute | solution.py:207
  33.9 0.0 collective-permute-done.8.refs_2_
  33.9 0.9 %shard_map.54 = (f32[16,512]{1,0:T(8,128)}, f32[16,16]{1,0:T(8,128)}) custom-call(f32[8,16,256]{2,1,0:T(8,128)S(1)} %get-tuple-element.8.refs_0_, f32[16,16]{1,0:T(8,128)S(1)} %get-tuple-element.9.refs_1_, f32[16,16]{1,0:T(8,128)S(1)} %collective-permute-done.8.refs_2_, f32[16,16]{1,0:T(8,128)S(1)} %collective-permute-done.9.refs_3_, ...), custom_call_target="tpu_custom_call" | custom-call | tf_op jit(solution)/shard_map/pallas_call | solution.py:193
  (1 shorter events, 0.0 us)
Async XLA Ops:
  0.6 5.5 %collective-permute-start.1 = (f32[16,512]{1,0:T(8,128)}, f32[16,512]{1,0:T(8,128)S(1)}, u32[]{:S(2)}, u32[]{:S(2)}) collective-permute-start(f32[16,512]{1,0:T(8,128)} %refs_0_.1), channel_id=1, source_target_pairs={{0,2},{1,3},{2,0},{3,1},{4,6},{5,7},{6,4},{7,5},{8,10},{9,11},{10,... | collective-permute-start | bytes 98312 | tf_op jit(solution)/shard_map/ppermute | solution.py:207
  3.6 2.5 %collective-permute-start = (f32[16,512]{1,0:T(8,128)}, f32[16,512]{1,0:T(8,128)S(1)}, u32[]{:S(2)}, u32[]{:S(2)}) collective-permute-start(f32[16,512]{1,0:T(8,128)} %refs_0_.1), channel_id=1, source_target_pairs={{0,1},{1,0},{2,3},{3,2},{4,5},{5,4},{6,7},{7,6},{8,9},{9,8},{10,11... | collective-permute-start | bytes 98312 | tf_op jit(solution)/shard_map/ppermute | solution.py:207
  3.6 3.6 %collective-permute-start.2 = (f32[16,512]{1,0:T(8,128)}, f32[16,512]{1,0:T(8,128)S(1)}, u32[]{:S(2)}, u32[]{:S(2)}) collective-permute-start(f32[16,512]{1,0:T(8,128)} %refs_0_.1), channel_id=1, source_target_pairs={{0,3},{1,2},{2,1},{3,0},{4,7},{5,6},{6,5},{7,4},{8,11},{9,10},{10,... | collective-permute-start | bytes 98312 | tf_op jit(solution)/shard_map/ppermute | solution.py:207
  3.8 3.3 %copy-start = (f32[16,512]{1,0:T(8,128)S(1)}, f32[16,512]{1,0:T(8,128)}, u32[]{:S(2)}) copy-start(f32[16,512]{1,0:T(8,128)} %refs_0_.1) | copy-start | bytes 98308
  3.8 3.3 %copy-start.1 = (s32[1,1,16]{2,1,0:T(1,128)S(1)}, s32[1,1,16]{2,1,0:T(1,128)}, u32[]{:S(2)}) copy-start(s32[1,1,16]{2,1,0:T(1,128)} %param.4) | copy-start | bytes 196
  9.0 6.8 %collective-permute-start.5 = (f32[4,16,256]{2,1,0:T(8,128)S(1)}, f32[4,16,256]{2,1,0:T(8,128)S(1)}, u32[]{:S(2)}, u32[]{:S(2)}) collective-permute-start(f32[4,16,256]{2,1,0:T(8,128)S(1)} %shard_map.51.refs_3_), channel_id=1, source_target_pairs={{0,8},{4,12},{8,0},{12,4},{1,9},{5,13},{9,1},{13,5},{2,10},{6,14},... | collective-permute-start | bytes 196616 | tf_op jit(solution)/shard_map/ppermute | solution.py:207
  11.6 4.6 %collective-permute-start.4 = (f32[4,16,256]{2,1,0:T(8,128)S(1)}, f32[4,16,256]{2,1,0:T(8,128)S(1)}, u32[]{:S(2)}, u32[]{:S(2)}) collective-permute-start(f32[4,16,256]{2,1,0:T(8,128)S(1)} %shard_map.51.refs_3_), channel_id=1, source_target_pairs={{0,4},{4,0},{8,12},{12,8},{1,5},{5,1},{9,13},{13,9},{2,6},{6,2},{1... | collective-permute-start | bytes 196616 | tf_op jit(solution)/shard_map/ppermute | solution.py:207
  13.2 6.1 %collective-permute-start.3 = (f32[4,16,256]{2,1,0:T(8,128)S(1)}, f32[4,16,256]{2,1,0:T(8,128)S(1)}, u32[]{:S(2)}, u32[]{:S(2)}) collective-permute-start(f32[4,16,256]{2,1,0:T(8,128)S(1)} %shard_map.51.refs_3_), channel_id=1, source_target_pairs={{0,12},{4,8},{8,4},{12,0},{1,13},{5,9},{9,5},{13,1},{2,14},{6,10},... | collective-permute-start | bytes 196616 | tf_op jit(solution)/shard_map/ppermute | solution.py:207
  20.5 1.4 %collective-permute-start.6 = (f32[8,16,256]{2,1,0:T(8,128)S(1)}, f32[8,16,256]{2,1,0:T(8,128)S(1)}, u32[]{:S(2)}, u32[]{:S(2)}) collective-permute-start(f32[8,16,256]{2,1,0:T(8,128)S(1)} %shard_map.52), channel_id=1, source_target_pairs={{0,1},{1,0},{2,3},{3,2},{4,5},{5,4},{6,7},{7,6},{8,9},{9,8},{10,11... | collective-permute-start | bytes 393224 | tf_op jit(solution)/shard_map/ppermute | solution.py:207
  21.9 5.6 %collective-permute-start.7 = (f32[8,16,256]{2,1,0:T(8,128)S(1)}, f32[8,16,256]{2,1,0:T(8,128)S(1)}, u32[]{:S(2)}, u32[]{:S(2)}) collective-permute-start(f32[8,16,256]{2,1,0:T(8,128)S(1)} %add.3.a_ref), channel_id=1, source_target_pairs={{0,2},{2,0},{1,3},{3,1},{4,6},{6,4},{5,7},{7,5},{8,10},{10,8},{9,1... | collective-permute-start | bytes 393224 | tf_op jit(solution)/shard_map/ppermute | solution.py:207
  27.8 5.5 %collective-permute-start.10 = (f32[16,16]{1,0:T(8,128)S(1)}, f32[16,16]{1,0:T(8,128)S(1)}, u32[]{:S(2)}, u32[]{:S(2)}) collective-permute-start(f32[16,16]{1,0:T(8,128)S(1)} %get-tuple-element.9.refs_1_), channel_id=1, source_target_pairs={{0,12},{4,8},{8,4},{12,0},{1,13},{5,9},{9,5},{13,1},{2,14},{6,10},... | collective-permute-start | bytes 3080 | tf_op jit(solution)/shard_map/ppermute | solution.py:207
  29.4 4.5 %collective-permute-start.9 = (f32[16,16]{1,0:T(8,128)S(1)}, f32[16,16]{1,0:T(8,128)S(1)}, u32[]{:S(2)}, u32[]{:S(2)}) collective-permute-start(f32[16,16]{1,0:T(8,128)S(1)} %get-tuple-element.9.refs_1_), channel_id=1, source_target_pairs={{0,8},{4,12},{8,0},{12,4},{1,9},{5,13},{9,1},{13,5},{2,10},{6,14},... | collective-permute-start | bytes 3080 | tf_op jit(solution)/shard_map/ppermute | solution.py:207
  29.8 4.1 %collective-permute-start.8 = (f32[16,16]{1,0:T(8,128)S(1)}, f32[16,16]{1,0:T(8,128)S(1)}, u32[]{:S(2)}, u32[]{:S(2)}) collective-permute-start(f32[16,16]{1,0:T(8,128)S(1)} %get-tuple-element.9.refs_1_), channel_id=1, source_target_pairs={{0,4},{4,0},{8,12},{12,8},{1,5},{5,1},{9,13},{13,9},{2,6},{6,2},{1... | collective-permute-start | bytes 3080 | tf_op jit(solution)/shard_map/ppermute | solution.py:207

commit v3 on v2

--- a/solution.py
+++ b/solution.py
@@ -10,6 +10,10 @@
 RBL = 4
 LANES = 128
 GROUP = ("row", "sub")
+LEAD = 1
+COLS = ((0, 1, 2, 3), (1, 0, 3, 2), (2, 3, 0, 1), (3, 2, 1, 0))
+Y_ORDERS = ((3, 1, 2), (2, 3, 1))
+G_ORDER = (3, 2, 1)
 VMEM_LIMIT = 24 * 1024 * 1024
 
 NT = (((1,), (1,)), ((), ()))
@@ -34,14 +38,16 @@
     return high, low
 
 
-def split_kernel(blocks_ref, high_ref, low_ref, held_ref, sems):
+def split_kernel(blocks_ref, high_ref, low_ref, high_t_ref, held_ref, sems):
     count = blocks_ref.shape[0]
     copies = [pltpu.make_async_copy(blocks_ref.at[i], held_ref.at[i], sems.at[i]) for i in range(count)]
     for copy in copies:
         copy.start()
     for i, copy in enumerate(copies):
         copy.wait()
-        high_ref[i], low_ref[i] = halves(held_ref[i])
+        high, low = halves(held_ref[i])
+        high_ref[i], low_ref[i] = high, low
+        high_t_ref[i] = high.T
 
 
 def split_blocks(blocks):
@@ -51,9 +57,10 @@
         out_shape=(
             pltpu.VMEM(blocks.shape, jnp.bfloat16),
             pltpu.VMEM(blocks.shape, jnp.bfloat16),
+            pltpu.VMEM(blocks.shape, jnp.bfloat16),
         ),
         in_specs=[pl.BlockSpec(memory_space=pltpu.HBM)],
-        out_specs=(vmem(), vmem()),
+        out_specs=(vmem(), vmem(), vmem()),
         scratch_shapes=[pltpu.VMEM(blocks.shape, jnp.float32), pltpu.SemaphoreType.DMA((n,))],
         compiler_params=params(),
         cost_estimate=pl.CostEstimate(flops=3 * n * rows * cols, bytes_accessed=8 * n * rows * cols, transcendentals=0),
@@ -67,10 +74,10 @@
     ref[index, pl.ds(count, count)] = low
 
 
-def product(pair, high, low, dims):
+def product(pair, high, low, dims, low_dims):
     count = pair.shape[0] // 2
     first = lax.dot_general(pair, high, dims, preferred_element_type=jnp.float32)
-    second = lax.dot_general(pair[:count], low, dims, preferred_element_type=jnp.float32)
+    second = lax.dot_general(pair[:count], low, low_dims, preferred_element_type=jnp.float32)
     return first[:count] + first[count:] + second
 
 
@@ -87,7 +94,7 @@
     for b in range(nblk):
         slot = slot_ref[b]
         r, c = slot // column_count, slot % column_count
-        out_ref[r] += product(pair_ref[c], high_ref[b], low_ref[b], NT)
+        out_ref[r] += product(pair_ref[c], high_ref[b], low_ref[b], NN, NT)
 
 
 def rows_product(slot, high, low, pieces):
@@ -116,7 +123,7 @@
     for b in range(nblk):
         slot = slot_ref[b]
         r, c = slot // column_count, slot % column_count
-        out_ref[c] += product(pair_ref[r], high_ref[b], low_ref[b], NN)
+        out_ref[c] += product(pair_ref[r], high_ref[b], low_ref[b], NN, NN)
 
 
 def cols_product(slot, high, low, pieces, column_count):
@@ -131,39 +138,54 @@
     )(slot, high, low, *pieces)
 
 
-def gram_kernel(a_ref, b_ref, z_ref, gram_ref):
-    total = None
-    for c in range(a_ref.shape[0]):
-        z = a_ref[c] + b_ref[c]
-        z_ref[c] = z
-        g = lax.dot_general(z, z, NT, precision=lax.Precision.HIGHEST, preferred_element_type=jnp.float32)
-        total = g if total is None else total + g
-    gram_ref[...] = total
-
-
-def gram_of(a, b):
-    count = a.shape[1]
-    return pl.pallas_call(
-        gram_kernel,
-        out_shape=(
-            jax.ShapeDtypeStruct(a.shape, jnp.float32),
-            jax.ShapeDtypeStruct((count, count), jnp.float32),
-        ),
+def gram_kernel(lead, a_ref, b_ref, mine_ref, other_ref, gram_ref, z_ref):
+    leads = True if lead is None else lax.axis_index("sub") == lead
+
+    @pl.when(leads)
+    def _():
+        total = None
+        for c in range(a_ref.shape[0]):
+            z = a_ref[c] + b_ref[c]
+            z_ref[c] = z
+            g = lax.dot_general(z, z, NT, precision=lax.Precision.HIGHEST, preferred_element_type=jnp.float32)
+            total = g if total is None else total + g
+        gram_ref[...] = total
+        me = lax.axis_index(GROUP)
+        count = mine_ref.shape[0]
+        for h in range(count):
+            mine_ref[h] = z_ref[me * count + h]
+            other_ref[h] = z_ref[(me ^ 1) * count + h]
+
+    @pl.when(jnp.logical_not(leads))
+    def _():
+        gram_ref[...] = jnp.zeros_like(gram_ref)
+        mine_ref[...] = jnp.zeros_like(mine_ref)
+        other_ref[...] = jnp.zeros_like(other_ref)
+
+
+def gram_of(a, b, per_share, lead):
+    _, count, edge = a.shape
+    share = jax.ShapeDtypeStruct((per_share, count, edge), jnp.float32)
+    return pl.pallas_call(
+        lambda *refs: gram_kernel(lead, *refs),
+        out_shape=(share, share, jax.ShapeDtypeStruct((count, count), jnp.float32)),
         in_specs=[vmem(), vmem()],
-        out_specs=(vmem(), vmem()),
+        out_specs=(vmem(), vmem(), vmem()),
+        scratch_shapes=[pltpu.VMEM(a.shape, jnp.float32)],
         compiler_params=params(),
     )(a, b)
 
 
-def solve_kernel(scale, z_ref, *refs):
-    grams, out_ref, factor_ref = refs[:-2], refs[-2], refs[-1]
+def solve_kernel(scale, *refs):
+    z_ref, gram_ref, out_ref, factor_ref = refs[0], refs[1], refs[-2], refs[-1]
     count, edge = factor_ref.shape[0], z_ref.shape[2]
     per_share = out_ref.shape[1] // edge
-    first = lax.axis_index(GROUP) * per_share
-    g = grams[0][...]
-    for piece in grams[1:]:
-        g = g + piece[...]
-    z = [z_ref[first + h] for h in range(per_share)]
+    g = gram_ref[...]
+    z = [z_ref[h] for h in range(per_share)]
+    if len(refs) > 4:
+        leads = lax.axis_index("sub") == LEAD
+        g = jnp.where(leads, g, refs[3][...])
+        z = [jnp.where(leads, x, refs[2][h]) for h, x in enumerate(z)]
     row_id = lax.broadcasted_iota(jnp.int32, (count, LANES), 0)
     lane_id = lax.broadcasted_iota(jnp.int32, (count, LANES), 1)
     columns = [jnp.broadcast_to(g[:, k:k + 1], (count, LANES)) for k in range(count)]
@@ -188,18 +210,18 @@
     factor_ref[...] = lower[:, :count].T
 
 
-def solve(z, grams, share, scale):
-    count = z.shape[1]
+def solve(scale, *arrays):
+    per_share, count, edge = arrays[0].shape
     return pl.pallas_call(
         lambda *refs: solve_kernel(scale, *refs),
         out_shape=(
-            jax.ShapeDtypeStruct((count, share), jnp.float32),
+            jax.ShapeDtypeStruct((count, per_share * edge), jnp.float32),
             jax.ShapeDtypeStruct((count, count), jnp.float32),
         ),
-        in_specs=[vmem()] * (1 + len(grams)),
+        in_specs=[vmem()] * len(arrays),
         out_specs=(vmem(), vmem()),
         compiler_params=params(),
-    )(z, *grams)
+    )(*arrays)
 
 
 def partner(x, axes, k):
@@ -216,11 +238,39 @@
     return [x] + [partner(x, axes, k) for k in range(1, n)]
 
 
-def to_sum(x, axis):
-    n = lax.axis_size(axis)
-    if n <= 4 and is_power(n):
-        return [x] + [partner(x, axis, k) for k in (3, 1, 2)]
-    return [lax.psum(x, axis)]
+def exchange(x, steps):
+    cols, rows, subs = (lax.axis_size(a) for a in ("col", "row", "sub"))
+    place = lambda c, r, s: (c * rows + r) * subs + s
+    pairs = [
+        (place(c, r, s), place(steps[s][0][c], r ^ steps[s][1], s))
+        for c in range(cols)
+        for r in range(rows)
+        for s in range(subs)
+    ]
+    return lax.ppermute(x, ("col", "row", "sub"), pairs)
+
+
+def general(slot, high, low, ypart, column_count, per_share, scale):
+    zpart = cols_product(slot, high, low, [lax.psum(ypart, "col")], column_count)
+    for axis in ("sub", "row"):
+        n = lax.axis_size(axis)
+        if is_power(n):
+            for i in range(n.bit_length() - 1):
+                zpart = zpart + partner(zpart, axis, 1 << i)
+        else:
+            zpart = lax.psum(zpart, axis)
+    z, _, gram = gram_of(zpart, jnp.zeros_like(zpart), per_share, None)
+    return solve(scale, z, lax.psum(gram, "col"))
+
+
+def four_by_two(slot, high, low, ypart, column_count, per_share, scale):
+    ypieces = [ypart] + [exchange(ypart, ((COLS[a], 0), (COLS[b], 0))) for a, b in zip(*Y_ORDERS)]
+    zpart = cols_product(slot, high, low, ypieces, column_count)
+    zpart = zpart + partner(zpart, "sub", 1)
+    z, other, gram = gram_of(zpart, exchange(zpart, ((COLS[1], 0), (COLS[0], 1))), per_share, LEAD)
+    far_z = partner(other, "sub", 1)
+    gram = gram + sum(exchange(gram, ((COLS[0], 1), (COLS[k], 0))) for k in G_ORDER)
+    return solve(scale, z, gram, far_z, partner(gram, "sub", 1))
 
 
 def body(blocks, block_slot, basis_in):
@@ -229,17 +279,14 @@
     share = basis_in.shape[1]
     column_count = share * lax.axis_size(GROUP) // edge
     slot = block_slot.reshape(nblk)
-    high, low = split_blocks(blocks.reshape(nblk, edge, edge))
-    high = pltpu.with_memory_space_constraint(high, pltpu.VMEM)
-    low = pltpu.with_memory_space_constraint(low, pltpu.VMEM)
-    ypart = rows_product(slot, high, low, gather(basis_in, GROUP))
-    zpart = cols_product(slot, high, low, to_sum(ypart, "col"), column_count)
-    rounds = [(axis, 1 << i) for axis in reversed(GROUP) for i in range(int(math.log2(lax.axis_size(axis))))]
-    for axis, k in rounds[:-1]:
-        zpart = zpart + partner(zpart, axis, k)
-    z, gram = gram_of(zpart, partner(zpart, *rounds[-1]))
+    high, low, high_t = [
+        pltpu.with_memory_space_constraint(x, pltpu.VMEM) for x in split_blocks(blocks.reshape(nblk, edge, edge))
+    ]
+    ypart = rows_product(slot, high_t, low, gather(basis_in, GROUP))
     scale = math.sqrt(share * lax.axis_size(("col",) + GROUP))
-    return solve(z, gather(gram, "col"), share, scale)
+    sizes = tuple(lax.axis_size(a) for a in ("col", "row", "sub"))
+    finish = four_by_two if sizes == (4, 2, 2) else general
+    return finish(slot, high, low, ypart, column_count, share // edge, scale)
 
 
 def solution(mesh):

time: 35 us -> 33.8 us (0.966)
  waiting for transfers between devices: 14.5 us -> 13.6 us
    ppermute x11 -> x6, waiting for transfers between devices: 14.5 us -> 3.07 us  [partner(): return lax.ppermute(x, axes, [(i, i ^ k) for i in range(n)])]
    ppermute x0 -> x7, waiting for transfers between devices: none -> 10.6 us  [exchange(): return lax.ppermute(x, ('col', 'row', 'sub'), pairs)]
    ppermute x11 -> x6, starting transfers between devices: 13.1 us -> 3.74 us  [partner(): return lax.ppermute(x, axes, [(i, i ^ k) for i in range(n)])]
    ppermute x0 -> x7, starting transfers between devices: none -> 9.23 us  [exchange(): return lax.ppermute(x, ('col', 'row', 'sub'), pairs)]
  transfers between devices with their start and end apart: 11 -> 13, of which waited for: 8 -> 9; matrix products, arithmetic and copies ran while one was open for 0% -> 0% of each run, Pallas kernels for 7% -> 8%
where the time goes in v3:
time: 33.8 us; the launch traced here: 33.6 us
  waiting for transfers between devices  13.6 us (40%)
  starting transfers between devices  13 us (38%)
  Pallas kernels  6.31 us (19%)
  between operations  0.68 us (2%)
    ppermute x7, waiting for transfers between devices, exchange(): return lax.ppermute(x, ('col', 'row', 'sub'), pairs)  10.6 us
    ppermute x7, starting transfers between devices, exchange(): return lax.ppermute(x, ('col', 'row', 'sub'), pairs)  9.23 us
    ppermute x6, starting transfers between devices, partner(): return lax.ppermute(x, axes, [(i, i ^ k) for i in range(n)])  3.74 us
    ppermute x6, waiting for transfers between devices, partner(): return lax.ppermute(x, axes, [(i, i ^ k) for i in range(n)])  3.07 us
    pallas_call x1, Pallas kernels, split_blocks(): pl.pallas_call(split_kernel, out_shape=(pltpu.VMEM(blocks.shape, jnp.bflo...  2.54 us
    pallas_call x1, Pallas kernels, rows_product(): pl.pallas_call(rows_kernel, out_shape=jax.ShapeDtypeStruct((RBL, count, e...  1.55 us
    pallas_call x1, Pallas kernels, cols_product(): pl.pallas_call(lambda *refs: cols_kernel(column_count, *refs), out_shape=...  1.27 us
    pallas_call x1, Pallas kernels, solve(): pl.pallas_call(lambda *refs: solve_kernel(scale, *refs), out_shape=(jax.S...  0.94 us
  transfers between devices with their start and end apart: 13, of which 9 were waited for; matrix products, arithmetic and copies ran while one was open for 0% of the time, Pallas kernels for 8%

profile of v3, /device:TPU:0, one launch (start us, length us, event | category | flops | bytes accessed | tf_op | source)
XLA Modules:
  0.0 33.6 jit_solution(6038298086707833122)
XLA Ops:
  0.6 0.5 %collective-permute-start = (f32[16,512]{1,0:T(8,128)}, f32[16,512]{1,0:T(8,128)S(1)}, u32[]{:S(2)}, u32[]{:S(2)}) collective-permute-start(f32[16,512]{1,0:T(8,128)} %refs_0_.1), channel_id=1, source_target_pairs={{0,1},{1,0},{2,3},{3,2},{4,5},{5,4},{6,7},{7,6},{8,9},{9,8},{10,11... | collective-permute-start | bytes 98312 | tf_op jit(solution)/shard_map/ppermute | solution.py:229
  1.1 2.6 %collective-permute-start.1 = (f32[16,512]{1,0:T(8,128)}, f32[16,512]{1,0:T(8,128)S(1)}, u32[]{:S(2)}, u32[]{:S(2)}) collective-permute-start(f32[16,512]{1,0:T(8,128)} %refs_0_.1), channel_id=1, source_target_pairs={{0,2},{1,3},{2,0},{3,1},{4,6},{5,7},{6,4},{7,5},{8,10},{9,11},{10,... | collective-permute-start | bytes 98312 | tf_op jit(solution)/shard_map/ppermute | solution.py:229
  3.7 0.1 collective-permute-start.2
  3.8 0.0 copy-start
  3.8 0.0 copy-start.1
  3.8 2.5 %shard_map.50 = (bf16[16,256,256]{2,1,0:T(8,128)(2,1)S(1)}, bf16[16,256,256]{2,1,0:T(8,128)(2,1)S(1)}, bf16[16,256,256]{2,1,0:T(8,128)(2,1)S(1)}) custom-call(f32[16,256,256]{2,1,0:T(8,128)} %bitcast.4), custom_call_target="tpu_custom_call" | custom-call | flops 3145728 | bytes 8388608 | tf_op jit(solution)/shard_map/pallas_call | solution.py:55
  6.3 0.0 collective-permute-done.refs_1_
  6.3 0.0 collective-permute-done.1.refs_2_
  6.4 0.9 %collective-permute-done.2.refs_3_ = f32[16,512]{1,0:T(8,128)S(1)} collective-permute-done((f32[16,512]{1,0:T(8,128)}, f32[16,512]{1,0:T(8,128)S(1)}, u32[]{:S(2)}, u32[]{:S(2)}) %collective-permute-start.2) | collective-permute-done | bytes 32800 | tf_op jit(solution)/shard_map/ppermute | solution.py:229
  7.3 0.0 copy-done
  7.3 0.0 copy-done.1
  7.3 1.5 %shard_map.51.refs_3_ = f32[4,16,256]{2,1,0:T(8,128)S(1)} custom-call(s32[16]{0:T(128)S(1)} %bitcast.2, bf16[16,256,256]{2,1,0:T(8,128)(2,1)S(1)} %get-tuple-element.10.high_ref, bf16[16,256,256]{2,1,0:T(8,128)(2,1)S(1)} %get-tuple-element.9.low_ref.refs_2_, f32[16,512]{1,0:T(8,128)S(1)} %copy-done, f32[16,512]{1,0:T(8,128)S(1)} %collective-permute-done.refs_1_, ...), custom_call_target="tpu_custom_call" | custom-call | tf_op jit(solution)/shard_map/pallas_call | solution.py:104
  8.8 3.6 %collective-permute-start.3 = (f32[4,16,256]{2,1,0:T(8,128)S(1)}, f32[4,16,256]{2,1,0:T(8,128)S(1)}, u32[]{:S(2)}, u32[]{:S(2)}) collective-permute-start(f32[4,16,256]{2,1,0:T(8,128)S(1)} %shard_map.51.refs_3_), channel_id=1, source_target_pairs={{0,12},{1,9},{2,14},{3,11},{4,8},{5,13},{6,10},{7,15},{8,4},{9,1},... | collective-permute-start | bytes 196616 | tf_op jit(solution)/shard_map/ppermute | solution.py:250
  12.4 0.0 collective-permute-start.4
  12.4 0.8 %collective-permute-start.5 = (f32[4,16,256]{2,1,0:T(8,128)S(1)}, f32[4,16,256]{2,1,0:T(8,128)S(1)}, u32[]{:S(2)}, u32[]{:S(2)}) collective-permute-start(f32[4,16,256]{2,1,0:T(8,128)S(1)} %shard_map.51.refs_3_), channel_id=1, source_target_pairs={{0,8},{1,5},{2,10},{3,7},{4,12},{5,1},{6,14},{7,3},{8,0},{9,13},{1... | collective-permute-start | bytes 196616 | tf_op jit(solution)/shard_map/ppermute | solution.py:250
  13.2 1.8 %collective-permute-done.3.refs_4_ = f32[4,16,256]{2,1,0:T(8,128)S(1)} collective-permute-done((f32[4,16,256]{2,1,0:T(8,128)S(1)}, f32[4,16,256]{2,1,0:T(8,128)S(1)}, u32[]{:S(2)}, u32[]{:S(2)}) %collective-permute-start.3) | collective-permute-done | bytes 65568 | tf_op jit(solution)/shard_map/ppermute | solution.py:250
  15.0 2.9 %collective-permute-done.4.refs_5_ = f32[4,16,256]{2,1,0:T(8,128)S(1)} collective-permute-done((f32[4,16,256]{2,1,0:T(8,128)S(1)}, f32[4,16,256]{2,1,0:T(8,128)S(1)}, u32[]{:S(2)}, u32[]{:S(2)}) %collective-permute-start.4) | collective-permute-done | bytes 65568 | tf_op jit(solution)/shard_map/ppermute | solution.py:250
  17.9 0.0 collective-permute-done.5.refs_6_
  17.9 1.3 %shard_map.52 = f32[8,16,256]{2,1,0:T(8,128)S(1)} custom-call(s32[16]{0:T(128)S(1)} %bitcast.3, bf16[16,256,256]{2,1,0:T(8,128)(2,1)S(1)} %get-tuple-element.8.refs_1_, bf16[16,256,256]{2,1,0:T(8,128)(2,1)S(1)} %get-tuple-element.9.low_ref.refs_2_, f32[4,16,256]{2,1,0:T(8,128)S(1)} %shard_map.51.refs_3_, f32[4,16,256]{2,1,0:T(8,128)S(1)} %collective-permute-done.3.refs_4_, ...), custom_call_target="tpu_custom_call" | custom-call | tf_op jit(solution)/shard_map/pallas_call | solution.py:131
  19.2 0.0 collective-permute-start.6
  19.2 1.3 %collective-permute-done.6 = f32[8,16,256]{2,1,0:T(8,128)S(1)} collective-permute-done((f32[8,16,256]{2,1,0:T(8,128)S(1)}, f32[8,16,256]{2,1,0:T(8,128)S(1)}, u32[]{:S(2)}, u32[]{:S(2)}) %collective-permute-start.6) | collective-permute-done | bytes 131104 | tf_op jit(solution)/shard_map/ppermute | solution.py:229
  20.6 1.8 %collective-permute-start.7 = (f32[8,16,256]{2,1,0:T(8,128)S(1)}, f32[8,16,256]{2,1,0:T(8,128)S(1)}, u32[]{:S(2)}, u32[]{:S(2)}) collective-permute-start(f32[8,16,256]{2,1,0:T(8,128)S(1)} %add.12.refs_0_), channel_id=1, source_target_pairs={{0,4},{1,3},{2,6},{3,1},{4,0},{5,7},{6,2},{7,5},{8,12},{9,11},{10,... | collective-permute-start | bytes 393224 | tf_op jit(solution)/shard_map/ppermute | solution.py:250
  22.3 3.2 %collective-permute-done.7.refs_1_ = f32[8,16,256]{2,1,0:T(8,128)S(1)} collective-permute-done((f32[8,16,256]{2,1,0:T(8,128)S(1)}, f32[8,16,256]{2,1,0:T(8,128)S(1)}, u32[]{:S(2)}, u32[]{:S(2)}) %collective-permute-start.7) | collective-permute-done | bytes 131104 | tf_op jit(solution)/shard_map/ppermute | solution.py:250
  25.6 1.0 %collective-permute-start.10 = (f32[16,16]{1,0:T(8,128)S(1)}, f32[16,16]{1,0:T(8,128)S(1)}, u32[]{:S(2)}, u32[]{:S(2)}) collective-permute-start(f32[16,16]{1,0:T(8,128)S(1)} %get-tuple-element.12), channel_id=1, source_target_pairs={{0,2},{1,5},{2,0},{3,7},{4,6},{5,1},{6,4},{7,3},{8,10},{9,13},{10,... | collective-permute-start | bytes 3080 | tf_op jit(solution)/shard_map/ppermute | solution.py:250
  26.6 1.0 %collective-permute-start.8 = (f32[16,16]{1,0:T(8,128)S(1)}, f32[16,16]{1,0:T(8,128)S(1)}, u32[]{:S(2)}, u32[]{:S(2)}) collective-permute-start(f32[16,16]{1,0:T(8,128)S(1)} %get-tuple-element.12), channel_id=1, source_target_pairs={{0,2},{1,13},{2,0},{3,15},{4,6},{5,9},{6,4},{7,11},{8,10},{9,5},{1... | collective-permute-start | bytes 3080 | tf_op jit(solution)/shard_map/ppermute | solution.py:250
  27.6 1.0 %collective-permute-start.9 = (f32[16,16]{1,0:T(8,128)S(1)}, f32[16,16]{1,0:T(8,128)S(1)}, u32[]{:S(2)}, u32[]{:S(2)}) collective-permute-start(f32[16,16]{1,0:T(8,128)S(1)} %get-tuple-element.12), channel_id=1, source_target_pairs={{0,2},{1,9},{2,0},{3,11},{4,6},{5,13},{6,4},{7,15},{8,10},{9,1},{1... | collective-permute-start | bytes 3080 | tf_op jit(solution)/shard_map/ppermute | solution.py:250
  28.7 0.0 collective-permute-start.11
  28.7 0.6 %collective-permute-done.10 = f32[16,16]{1,0:T(8,128)S(1)} collective-permute-done((f32[16,16]{1,0:T(8,128)S(1)}, f32[16,16]{1,0:T(8,128)S(1)}, u32[]{:S(2)}, u32[]{:S(2)}) %collective-permute-start.10) | collective-permute-done | bytes 1056 | tf_op jit(solution)/shard_map/ppermute | solution.py:250
  29.3 1.0 %collective-permute-done.8 = f32[16,16]{1,0:T(8,128)S(1)} collective-permute-done((f32[16,16]{1,0:T(8,128)S(1)}, f32[16,16]{1,0:T(8,128)S(1)}, u32[]{:S(2)}, u32[]{:S(2)}) %collective-permute-start.8) | collective-permute-done | bytes 1056 | tf_op jit(solution)/shard_map/ppermute | solution.py:250
  30.3 1.0 %collective-permute-done.9 = f32[16,16]{1,0:T(8,128)S(1)} collective-permute-done((f32[16,16]{1,0:T(8,128)S(1)}, f32[16,16]{1,0:T(8,128)S(1)}, u32[]{:S(2)}, u32[]{:S(2)}) %collective-permute-start.9) | collective-permute-done | bytes 1056 | tf_op jit(solution)/shard_map/ppermute | solution.py:250
  31.3 0.6 %collective-permute-start.12 = (f32[16,16]{1,0:T(8,128)S(1)}, f32[16,16]{1,0:T(8,128)S(1)}, u32[]{:S(2)}, u32[]{:S(2)}) collective-permute-start(f32[16,16]{1,0:T(8,128)S(1)} %add_add_fusion.refs_1_), channel_id=1, source_target_pairs={{0,1},{1,0},{2,3},{3,2},{4,5},{5,4},{6,7},{7,6},{8,9},{9,8},{10,11... | collective-permute-start | bytes 3080 | tf_op jit(solution)/shard_map/ppermute | solution.py:229
  31.9 0.8 %collective-permute-done.12.refs_3_ = f32[16,16]{1,0:T(8,128)S(1)} collective-permute-done((f32[16,16]{1,0:T(8,128)S(1)}, f32[16,16]{1,0:T(8,128)S(1)}, u32[]{:S(2)}, u32[]{:S(2)}) %collective-permute-start.12) | collective-permute-done | bytes 1056 | tf_op jit(solution)/shard_map/ppermute | solution.py:229
  32.7 0.0 collective-permute-done.11.refs_2_
  32.7 0.9 %shard_map.54 = (f32[16,512]{1,0:T(8,128)}, f32[16,16]{1,0:T(8,128)}) custom-call(f32[2,16,256]{2,1,0:T(8,128)S(1)} %get-tuple-element.11.refs_0_, f32[16,16]{1,0:T(8,128)S(1)} %add_add_fusion.refs_1_, f32[2,16,256]{2,1,0:T(8,128)S(1)} %collective-permute-done.11.refs_2_, f32[16,16]{1,0:T(8,128)S(1)} %collective-permute-done.12.refs_3_), custom_call_target="tpu_custom_call" | custom-call | tf_op jit(solution)/shard_map/pallas_call | solution.py:215
  (3 shorter events, 0.0 us)
Async XLA Ops:
  0.6 5.7 %collective-permute-start = (f32[16,512]{1,0:T(8,128)}, f32[16,512]{1,0:T(8,128)S(1)}, u32[]{:S(2)}, u32[]{:S(2)}) collective-permute-start(f32[16,512]{1,0:T(8,128)} %refs_0_.1), channel_id=1, source_target_pairs={{0,1},{1,0},{2,3},{3,2},{4,5},{5,4},{6,7},{7,6},{8,9},{9,8},{10,11... | collective-permute-start | bytes 98312 | tf_op jit(solution)/shard_map/ppermute | solution.py:229
  1.1 5.2 %collective-permute-start.1 = (f32[16,512]{1,0:T(8,128)}, f32[16,512]{1,0:T(8,128)S(1)}, u32[]{:S(2)}, u32[]{:S(2)}) collective-permute-start(f32[16,512]{1,0:T(8,128)} %refs_0_.1), channel_id=1, source_target_pairs={{0,2},{1,3},{2,0},{3,1},{4,6},{5,7},{6,4},{7,5},{8,10},{9,11},{10,... | collective-permute-start | bytes 98312 | tf_op jit(solution)/shard_map/ppermute | solution.py:229
  3.7 3.6 %collective-permute-start.2 = (f32[16,512]{1,0:T(8,128)}, f32[16,512]{1,0:T(8,128)S(1)}, u32[]{:S(2)}, u32[]{:S(2)}) collective-permute-start(f32[16,512]{1,0:T(8,128)} %refs_0_.1), channel_id=1, source_target_pairs={{0,3},{1,2},{2,1},{3,0},{4,7},{5,6},{6,5},{7,4},{8,11},{9,10},{10,... | collective-permute-start | bytes 98312 | tf_op jit(solution)/shard_map/ppermute | solution.py:229
  3.8 3.5 %copy-start = (f32[16,512]{1,0:T(8,128)S(1)}, f32[16,512]{1,0:T(8,128)}, u32[]{:S(2)}) copy-start(f32[16,512]{1,0:T(8,128)} %refs_0_.1) | copy-start | bytes 98308
  3.8 3.5 %copy-start.1 = (s32[1,1,16]{2,1,0:T(1,128)S(1)}, s32[1,1,16]{2,1,0:T(1,128)}, u32[]{:S(2)}) copy-start(s32[1,1,16]{2,1,0:T(1,128)} %param.4) | copy-start | bytes 196
  8.8 6.2 %collective-permute-start.3 = (f32[4,16,256]{2,1,0:T(8,128)S(1)}, f32[4,16,256]{2,1,0:T(8,128)S(1)}, u32[]{:S(2)}, u32[]{:S(2)}) collective-permute-start(f32[4,16,256]{2,1,0:T(8,128)S(1)} %shard_map.51.refs_3_), channel_id=1, source_target_pairs={{0,12},{1,9},{2,14},{3,11},{4,8},{5,13},{6,10},{7,15},{8,4},{9,1},... | collective-permute-start | bytes 196616 | tf_op jit(solution)/shard_map/ppermute | solution.py:250
  12.4 5.5 %collective-permute-start.4 = (f32[4,16,256]{2,1,0:T(8,128)S(1)}, f32[4,16,256]{2,1,0:T(8,128)S(1)}, u32[]{:S(2)}, u32[]{:S(2)}) collective-permute-start(f32[4,16,256]{2,1,0:T(8,128)S(1)} %shard_map.51.refs_3_), channel_id=1, source_target_pairs={{0,4},{1,13},{2,6},{3,15},{4,0},{5,9},{6,2},{7,11},{8,12},{9,5},{1... | collective-permute-start | bytes 196616 | tf_op jit(solution)/shard_map/ppermute | solution.py:250
  12.4 5.5 %collective-permute-start.5 = (f32[4,16,256]{2,1,0:T(8,128)S(1)}, f32[4,16,256]{2,1,0:T(8,128)S(1)}, u32[]{:S(2)}, u32[]{:S(2)}) collective-permute-start(f32[4,16,256]{2,1,0:T(8,128)S(1)} %shard_map.51.refs_3_), channel_id=1, source_target_pairs={{0,8},{1,5},{2,10},{3,7},{4,12},{5,1},{6,14},{7,3},{8,0},{9,13},{1... | collective-permute-start | bytes 196616 | tf_op jit(solution)/shard_map/ppermute | solution.py:250
  19.2 1.4 %collective-permute-start.6 = (f32[8,16,256]{2,1,0:T(8,128)S(1)}, f32[8,16,256]{2,1,0:T(8,128)S(1)}, u32[]{:S(2)}, u32[]{:S(2)}) collective-permute-start(f32[8,16,256]{2,1,0:T(8,128)S(1)} %shard_map.52), channel_id=1, source_target_pairs={{0,1},{1,0},{2,3},{3,2},{4,5},{5,4},{6,7},{7,6},{8,9},{9,8},{10,11... | collective-permute-start | bytes 393224 | tf_op jit(solution)/shard_map/ppermute | solution.py:229
  20.6 5.0 %collective-permute-start.7 = (f32[8,16,256]{2,1,0:T(8,128)S(1)}, f32[8,16,256]{2,1,0:T(8,128)S(1)}, u32[]{:S(2)}, u32[]{:S(2)}) collective-permute-start(f32[8,16,256]{2,1,0:T(8,128)S(1)} %add.12.refs_0_), channel_id=1, source_target_pairs={{0,4},{1,3},{2,6},{3,1},{4,0},{5,7},{6,2},{7,5},{8,12},{9,11},{10,... | collective-permute-start | bytes 393224 | tf_op jit(solution)/shard_map/ppermute | solution.py:250
  25.6 3.7 %collective-permute-start.10 = (f32[16,16]{1,0:T(8,128)S(1)}, f32[16,16]{1,0:T(8,128)S(1)}, u32[]{:S(2)}, u32[]{:S(2)}) collective-permute-start(f32[16,16]{1,0:T(8,128)S(1)} %get-tuple-element.12), channel_id=1, source_target_pairs={{0,2},{1,5},{2,0},{3,7},{4,6},{5,1},{6,4},{7,3},{8,10},{9,13},{10,... | collective-permute-start | bytes 3080 | tf_op jit(solution)/shard_map/ppermute | solution.py:250
  26.6 3.7 %collective-permute-start.8 = (f32[16,16]{1,0:T(8,128)S(1)}, f32[16,16]{1,0:T(8,128)S(1)}, u32[]{:S(2)}, u32[]{:S(2)}) collective-permute-start(f32[16,16]{1,0:T(8,128)S(1)} %get-tuple-element.12), channel_id=1, source_target_pairs={{0,2},{1,13},{2,0},{3,15},{4,6},{5,9},{6,4},{7,11},{8,10},{9,5},{1... | collective-permute-start | bytes 3080 | tf_op jit(solution)/shard_map/ppermute | solution.py:250
  27.6 3.7 %collective-permute-start.9 = (f32[16,16]{1,0:T(8,128)S(1)}, f32[16,16]{1,0:T(8,128)S(1)}, u32[]{:S(2)}, u32[]{:S(2)}) collective-permute-start(f32[16,16]{1,0:T(8,128)S(1)} %get-tuple-element.12), channel_id=1, source_target_pairs={{0,2},{1,9},{2,0},{3,11},{4,6},{5,13},{6,4},{7,15},{8,10},{9,1},{1... | collective-permute-start | bytes 3080 | tf_op jit(solution)/shard_map/ppermute | solution.py:250
  28.7 4.0 %collective-permute-start.11 = (f32[2,16,256]{2,1,0:T(8,128)S(1)}, f32[2,16,256]{2,1,0:T(8,128)S(1)}, u32[]{:S(2)}, u32[]{:S(2)}) collective-permute-start(f32[2,16,256]{2,1,0:T(8,128)S(1)} %get-tuple-element.13), channel_id=1, source_target_pairs={{0,1},{1,0},{2,3},{3,2},{4,5},{5,4},{6,7},{7,6},{8,9},{9,8},{10,11... | collective-permute-start | bytes 98312 | tf_op jit(solution)/shard_map/ppermute | solution.py:229
  31.3 1.4 %collective-permute-start.12 = (f32[16,16]{1,0:T(8,128)S(1)}, f32[16,16]{1,0:T(8,128)S(1)}, u32[]{:S(2)}, u32[]{:S(2)}) collective-permute-start(f32[16,16]{1,0:T(8,128)S(1)} %add_add_fusion.refs_1_), channel_id=1, source_target_pairs={{0,1},{1,0},{2,3},{3,2},{4,5},{5,4},{6,7},{7,6},{8,9},{9,8},{10,11... | collective-permute-start | bytes 3080 | tf_op jit(solution)/shard_map/ppermute | solution.py:229

commit v4 on v3

--- a/solution.py
+++ b/solution.py
@@ -38,8 +38,10 @@
     return high, low
 
 
-def split_kernel(blocks_ref, high_ref, low_ref, high_t_ref, held_ref, sems):
+def split_kernel(blocks_ref, slot_ref, high_ref, low_ref, high_t_ref, place_ref, held_ref, sems, slot_sem):
     count = blocks_ref.shape[0]
+    place = pltpu.make_async_copy(slot_ref, place_ref, slot_sem)
+    place.start()
     copies = [pltpu.make_async_copy(blocks_ref.at[i], held_ref.at[i], sems.at[i]) for i in range(count)]
     for copy in copies:
         copy.start()
@@ -48,9 +50,10 @@
         high, low = halves(held_ref[i])
         high_ref[i], low_ref[i] = high, low
         high_t_ref[i] = high.T
-
-
-def split_blocks(blocks):
+    place.wait()
+
+
+def split_blocks(blocks, slot):
     n, rows, cols = blocks.shape
     return pl.pallas_call(
         split_kernel,
@@ -58,13 +61,18 @@
             pltpu.VMEM(blocks.shape, jnp.bfloat16),
             pltpu.VMEM(blocks.shape, jnp.bfloat16),
             pltpu.VMEM(blocks.shape, jnp.bfloat16),
+            pltpu.SMEM(slot.shape, jnp.int32),
         ),
-        in_specs=[pl.BlockSpec(memory_space=pltpu.HBM)],
-        out_specs=(vmem(), vmem(), vmem()),
-        scratch_shapes=[pltpu.VMEM(blocks.shape, jnp.float32), pltpu.SemaphoreType.DMA((n,))],
+        in_specs=[pl.BlockSpec(memory_space=pltpu.HBM)] * 2,
+        out_specs=(vmem(), vmem(), vmem(), smem()),
+        scratch_shapes=[
+            pltpu.VMEM(blocks.shape, jnp.float32),
+            pltpu.SemaphoreType.DMA((n,)),
+            pltpu.SemaphoreType.DMA,
+        ],
         compiler_params=params(),
         cost_estimate=pl.CostEstimate(flops=3 * n * rows * cols, bytes_accessed=8 * n * rows * cols, transcendentals=0),
-    )(pltpu.with_memory_space_constraint(blocks, pltpu.HBM))
+    )(*[pltpu.with_memory_space_constraint(x, pltpu.HBM) for x in (blocks, slot)])
 
 
 def store_halves(ref, index, x):
@@ -279,9 +287,9 @@
     share = basis_in.shape[1]
     column_count = share * lax.axis_size(GROUP) // edge
     slot = block_slot.reshape(nblk)
-    high, low, high_t = [
-        pltpu.with_memory_space_constraint(x, pltpu.VMEM) for x in split_blocks(blocks.reshape(nblk, edge, edge))
-    ]
+    *split, slot = split_blocks(blocks.reshape(nblk, edge, edge), slot)
+    high, low, high_t = [pltpu.with_memory_space_constraint(x, pltpu.VMEM) for x in split]
+    slot = pltpu.with_memory_space_constraint(slot, pltpu.SMEM)
     ypart = rows_product(slot, high_t, low, gather(basis_in, GROUP))
     scale = math.sqrt(share * lax.axis_size(("col",) + GROUP))
     sizes = tuple(lax.axis_size(a) for a in ("col", "row", "sub"))

time: 33.8 us -> 32.7 us (0.967)
  Pallas kernels: 6.31 us -> 5.24 us
    pallas_call x1, Pallas kernels: 1.55 us -> 1 us  [rows_product(): pl.pallas_call(rows_kernel, out_shape=jax.ShapeDtypeStruct((RBL, count, e...]
    pallas_call x1, Pallas kernels: 1.27 us -> 0.73 us  [cols_product(): pl.pallas_call(lambda *refs: cols_kernel(column_count, *refs), out_shape=...]
where the time goes in v4:
time: 32.7 us; the launch traced here: 32.5 us
  waiting for transfers between devices  13.7 us (42%)
  starting transfers between devices  12.9 us (39%)
  Pallas kernels  5.24 us (16%)
  between operations  0.68 us (2%)
    ppermute x7, waiting for transfers between devices, exchange(): return lax.ppermute(x, ('col', 'row', 'sub'), pairs)  10.6 us
    ppermute x7, starting transfers between devices, exchange(): return lax.ppermute(x, ('col', 'row', 'sub'), pairs)  9.21 us
    ppermute x6, starting transfers between devices, partner(): return lax.ppermute(x, axes, [(i, i ^ k) for i in range(n)])  3.73 us
    ppermute x6, waiting for transfers between devices, partner(): return lax.ppermute(x, axes, [(i, i ^ k) for i in range(n)])  3.07 us
    pallas_call x1, Pallas kernels, split_blocks(): pl.pallas_call(split_kernel, out_shape=(pltpu.VMEM(blocks.shape, jnp.bflo...  2.56 us
    pallas_call x1, Pallas kernels, rows_product(): pl.pallas_call(rows_kernel, out_shape=jax.ShapeDtypeStruct((RBL, count, e...  1 us
    pallas_call x1, Pallas kernels, solve(): pl.pallas_call(lambda *refs: solve_kernel(scale, *refs), out_shape=(jax.S...  0.94 us
    pallas_call x1, Pallas kernels, cols_product(): pl.pallas_call(lambda *refs: cols_kernel(column_count, *refs), out_shape=...  0.73 us
  transfers between devices with their start and end apart: 13, of which 9 were waited for; matrix products, arithmetic and copies ran while one was open for 0% of the time, Pallas kernels for 8%

profile of v4, /device:TPU:0, one launch (start us, length us, event | category | flops | bytes accessed | tf_op | source)
XLA Modules:
  0.0 32.5 jit_solution(1154319276589427118)
XLA Ops:
  0.6 0.5 %collective-permute-start = (f32[16,512]{1,0:T(8,128)}, f32[16,512]{1,0:T(8,128)S(1)}, u32[]{:S(2)}, u32[]{:S(2)}) collective-permute-start(f32[16,512]{1,0:T(8,128)} %refs_0_.1), channel_id=1, source_target_pairs={{0,1},{1,0},{2,3},{3,2},{4,5},{5,4},{6,7},{7,6},{8,9},{9,8},{10,11... | collective-permute-start | bytes 98312 | tf_op jit(solution)/shard_map/ppermute | solution.py:237
  1.1 2.6 %collective-permute-start.1 = (f32[16,512]{1,0:T(8,128)}, f32[16,512]{1,0:T(8,128)S(1)}, u32[]{:S(2)}, u32[]{:S(2)}) collective-permute-start(f32[16,512]{1,0:T(8,128)} %refs_0_.1), channel_id=1, source_target_pairs={{0,2},{1,3},{2,0},{3,1},{4,6},{5,7},{6,4},{7,5},{8,10},{9,11},{10,... | collective-permute-start | bytes 98312 | tf_op jit(solution)/shard_map/ppermute | solution.py:237
  3.7 0.1 collective-permute-start.2
  3.8 0.0 copy-start
  3.8 2.6 %shard_map.50 = (bf16[16,256,256]{2,1,0:T(8,128)(2,1)S(1)}, bf16[16,256,256]{2,1,0:T(8,128)(2,1)S(1)}, bf16[16,256,256]{2,1,0:T(8,128)(2,1)S(1)}, s32[16]{0:T(128)S(4)}) custom-call(f32[16,256,256]{2,1,0:T(8,128)} %bitcast.2, s32[16]{0:T(128)} %bitcast.3), custom_call_target="tpu_custom_call" | custom-call | flops 3145728 | bytes 8388608 | tf_op jit(solution)/shard_map/pallas_call | solution.py:58
  6.4 0.0 collective-permute-done.refs_1_
  6.4 0.0 collective-permute-done.1.refs_2_
  6.4 0.9 %collective-permute-done.2.refs_3_ = f32[16,512]{1,0:T(8,128)S(1)} collective-permute-done((f32[16,512]{1,0:T(8,128)}, f32[16,512]{1,0:T(8,128)S(1)}, u32[]{:S(2)}, u32[]{:S(2)}) %collective-permute-start.2) | collective-permute-done | bytes 32800 | tf_op jit(solution)/shard_map/ppermute | solution.py:237
  7.3 0.0 copy-done
  7.3 1.0 %shard_map.51.refs_3_ = f32[4,16,256]{2,1,0:T(8,128)S(1)} custom-call(s32[16]{0:T(128)S(4)} %get-tuple-element.9.slot_ref.refs_0_, bf16[16,256,256]{2,1,0:T(8,128)(2,1)S(1)} %get-tuple-element.12.high_ref, bf16[16,256,256]{2,1,0:T(8,128)(2,1)S(1)} %get-tuple-element.11.low_ref.refs_2_, f32[16,512]{1,0:T(8,128)S(1)} %copy-done, ...), custom_call_target="tpu_custom_call" | custom-call | tf_op jit(solution)/shard_map/pallas_call | solution.py:112
  8.3 3.6 %collective-permute-start.3 = (f32[4,16,256]{2,1,0:T(8,128)S(1)}, f32[4,16,256]{2,1,0:T(8,128)S(1)}, u32[]{:S(2)}, u32[]{:S(2)}) collective-permute-start(f32[4,16,256]{2,1,0:T(8,128)S(1)} %shard_map.51.refs_3_), channel_id=1, source_target_pairs={{0,12},{1,9},{2,14},{3,11},{4,8},{5,13},{6,10},{7,15},{8,4},{9,1},... | collective-permute-start | bytes 196616 | tf_op jit(solution)/shard_map/ppermute | solution.py:258
  11.9 0.0 collective-permute-start.4
  11.9 0.8 %collective-permute-start.5 = (f32[4,16,256]{2,1,0:T(8,128)S(1)}, f32[4,16,256]{2,1,0:T(8,128)S(1)}, u32[]{:S(2)}, u32[]{:S(2)}) collective-permute-start(f32[4,16,256]{2,1,0:T(8,128)S(1)} %shard_map.51.refs_3_), channel_id=1, source_target_pairs={{0,8},{1,5},{2,10},{3,7},{4,12},{5,1},{6,14},{7,3},{8,0},{9,13},{1... | collective-permute-start | bytes 196616 | tf_op jit(solution)/shard_map/ppermute | solution.py:258
  12.7 1.8 %collective-permute-done.3.refs_4_ = f32[4,16,256]{2,1,0:T(8,128)S(1)} collective-permute-done((f32[4,16,256]{2,1,0:T(8,128)S(1)}, f32[4,16,256]{2,1,0:T(8,128)S(1)}, u32[]{:S(2)}, u32[]{:S(2)}) %collective-permute-start.3) | collective-permute-done | bytes 65568 | tf_op jit(solution)/shard_map/ppermute | solution.py:258
  14.5 2.9 %collective-permute-done.4.refs_5_ = f32[4,16,256]{2,1,0:T(8,128)S(1)} collective-permute-done((f32[4,16,256]{2,1,0:T(8,128)S(1)}, f32[4,16,256]{2,1,0:T(8,128)S(1)}, u32[]{:S(2)}, u32[]{:S(2)}) %collective-permute-start.4) | collective-permute-done | bytes 65568 | tf_op jit(solution)/shard_map/ppermute | solution.py:258
  17.4 0.0 collective-permute-done.5.refs_6_
  17.4 0.7 %shard_map.52 = f32[8,16,256]{2,1,0:T(8,128)S(1)} custom-call(s32[16]{0:T(128)S(4)} %get-tuple-element.9.slot_ref.refs_0_, bf16[16,256,256]{2,1,0:T(8,128)(2,1)S(1)} %get-tuple-element.10.refs_1_, bf16[16,256,256]{2,1,0:T(8,128)(2,1)S(1)} %get-tuple-element.11.low_ref.refs_2_, f32[4,16,256]{2,1,0:T(8,128)S(1)} %shard_map.51.refs_3_, ...), custom_call_target="tpu_custom_call" | custom-call | tf_op jit(solution)/shard_map/pallas_call | solution.py:139
  18.1 0.0 collective-permute-start.6
  18.1 1.3 %collective-permute-done.6 = f32[8,16,256]{2,1,0:T(8,128)S(1)} collective-permute-done((f32[8,16,256]{2,1,0:T(8,128)S(1)}, f32[8,16,256]{2,1,0:T(8,128)S(1)}, u32[]{:S(2)}, u32[]{:S(2)}) %collective-permute-start.6) | collective-permute-done | bytes 131104 | tf_op jit(solution)/shard_map/ppermute | solution.py:237
  19.5 1.8 %collective-permute-start.7 = (f32[8,16,256]{2,1,0:T(8,128)S(1)}, f32[8,16,256]{2,1,0:T(8,128)S(1)}, u32[]{:S(2)}, u32[]{:S(2)}) collective-permute-start(f32[8,16,256]{2,1,0:T(8,128)S(1)} %add.12.refs_0_), channel_id=1, source_target_pairs={{0,4},{1,3},{2,6},{3,1},{4,0},{5,7},{6,2},{7,5},{8,12},{9,11},{10,... | collective-permute-start | bytes 393224 | tf_op jit(solution)/shard_map/ppermute | solution.py:258
  21.2 3.3 %collective-permute-done.7.refs_1_ = f32[8,16,256]{2,1,0:T(8,128)S(1)} collective-permute-done((f32[8,16,256]{2,1,0:T(8,128)S(1)}, f32[8,16,256]{2,1,0:T(8,128)S(1)}, u32[]{:S(2)}, u32[]{:S(2)}) %collective-permute-start.7) | collective-permute-done | bytes 131104 | tf_op jit(solution)/shard_map/ppermute | solution.py:258
  24.5 1.0 %collective-permute-start.10 = (f32[16,16]{1,0:T(8,128)S(1)}, f32[16,16]{1,0:T(8,128)S(1)}, u32[]{:S(2)}, u32[]{:S(2)}) collective-permute-start(f32[16,16]{1,0:T(8,128)S(1)} %get-tuple-element.14), channel_id=1, source_target_pairs={{0,2},{1,5},{2,0},{3,7},{4,6},{5,1},{6,4},{7,3},{8,10},{9,13},{10,... | collective-permute-start | bytes 3080 | tf_op jit(solution)/shard_map/ppermute | solution.py:258
  25.5 1.0 %collective-permute-start.8 = (f32[16,16]{1,0:T(8,128)S(1)}, f32[16,16]{1,0:T(8,128)S(1)}, u32[]{:S(2)}, u32[]{:S(2)}) collective-permute-start(f32[16,16]{1,0:T(8,128)S(1)} %get-tuple-element.14), channel_id=1, source_target_pairs={{0,2},{1,13},{2,0},{3,15},{4,6},{5,9},{6,4},{7,11},{8,10},{9,5},{1... | collective-permute-start | bytes 3080 | tf_op jit(solution)/shard_map/ppermute | solution.py:258
  26.5 1.0 %collective-permute-start.9 = (f32[16,16]{1,0:T(8,128)S(1)}, f32[16,16]{1,0:T(8,128)S(1)}, u32[]{:S(2)}, u32[]{:S(2)}) collective-permute-start(f32[16,16]{1,0:T(8,128)S(1)} %get-tuple-element.14), channel_id=1, source_target_pairs={{0,2},{1,9},{2,0},{3,11},{4,6},{5,13},{6,4},{7,15},{8,10},{9,1},{1... | collective-permute-start | bytes 3080 | tf_op jit(solution)/shard_map/ppermute | solution.py:258
  27.6 0.0 collective-permute-start.11
  27.6 0.6 %collective-permute-done.10 = f32[16,16]{1,0:T(8,128)S(1)} collective-permute-done((f32[16,16]{1,0:T(8,128)S(1)}, f32[16,16]{1,0:T(8,128)S(1)}, u32[]{:S(2)}, u32[]{:S(2)}) %collective-permute-start.10) | collective-permute-done | bytes 1056 | tf_op jit(solution)/shard_map/ppermute | solution.py:258
  28.2 1.0 %collective-permute-done.8 = f32[16,16]{1,0:T(8,128)S(1)} collective-permute-done((f32[16,16]{1,0:T(8,128)S(1)}, f32[16,16]{1,0:T(8,128)S(1)}, u32[]{:S(2)}, u32[]{:S(2)}) %collective-permute-start.8) | collective-permute-done | bytes 1056 | tf_op jit(solution)/shard_map/ppermute | solution.py:258
  29.2 1.0 %collective-permute-done.9 = f32[16,16]{1,0:T(8,128)S(1)} collective-permute-done((f32[16,16]{1,0:T(8,128)S(1)}, f32[16,16]{1,0:T(8,128)S(1)}, u32[]{:S(2)}, u32[]{:S(2)}) %collective-permute-start.9) | collective-permute-done | bytes 1056 | tf_op jit(solution)/shard_map/ppermute | solution.py:258
  30.2 0.6 %collective-permute-start.12 = (f32[16,16]{1,0:T(8,128)S(1)}, f32[16,16]{1,0:T(8,128)S(1)}, u32[]{:S(2)}, u32[]{:S(2)}) collective-permute-start(f32[16,16]{1,0:T(8,128)S(1)} %add_add_fusion.refs_1_), channel_id=1, source_target_pairs={{0,1},{1,0},{2,3},{3,2},{4,5},{5,4},{6,7},{7,6},{8,9},{9,8},{10,11... | collective-permute-start | bytes 3080 | tf_op jit(solution)/shard_map/ppermute | solution.py:237
  30.8 0.8 %collective-permute-done.12.refs_3_ = f32[16,16]{1,0:T(8,128)S(1)} collective-permute-done((f32[16,16]{1,0:T(8,128)S(1)}, f32[16,16]{1,0:T(8,128)S(1)}, u32[]{:S(2)}, u32[]{:S(2)}) %collective-permute-start.12) | collective-permute-done | bytes 1056 | tf_op jit(solution)/shard_map/ppermute | solution.py:237
  31.6 0.0 collective-permute-done.11.refs_2_
  31.6 0.9 %shard_map.54 = (f32[16,512]{1,0:T(8,128)}, f32[16,16]{1,0:T(8,128)}) custom-call(f32[2,16,256]{2,1,0:T(8,128)S(1)} %get-tuple-element.13.refs_0_, f32[16,16]{1,0:T(8,128)S(1)} %add_add_fusion.refs_1_, f32[2,16,256]{2,1,0:T(8,128)S(1)} %collective-permute-done.11.refs_2_, f32[16,16]{1,0:T(8,128)S(1)} %collective-permute-done.12.refs_3_), custom_call_target="tpu_custom_call" | custom-call | tf_op jit(solution)/shard_map/pallas_call | solution.py:223
  (3 shorter events, 0.0 us)
Async XLA Ops:
  0.6 5.7 %collective-permute-start = (f32[16,512]{1,0:T(8,128)}, f32[16,512]{1,0:T(8,128)S(1)}, u32[]{:S(2)}, u32[]{:S(2)}) collective-permute-start(f32[16,512]{1,0:T(8,128)} %refs_0_.1), channel_id=1, source_target_pairs={{0,1},{1,0},{2,3},{3,2},{4,5},{5,4},{6,7},{7,6},{8,9},{9,8},{10,11... | collective-permute-start | bytes 98312 | tf_op jit(solution)/shard_map/ppermute | solution.py:237
  1.1 5.2 %collective-permute-start.1 = (f32[16,512]{1,0:T(8,128)}, f32[16,512]{1,0:T(8,128)S(1)}, u32[]{:S(2)}, u32[]{:S(2)}) collective-permute-start(f32[16,512]{1,0:T(8,128)} %refs_0_.1), channel_id=1, source_target_pairs={{0,2},{1,3},{2,0},{3,1},{4,6},{5,7},{6,4},{7,5},{8,10},{9,11},{10,... | collective-permute-start | bytes 98312 | tf_op jit(solution)/shard_map/ppermute | solution.py:237
  3.7 3.6 %collective-permute-start.2 = (f32[16,512]{1,0:T(8,128)}, f32[16,512]{1,0:T(8,128)S(1)}, u32[]{:S(2)}, u32[]{:S(2)}) collective-permute-start(f32[16,512]{1,0:T(8,128)} %refs_0_.1), channel_id=1, source_target_pairs={{0,3},{1,2},{2,1},{3,0},{4,7},{5,6},{6,5},{7,4},{8,11},{9,10},{10,... | collective-permute-start | bytes 98312 | tf_op jit(solution)/shard_map/ppermute | solution.py:237
  3.8 3.5 %copy-start = (f32[16,512]{1,0:T(8,128)S(1)}, f32[16,512]{1,0:T(8,128)}, u32[]{:S(2)}) copy-start(f32[16,512]{1,0:T(8,128)} %refs_0_.1) | copy-start | bytes 98308
  8.3 6.2 %collective-permute-start.3 = (f32[4,16,256]{2,1,0:T(8,128)S(1)}, f32[4,16,256]{2,1,0:T(8,128)S(1)}, u32[]{:S(2)}, u32[]{:S(2)}) collective-permute-start(f32[4,16,256]{2,1,0:T(8,128)S(1)} %shard_map.51.refs_3_), channel_id=1, source_target_pairs={{0,12},{1,9},{2,14},{3,11},{4,8},{5,13},{6,10},{7,15},{8,4},{9,1},... | collective-permute-start | bytes 196616 | tf_op jit(solution)/shard_map/ppermute | solution.py:258
  11.9 5.5 %collective-permute-start.4 = (f32[4,16,256]{2,1,0:T(8,128)S(1)}, f32[4,16,256]{2,1,0:T(8,128)S(1)}, u32[]{:S(2)}, u32[]{:S(2)}) collective-permute-start(f32[4,16,256]{2,1,0:T(8,128)S(1)} %shard_map.51.refs_3_), channel_id=1, source_target_pairs={{0,4},{1,13},{2,6},{3,15},{4,0},{5,9},{6,2},{7,11},{8,12},{9,5},{1... | collective-permute-start | bytes 196616 | tf_op jit(solution)/shard_map/ppermute | solution.py:258
  11.9 5.5 %collective-permute-start.5 = (f32[4,16,256]{2,1,0:T(8,128)S(1)}, f32[4,16,256]{2,1,0:T(8,128)S(1)}, u32[]{:S(2)}, u32[]{:S(2)}) collective-permute-start(f32[4,16,256]{2,1,0:T(8,128)S(1)} %shard_map.51.refs_3_), channel_id=1, source_target_pairs={{0,8},{1,5},{2,10},{3,7},{4,12},{5,1},{6,14},{7,3},{8,0},{9,13},{1... | collective-permute-start | bytes 196616 | tf_op jit(solution)/shard_map/ppermute | solution.py:258
  18.1 1.4 %collective-permute-start.6 = (f32[8,16,256]{2,1,0:T(8,128)S(1)}, f32[8,16,256]{2,1,0:T(8,128)S(1)}, u32[]{:S(2)}, u32[]{:S(2)}) collective-permute-start(f32[8,16,256]{2,1,0:T(8,128)S(1)} %shard_map.52), channel_id=1, source_target_pairs={{0,1},{1,0},{2,3},{3,2},{4,5},{5,4},{6,7},{7,6},{8,9},{9,8},{10,11... | collective-permute-start | bytes 393224 | tf_op jit(solution)/shard_map/ppermute | solution.py:237
  19.5 5.0 %collective-permute-start.7 = (f32[8,16,256]{2,1,0:T(8,128)S(1)}, f32[8,16,256]{2,1,0:T(8,128)S(1)}, u32[]{:S(2)}, u32[]{:S(2)}) collective-permute-start(f32[8,16,256]{2,1,0:T(8,128)S(1)} %add.12.refs_0_), channel_id=1, source_target_pairs={{0,4},{1,3},{2,6},{3,1},{4,0},{5,7},{6,2},{7,5},{8,12},{9,11},{10,... | collective-permute-start | bytes 393224 | tf_op jit(solution)/shard_map/ppermute | solution.py:258
  24.5 3.7 %collective-permute-start.10 = (f32[16,16]{1,0:T(8,128)S(1)}, f32[16,16]{1,0:T(8,128)S(1)}, u32[]{:S(2)}, u32[]{:S(2)}) collective-permute-start(f32[16,16]{1,0:T(8,128)S(1)} %get-tuple-element.14), channel_id=1, source_target_pairs={{0,2},{1,5},{2,0},{3,7},{4,6},{5,1},{6,4},{7,3},{8,10},{9,13},{10,... | collective-permute-start | bytes 3080 | tf_op jit(solution)/shard_map/ppermute | solution.py:258
  25.5 3.7 %collective-permute-start.8 = (f32[16,16]{1,0:T(8,128)S(1)}, f32[16,16]{1,0:T(8,128)S(1)}, u32[]{:S(2)}, u32[]{:S(2)}) collective-permute-start(f32[16,16]{1,0:T(8,128)S(1)} %get-tuple-element.14), channel_id=1, source_target_pairs={{0,2},{1,13},{2,0},{3,15},{4,6},{5,9},{6,4},{7,11},{8,10},{9,5},{1... | collective-permute-start | bytes 3080 | tf_op jit(solution)/shard_map/ppermute | solution.py:258
  26.5 3.7 %collective-permute-start.9 = (f32[16,16]{1,0:T(8,128)S(1)}, f32[16,16]{1,0:T(8,128)S(1)}, u32[]{:S(2)}, u32[]{:S(2)}) collective-permute-start(f32[16,16]{1,0:T(8,128)S(1)} %get-tuple-element.14), channel_id=1, source_target_pairs={{0,2},{1,9},{2,0},{3,11},{4,6},{5,13},{6,4},{7,15},{8,10},{9,1},{1... | collective-permute-start | bytes 3080 | tf_op jit(solution)/shard_map/ppermute | solution.py:258
  27.6 4.0 %collective-permute-start.11 = (f32[2,16,256]{2,1,0:T(8,128)S(1)}, f32[2,16,256]{2,1,0:T(8,128)S(1)}, u32[]{:S(2)}, u32[]{:S(2)}) collective-permute-start(f32[2,16,256]{2,1,0:T(8,128)S(1)} %get-tuple-element.15), channel_id=1, source_target_pairs={{0,1},{1,0},{2,3},{3,2},{4,5},{5,4},{6,7},{7,6},{8,9},{9,8},{10,11... | collective-permute-start | bytes 98312 | tf_op jit(solution)/shard_map/ppermute | solution.py:237
  30.2 1.4 %collective-permute-start.12 = (f32[16,16]{1,0:T(8,128)S(1)}, f32[16,16]{1,0:T(8,128)S(1)}, u32[]{:S(2)}, u32[]{:S(2)}) collective-permute-start(f32[16,16]{1,0:T(8,128)S(1)} %add_add_fusion.refs_1_), channel_id=1, source_target_pairs={{0,1},{1,0},{2,3},{3,2},{4,5},{5,4},{6,7},{7,6},{8,9},{9,8},{10,11... | collective-permute-start | bytes 3080 | tf_op jit(solution)/shard_map/ppermute | solution.py:237

commit v5 on v4

--- a/solution.py
+++ b/solution.py
@@ -11,9 +11,9 @@
 LANES = 128
 GROUP = ("row", "sub")
 LEAD = 1
-COLS = ((0, 1, 2, 3), (1, 0, 3, 2), (2, 3, 0, 1), (3, 2, 1, 0))
+COLS = ((0, 1, 2, 3), (1, 0, 3, 2), (2, 3, 0, 1), (3, 2, 1, 0), (1, 3, 0, 2), (2, 0, 3, 1))
 Y_ORDERS = ((3, 1, 2), (2, 3, 1))
-G_ORDER = (3, 2, 1)
+G_ORDER = (4, 3, 5)
 VMEM_LIMIT = 24 * 1024 * 1024
 
 NT = (((1,), (1,)), ((), ()))
@@ -184,16 +184,8 @@
     )(a, b)
 
 
-def solve_kernel(scale, *refs):
-    z_ref, gram_ref, out_ref, factor_ref = refs[0], refs[1], refs[-2], refs[-1]
-    count, edge = factor_ref.shape[0], z_ref.shape[2]
-    per_share = out_ref.shape[1] // edge
-    g = gram_ref[...]
-    z = [z_ref[h] for h in range(per_share)]
-    if len(refs) > 4:
-        leads = lax.axis_index("sub") == LEAD
-        g = jnp.where(leads, g, refs[3][...])
-        z = [jnp.where(leads, x, refs[2][h]) for h, x in enumerate(z)]
+def eliminate(g, z, scale):
+    count, edge = g.shape[0], z[0].shape[1]
     row_id = lax.broadcasted_iota(jnp.int32, (count, LANES), 0)
     lane_id = lax.broadcasted_iota(jnp.int32, (count, LANES), 1)
     columns = [jnp.broadcast_to(g[:, k:k + 1], (count, LANES)) for k in range(count)]
@@ -213,23 +205,66 @@
             wide_inverse = jnp.concatenate([inverse] * (edge // LANES), 1)
             z = [x - wide * (x[j:j + 1, :] * wide_inverse) for x in z]
     scales = jnp.concatenate([scales * scale] * (edge // LANES), 1)
-    for h in range(per_share):
-        out_ref[:, h * edge:(h + 1) * edge] = z[h] * scales
-    factor_ref[...] = lower[:, :count].T
-
-
-def solve(scale, *arrays):
-    per_share, count, edge = arrays[0].shape
-    return pl.pallas_call(
-        lambda *refs: solve_kernel(scale, *refs),
+    return lower[:, :count].T, [x * scales for x in z]
+
+
+def solve_kernel(scale, lead, z_ref, far_z_ref, *refs):
+    grams, mine_ref, other_ref = refs[:-2], refs[-2], refs[-1]
+    leads = True if lead is None else lax.axis_index("sub") == lead
+    per_share, count, edge = z_ref.shape
+
+    @pl.when(leads)
+    def _():
+        g = grams[0][...]
+        for ref in grams[1:]:
+            g = g + ref[...]
+        factor, z = eliminate(g, [ref[h] for ref in (z_ref, far_z_ref) for h in range(per_share)], scale)
+        for h in range(per_share):
+            mine_ref[:, h * edge:(h + 1) * edge] = z[h]
+            other_ref[:, h * edge:(h + 1) * edge] = z[per_share + h]
+        other_ref[:, per_share * edge:] = jnp.zeros((count, LANES), jnp.float32)
+        other_ref[:, per_share * edge:per_share * edge + count] = factor
+
+    @pl.when(jnp.logical_not(leads))
+    def _():
+        mine_ref[...] = jnp.zeros_like(mine_ref)
+        other_ref[...] = jnp.zeros_like(other_ref)
+
+
+def solve(scale, lead, z, far_z, grams):
+    per_share, count, edge = z.shape
+    share = per_share * edge
+    return pl.pallas_call(
+        lambda *refs: solve_kernel(scale, lead, *refs),
         out_shape=(
-            jax.ShapeDtypeStruct((count, per_share * edge), jnp.float32),
+            jax.ShapeDtypeStruct((count, share), jnp.float32),
+            jax.ShapeDtypeStruct((count, share + LANES), jnp.float32),
+        ),
+        in_specs=[vmem()] * (2 + len(grams)),
+        out_specs=(vmem(), vmem()),
+        compiler_params=params(),
+    )(z, far_z, *grams)
+
+
+def pick_kernel(mine_ref, other_ref, far_ref, out_ref, factor_ref):
+    leads = lax.axis_index("sub") == LEAD
+    share, count = out_ref.shape[1], factor_ref.shape[0]
+    out_ref[...] = jnp.where(leads, mine_ref[...], far_ref[:, :share])
+    factor_ref[...] = jnp.where(leads, other_ref[:, share:share + count], far_ref[:, share:share + count])
+
+
+def pick(mine, other, far):
+    count, share = mine.shape
+    return pl.pallas_call(
+        pick_kernel,
+        out_shape=(
+            jax.ShapeDtypeStruct((count, share), jnp.float32),
             jax.ShapeDtypeStruct((count, count), jnp.float32),
         ),
-        in_specs=[vmem()] * len(arrays),
+        in_specs=[vmem()] * 3,
         out_specs=(vmem(), vmem()),
         compiler_params=params(),
-    )(*arrays)
+    )(mine, other, far)
 
 
 def partner(x, axes, k):
@@ -267,8 +302,9 @@
                 zpart = zpart + partner(zpart, axis, 1 << i)
         else:
             zpart = lax.psum(zpart, axis)
-    z, _, gram = gram_of(zpart, jnp.zeros_like(zpart), per_share, None)
-    return solve(scale, z, lax.psum(gram, "col"))
+    z, other, gram = gram_of(zpart, jnp.zeros_like(zpart), per_share, None)
+    mine, other = solve(scale, None, z, other, [lax.psum(gram, "col")])
+    return mine, other[:, mine.shape[1]:mine.shape[1] + gram.shape[0]]
 
 
 def four_by_two(slot, high, low, ypart, column_count, per_share, scale):
@@ -276,9 +312,9 @@
     zpart = cols_product(slot, high, low, ypieces, column_count)
     zpart = zpart + partner(zpart, "sub", 1)
     z, other, gram = gram_of(zpart, exchange(zpart, ((COLS[1], 0), (COLS[0], 1))), per_share, LEAD)
-    far_z = partner(other, "sub", 1)
-    gram = gram + sum(exchange(gram, ((COLS[0], 1), (COLS[k], 0))) for k in G_ORDER)
-    return solve(scale, z, gram, far_z, partner(gram, "sub", 1))
+    grams = [gram] + [exchange(gram, ((COLS[0], 1), (COLS[k], 0))) for k in G_ORDER]
+    mine, other = solve(scale, LEAD, z, other, grams)
+    return pick(mine, other, partner(other, "sub", 1))
 
 
 def body(blocks, block_slot, basis_in):

time: 32.7 us -> 32.2 us (0.985)
  starting transfers between devices: 12.9 us -> 12.5 us
    ppermute x6 -> x5, starting transfers between devices: 3.73 us -> 3.27 us  [partner(): return lax.ppermute(x, axes, [(i, i ^ k) for i in range(n)])]
    pallas_call x1 -> x2, Pallas kernels: 0.94 us -> 0.63 us  [the longest x1 0.62 us: pick(): pl.pallas_call(pick_kernel, out_shape=(jax.ShapeDtypeStruct((count, share...]
    ppermute x6 -> x5, waiting for transfers between devices: 3.07 us -> 3.35 us  [partner(): return lax.ppermute(x, axes, [(i, i ^ k) for i in range(n)])]
  transfers between devices with their start and end apart: 13 -> 12, of which waited for: 9 -> 9; matrix products, arithmetic and copies ran while one was open for 0% -> 0% of each run, Pallas kernels for 8% -> 8%
where the time goes in v5:
time: 32.2 us; the launch traced here: 32 us
  waiting for transfers between devices  13.9 us (43%)
  starting transfers between devices  12.5 us (39%)
  Pallas kernels  4.93 us (15%)
  between operations  0.68 us (2%)
    ppermute x7, waiting for transfers between devices, exchange(): return lax.ppermute(x, ('col', 'row', 'sub'), pairs)  10.6 us
    ppermute x7, starting transfers between devices, exchange(): return lax.ppermute(x, ('col', 'row', 'sub'), pairs)  9.21 us
    ppermute x5, waiting for transfers between devices, partner(): return lax.ppermute(x, axes, [(i, i ^ k) for i in range(n)])  3.35 us
    ppermute x5, starting transfers between devices, partner(): return lax.ppermute(x, axes, [(i, i ^ k) for i in range(n)])  3.27 us
    pallas_call x1, Pallas kernels, split_blocks(): pl.pallas_call(split_kernel, out_shape=(pltpu.VMEM(blocks.shape, jnp.bflo...  2.56 us
    pallas_call x1, Pallas kernels, rows_product(): pl.pallas_call(rows_kernel, out_shape=jax.ShapeDtypeStruct((RBL, count, e...  1.01 us
    pallas_call x1, Pallas kernels, cols_product(): pl.pallas_call(lambda *refs: cols_kernel(column_count, *refs), out_shape=...  0.73 us
  transfers between devices with their start and end apart: 12, of which 9 were waited for; matrix products, arithmetic and copies ran while one was open for 0% of the time, Pallas kernels for 8%

profile of v5, /device:TPU:0, one launch (start us, length us, event | category | flops | bytes accessed | tf_op | source)
XLA Modules:
  0.0 32.0 jit_solution(13586621265154743461)
XLA Ops:
  0.6 0.5 %collective-permute-start = (f32[16,512]{1,0:T(8,128)}, f32[16,512]{1,0:T(8,128)S(1)}, u32[]{:S(2)}, u32[]{:S(2)}) collective-permute-start(f32[16,512]{1,0:T(8,128)} %refs_0_.1), channel_id=1, source_target_pairs={{0,1},{1,0},{2,3},{3,2},{4,5},{5,4},{6,7},{7,6},{8,9},{9,8},{10,11... | collective-permute-start | bytes 98312 | tf_op jit(solution)/shard_map/ppermute | solution.py:272
  1.1 2.6 %collective-permute-start.1 = (f32[16,512]{1,0:T(8,128)}, f32[16,512]{1,0:T(8,128)S(1)}, u32[]{:S(2)}, u32[]{:S(2)}) collective-permute-start(f32[16,512]{1,0:T(8,128)} %refs_0_.1), channel_id=1, source_target_pairs={{0,2},{1,3},{2,0},{3,1},{4,6},{5,7},{6,4},{7,5},{8,10},{9,11},{10,... | collective-permute-start | bytes 98312 | tf_op jit(solution)/shard_map/ppermute | solution.py:272
  3.7 0.1 collective-permute-start.2
  3.8 0.0 copy-start
  3.8 2.6 %shard_map.50 = (bf16[16,256,256]{2,1,0:T(8,128)(2,1)S(1)}, bf16[16,256,256]{2,1,0:T(8,128)(2,1)S(1)}, bf16[16,256,256]{2,1,0:T(8,128)(2,1)S(1)}, s32[16]{0:T(128)S(4)}) custom-call(f32[16,256,256]{2,1,0:T(8,128)} %bitcast.2, s32[16]{0:T(128)} %bitcast.3), custom_call_target="tpu_custom_call" | custom-call | flops 3145728 | bytes 8388608 | tf_op jit(solution)/shard_map/pallas_call | solution.py:58
  6.4 0.0 collective-permute-done.refs_1_
  6.4 0.0 collective-permute-done.1.refs_2_
  6.4 0.9 %collective-permute-done.2.refs_3_ = f32[16,512]{1,0:T(8,128)S(1)} collective-permute-done((f32[16,512]{1,0:T(8,128)}, f32[16,512]{1,0:T(8,128)S(1)}, u32[]{:S(2)}, u32[]{:S(2)}) %collective-permute-start.2) | collective-permute-done | bytes 32800 | tf_op jit(solution)/shard_map/ppermute | solution.py:272
  7.3 0.0 copy-done
  7.3 1.0 %shard_map.51.refs_3_ = f32[4,16,256]{2,1,0:T(8,128)S(1)} custom-call(s32[16]{0:T(128)S(4)} %get-tuple-element.11.slot_ref.refs_0_, bf16[16,256,256]{2,1,0:T(8,128)(2,1)S(1)} %get-tuple-element.14.high_ref, bf16[16,256,256]{2,1,0:T(8,128)(2,1)S(1)} %get-tuple-element.13.low_ref.refs_2_, f32[16,512]{1,0:T(8,128)S(1)} %copy-done, ...), custom_call_target="tpu_custom_call" | custom-call | tf_op jit(solution)/shard_map/pallas_call | solution.py:112
  8.3 3.6 %collective-permute-start.3 = (f32[4,16,256]{2,1,0:T(8,128)S(1)}, f32[4,16,256]{2,1,0:T(8,128)S(1)}, u32[]{:S(2)}, u32[]{:S(2)}) collective-permute-start(f32[4,16,256]{2,1,0:T(8,128)S(1)} %shard_map.51.refs_3_), channel_id=1, source_target_pairs={{0,12},{1,9},{2,14},{3,11},{4,8},{5,13},{6,10},{7,15},{8,4},{9,1},... | collective-permute-start | bytes 196616 | tf_op jit(solution)/shard_map/ppermute | solution.py:293
  11.9 0.0 collective-permute-start.4
  11.9 0.8 %collective-permute-start.5 = (f32[4,16,256]{2,1,0:T(8,128)S(1)}, f32[4,16,256]{2,1,0:T(8,128)S(1)}, u32[]{:S(2)}, u32[]{:S(2)}) collective-permute-start(f32[4,16,256]{2,1,0:T(8,128)S(1)} %shard_map.51.refs_3_), channel_id=1, source_target_pairs={{0,8},{1,5},{2,10},{3,7},{4,12},{5,1},{6,14},{7,3},{8,0},{9,13},{1... | collective-permute-start | bytes 196616 | tf_op jit(solution)/shard_map/ppermute | solution.py:293
  12.7 1.8 %collective-permute-done.3.refs_4_ = f32[4,16,256]{2,1,0:T(8,128)S(1)} collective-permute-done((f32[4,16,256]{2,1,0:T(8,128)S(1)}, f32[4,16,256]{2,1,0:T(8,128)S(1)}, u32[]{:S(2)}, u32[]{:S(2)}) %collective-permute-start.3) | collective-permute-done | bytes 65568 | tf_op jit(solution)/shard_map/ppermute | solution.py:293
  14.5 2.9 %collective-permute-done.4.refs_5_ = f32[4,16,256]{2,1,0:T(8,128)S(1)} collective-permute-done((f32[4,16,256]{2,1,0:T(8,128)S(1)}, f32[4,16,256]{2,1,0:T(8,128)S(1)}, u32[]{:S(2)}, u32[]{:S(2)}) %collective-permute-start.4) | collective-permute-done | bytes 65568 | tf_op jit(solution)/shard_map/ppermute | solution.py:293
  17.4 0.0 collective-permute-done.5.refs_6_
  17.4 0.7 %shard_map.52 = f32[8,16,256]{2,1,0:T(8,128)S(1)} custom-call(s32[16]{0:T(128)S(4)} %get-tuple-element.11.slot_ref.refs_0_, bf16[16,256,256]{2,1,0:T(8,128)(2,1)S(1)} %get-tuple-element.12.refs_1_, bf16[16,256,256]{2,1,0:T(8,128)(2,1)S(1)} %get-tuple-element.13.low_ref.refs_2_, f32[4,16,256]{2,1,0:T(8,128)S(1)} %shard_map.51.refs_3_, ...), custom_call_target="tpu_custom_call" | custom-call | tf_op jit(solution)/shard_map/pallas_call | solution.py:139
  18.1 0.0 collective-permute-start.6
  18.1 1.3 %collective-permute-done.6 = f32[8,16,256]{2,1,0:T(8,128)S(1)} collective-permute-done((f32[8,16,256]{2,1,0:T(8,128)S(1)}, f32[8,16,256]{2,1,0:T(8,128)S(1)}, u32[]{:S(2)}, u32[]{:S(2)}) %collective-permute-start.6) | collective-permute-done | bytes 131104 | tf_op jit(solution)/shard_map/ppermute | solution.py:272
  19.5 1.8 %collective-permute-start.7 = (f32[8,16,256]{2,1,0:T(8,128)S(1)}, f32[8,16,256]{2,1,0:T(8,128)S(1)}, u32[]{:S(2)}, u32[]{:S(2)}) collective-permute-start(f32[8,16,256]{2,1,0:T(8,128)S(1)} %add.3.refs_0_), channel_id=1, source_target_pairs={{0,4},{1,3},{2,6},{3,1},{4,0},{5,7},{6,2},{7,5},{8,12},{9,11},{10,... | collective-permute-start | bytes 393224 | tf_op jit(solution)/shard_map/ppermute | solution.py:293
  21.2 3.3 %collective-permute-done.7.refs_1_ = f32[8,16,256]{2,1,0:T(8,128)S(1)} collective-permute-done((f32[8,16,256]{2,1,0:T(8,128)S(1)}, f32[8,16,256]{2,1,0:T(8,128)S(1)}, u32[]{:S(2)}, u32[]{:S(2)}) %collective-permute-start.7) | collective-permute-done | bytes 131104 | tf_op jit(solution)/shard_map/ppermute | solution.py:293
  24.5 1.0 %collective-permute-start.8 = (f32[16,16]{1,0:T(8,128)S(1)}, f32[16,16]{1,0:T(8,128)S(1)}, u32[]{:S(2)}, u32[]{:S(2)}) collective-permute-start(f32[16,16]{1,0:T(8,128)S(1)} %get-tuple-element.17.refs_2_), channel_id=1, source_target_pairs={{0,2},{1,5},{2,0},{3,7},{4,6},{5,13},{6,4},{7,15},{8,10},{9,1},{10... | collective-permute-start | bytes 3080 | tf_op jit(solution)/shard_map/ppermute | solution.py:293
  25.5 1.0 %collective-permute-start.9 = (f32[16,16]{1,0:T(8,128)S(1)}, f32[16,16]{1,0:T(8,128)S(1)}, u32[]{:S(2)}, u32[]{:S(2)}) collective-permute-start(f32[16,16]{1,0:T(8,128)S(1)} %get-tuple-element.17.refs_2_), channel_id=1, source_target_pairs={{0,2},{1,13},{2,0},{3,15},{4,6},{5,9},{6,4},{7,11},{8,10},{9,5},{1... | collective-permute-start | bytes 3080 | tf_op jit(solution)/shard_map/ppermute | solution.py:293
  26.5 1.0 %collective-permute-start.10 = (f32[16,16]{1,0:T(8,128)S(1)}, f32[16,16]{1,0:T(8,128)S(1)}, u32[]{:S(2)}, u32[]{:S(2)}) collective-permute-start(f32[16,16]{1,0:T(8,128)S(1)} %get-tuple-element.17.refs_2_), channel_id=1, source_target_pairs={{0,2},{1,9},{2,0},{3,11},{4,6},{5,1},{6,4},{7,3},{8,10},{9,13},{10... | collective-permute-start | bytes 3080 | tf_op jit(solution)/shard_map/ppermute | solution.py:293
  27.6 0.6 %collective-permute-done.8.refs_3_ = f32[16,16]{1,0:T(8,128)S(1)} collective-permute-done((f32[16,16]{1,0:T(8,128)S(1)}, f32[16,16]{1,0:T(8,128)S(1)}, u32[]{:S(2)}, u32[]{:S(2)}) %collective-permute-start.8) | collective-permute-done | bytes 1056 | tf_op jit(solution)/shard_map/ppermute | solution.py:293
  28.2 1.0 %collective-permute-done.9.refs_4_ = f32[16,16]{1,0:T(8,128)S(1)} collective-permute-done((f32[16,16]{1,0:T(8,128)S(1)}, f32[16,16]{1,0:T(8,128)S(1)}, u32[]{:S(2)}, u32[]{:S(2)}) %collective-permute-start.9) | collective-permute-done | bytes 1056 | tf_op jit(solution)/shard_map/ppermute | solution.py:293
  29.2 1.0 %collective-permute-done.10.refs_5_ = f32[16,16]{1,0:T(8,128)S(1)} collective-permute-done((f32[16,16]{1,0:T(8,128)S(1)}, f32[16,16]{1,0:T(8,128)S(1)}, u32[]{:S(2)}, u32[]{:S(2)}) %collective-permute-start.10) | collective-permute-done | bytes 1056 | tf_op jit(solution)/shard_map/ppermute | solution.py:293
  30.2 0.1 collective-permute-start.11
  30.3 1.1 %collective-permute-done.11.far_ref = f32[16,640]{1,0:T(8,128)S(1)} collective-permute-done((f32[16,640]{1,0:T(8,128)S(1)}, f32[16,640]{1,0:T(8,128)S(1)}, u32[]{:S(2)}, u32[]{:S(2)}) %collective-permute-start.11) | collective-permute-done | bytes 40992 | tf_op jit(solution)/shard_map/ppermute | solution.py:272
  31.4 0.6 %shard_map.55 = (f32[16,512]{1,0:T(8,128)}, f32[16,16]{1,0:T(8,128)}) custom-call(f32[16,512]{1,0:T(8,128)S(1)} %get-tuple-element.18.mine_ref, f32[16,640]{1,0:T(8,128)S(1)} %get-tuple-element.19.other_ref, f32[16,640]{1,0:T(8,128)S(1)} %collective-permute-done.11.far_ref), custom_call_target="tpu_custom_call" | custom-call | tf_op jit(solution)/shard_map/pallas_call | solution.py:258
  (3 shorter events, 0.0 us)
Async XLA Ops:
  0.6 5.7 %collective-permute-start = (f32[16,512]{1,0:T(8,128)}, f32[16,512]{1,0:T(8,128)S(1)}, u32[]{:S(2)}, u32[]{:S(2)}) collective-permute-start(f32[16,512]{1,0:T(8,128)} %refs_0_.1), channel_id=1, source_target_pairs={{0,1},{1,0},{2,3},{3,2},{4,5},{5,4},{6,7},{7,6},{8,9},{9,8},{10,11... | collective-permute-start | bytes 98312 | tf_op jit(solution)/shard_map/ppermute | solution.py:272
  1.1 5.2 %collective-permute-start.1 = (f32[16,512]{1,0:T(8,128)}, f32[16,512]{1,0:T(8,128)S(1)}, u32[]{:S(2)}, u32[]{:S(2)}) collective-permute-start(f32[16,512]{1,0:T(8,128)} %refs_0_.1), channel_id=1, source_target_pairs={{0,2},{1,3},{2,0},{3,1},{4,6},{5,7},{6,4},{7,5},{8,10},{9,11},{10,... | collective-permute-start | bytes 98312 | tf_op jit(solution)/shard_map/ppermute | solution.py:272
  3.7 3.6 %collective-permute-start.2 = (f32[16,512]{1,0:T(8,128)}, f32[16,512]{1,0:T(8,128)S(1)}, u32[]{:S(2)}, u32[]{:S(2)}) collective-permute-start(f32[16,512]{1,0:T(8,128)} %refs_0_.1), channel_id=1, source_target_pairs={{0,3},{1,2},{2,1},{3,0},{4,7},{5,6},{6,5},{7,4},{8,11},{9,10},{10,... | collective-permute-start | bytes 98312 | tf_op jit(solution)/shard_map/ppermute | solution.py:272
  3.8 3.5 %copy-start = (f32[16,512]{1,0:T(8,128)S(1)}, f32[16,512]{1,0:T(8,128)}, u32[]{:S(2)}) copy-start(f32[16,512]{1,0:T(8,128)} %refs_0_.1) | copy-start | bytes 98308
  8.3 6.2 %collective-permute-start.3 = (f32[4,16,256]{2,1,0:T(8,128)S(1)}, f32[4,16,256]{2,1,0:T(8,128)S(1)}, u32[]{:S(2)}, u32[]{:S(2)}) collective-permute-start(f32[4,16,256]{2,1,0:T(8,128)S(1)} %shard_map.51.refs_3_), channel_id=1, source_target_pairs={{0,12},{1,9},{2,14},{3,11},{4,8},{5,13},{6,10},{7,15},{8,4},{9,1},... | collective-permute-start | bytes 196616 | tf_op jit(solution)/shard_map/ppermute | solution.py:293
  11.9 5.5 %collective-permute-start.4 = (f32[4,16,256]{2,1,0:T(8,128)S(1)}, f32[4,16,256]{2,1,0:T(8,128)S(1)}, u32[]{:S(2)}, u32[]{:S(2)}) collective-permute-start(f32[4,16,256]{2,1,0:T(8,128)S(1)} %shard_map.51.refs_3_), channel_id=1, source_target_pairs={{0,4},{1,13},{2,6},{3,15},{4,0},{5,9},{6,2},{7,11},{8,12},{9,5},{1... | collective-permute-start | bytes 196616 | tf_op jit(solution)/shard_map/ppermute | solution.py:293
  11.9 5.5 %collective-permute-start.5 = (f32[4,16,256]{2,1,0:T(8,128)S(1)}, f32[4,16,256]{2,1,0:T(8,128)S(1)}, u32[]{:S(2)}, u32[]{:S(2)}) collective-permute-start(f32[4,16,256]{2,1,0:T(8,128)S(1)} %shard_map.51.refs_3_), channel_id=1, source_target_pairs={{0,8},{1,5},{2,10},{3,7},{4,12},{5,1},{6,14},{7,3},{8,0},{9,13},{1... | collective-permute-start | bytes 196616 | tf_op jit(solution)/shard_map/ppermute | solution.py:293
  18.1 1.4 %collective-permute-start.6 = (f32[8,16,256]{2,1,0:T(8,128)S(1)}, f32[8,16,256]{2,1,0:T(8,128)S(1)}, u32[]{:S(2)}, u32[]{:S(2)}) collective-permute-start(f32[8,16,256]{2,1,0:T(8,128)S(1)} %shard_map.52), channel_id=1, source_target_pairs={{0,1},{1,0},{2,3},{3,2},{4,5},{5,4},{6,7},{7,6},{8,9},{9,8},{10,11... | collective-permute-start | bytes 393224 | tf_op jit(solution)/shard_map/ppermute | solution.py:272
  19.5 5.0 %collective-permute-start.7 = (f32[8,16,256]{2,1,0:T(8,128)S(1)}, f32[8,16,256]{2,1,0:T(8,128)S(1)}, u32[]{:S(2)}, u32[]{:S(2)}) collective-permute-start(f32[8,16,256]{2,1,0:T(8,128)S(1)} %add.3.refs_0_), channel_id=1, source_target_pairs={{0,4},{1,3},{2,6},{3,1},{4,0},{5,7},{6,2},{7,5},{8,12},{9,11},{10,... | collective-permute-start | bytes 393224 | tf_op jit(solution)/shard_map/ppermute | solution.py:293
  24.5 3.7 %collective-permute-start.8 = (f32[16,16]{1,0:T(8,128)S(1)}, f32[16,16]{1,0:T(8,128)S(1)}, u32[]{:S(2)}, u32[]{:S(2)}) collective-permute-start(f32[16,16]{1,0:T(8,128)S(1)} %get-tuple-element.17.refs_2_), channel_id=1, source_target_pairs={{0,2},{1,5},{2,0},{3,7},{4,6},{5,13},{6,4},{7,15},{8,10},{9,1},{10... | collective-permute-start | bytes 3080 | tf_op jit(solution)/shard_map/ppermute | solution.py:293
  25.5 3.7 %collective-permute-start.9 = (f32[16,16]{1,0:T(8,128)S(1)}, f32[16,16]{1,0:T(8,128)S(1)}, u32[]{:S(2)}, u32[]{:S(2)}) collective-permute-start(f32[16,16]{1,0:T(8,128)S(1)} %get-tuple-element.17.refs_2_), channel_id=1, source_target_pairs={{0,2},{1,13},{2,0},{3,15},{4,6},{5,9},{6,4},{7,11},{8,10},{9,5},{1... | collective-permute-start | bytes 3080 | tf_op jit(solution)/shard_map/ppermute | solution.py:293
  26.5 3.7 %collective-permute-start.10 = (f32[16,16]{1,0:T(8,128)S(1)}, f32[16,16]{1,0:T(8,128)S(1)}, u32[]{:S(2)}, u32[]{:S(2)}) collective-permute-start(f32[16,16]{1,0:T(8,128)S(1)} %get-tuple-element.17.refs_2_), channel_id=1, source_target_pairs={{0,2},{1,9},{2,0},{3,11},{4,6},{5,1},{6,4},{7,3},{8,10},{9,13},{10... | collective-permute-start | bytes 3080 | tf_op jit(solution)/shard_map/ppermute | solution.py:293
  30.2 1.2 %collective-permute-start.11 = (f32[16,640]{1,0:T(8,128)S(1)}, f32[16,640]{1,0:T(8,128)S(1)}, u32[]{:S(2)}, u32[]{:S(2)}) collective-permute-start(f32[16,640]{1,0:T(8,128)S(1)} %get-tuple-element.19.other_ref), channel_id=1, source_target_pairs={{0,1},{1,0},{2,3},{3,2},{4,5},{5,4},{6,7},{7,6},{8,9},{9,8},{10,11... | collective-permute-start | bytes 122888 | tf_op jit(solution)/shard_map/ppermute | solution.py:272

commit v6 on v5

--- a/solution.py
+++ b/solution.py
@@ -89,28 +89,28 @@
     return first[:count] + first[count:] + second
 
 
-def rows_kernel(slot_ref, high_ref, low_ref, *refs):
+def rows_kernel(steps, slot_ref, high_ref, low_ref, *refs):
     pieces, out_ref, pair_ref = refs[:-2], refs[-2], refs[-1]
     nblk, edge = high_ref.shape[0], high_ref.shape[1]
     per_piece = pieces[0].shape[1] // edge
     column_count = per_piece * len(pieces)
     me = lax.axis_index(GROUP)
-    for k, piece in enumerate(pieces):
+    for k, piece in zip(steps, pieces):
         for h in range(per_piece):
             store_halves(pair_ref, (me ^ k) * per_piece + h, piece[:, h * edge:(h + 1) * edge])
     out_ref[...] = jnp.zeros_like(out_ref)
     for b in range(nblk):
         slot = slot_ref[b]
-        r, c = slot // column_count, slot % column_count
+        r, c = lax.div(slot, column_count), lax.rem(slot, column_count)
         out_ref[r] += product(pair_ref[c], high_ref[b], low_ref[b], NN, NT)
 
 
-def rows_product(slot, high, low, pieces):
+def rows_product(slot, high, low, pieces, steps):
     count = pieces[0].shape[0]
     nblk, edge = high.shape[0], high.shape[1]
     column_count = len(pieces) * pieces[0].shape[1] // edge
     return pl.pallas_call(
-        rows_kernel,
+        lambda *refs: rows_kernel(steps, *refs),
         out_shape=jax.ShapeDtypeStruct((RBL, count, edge), jnp.float32),
         in_specs=[smem()] + [vmem()] * (2 + len(pieces)),
         out_specs=vmem(),
@@ -130,7 +130,7 @@
     out_ref[...] = jnp.zeros_like(out_ref)
     for b in range(nblk):
         slot = slot_ref[b]
-        r, c = slot // column_count, slot % column_count
+        r, c = lax.div(slot, column_count), lax.rem(slot, column_count)
         out_ref[c] += product(pair_ref[r], high_ref[b], low_ref[b], NN, NN)
 
 
@@ -276,9 +276,8 @@
     return n & (n - 1) == 0
 
 
-def gather(x, axes):
-    n = lax.axis_size(axes)
-    return [x] + [partner(x, axes, k) for k in range(1, n)]
+def gather(x, axes, steps):
+    return [x] + [partner(x, axes, k) for k in steps]
 
 
 def exchange(x, steps):
@@ -326,7 +325,8 @@
     *split, slot = split_blocks(blocks.reshape(nblk, edge, edge), slot)
     high, low, high_t = [pltpu.with_memory_space_constraint(x, pltpu.VMEM) for x in split]
     slot = pltpu.with_memory_space_constraint(slot, pltpu.SMEM)
-    ypart = rows_product(slot, high_t, low, gather(basis_in, GROUP))
+    steps = (3, 2, 1) if lax.axis_size(GROUP) == 4 else tuple(range(1, lax.axis_size(GROUP)))
+    ypart = rows_product(slot, high_t, low, gather(basis_in, GROUP, steps), (0,) + steps)
     scale = math.sqrt(share * lax.axis_size(("col",) + GROUP))
     sizes = tuple(lax.axis_size(a) for a in ("col", "row", "sub"))
     finish = four_by_two if sizes == (4, 2, 2) else general

time: 32.2 us -> 32 us (level)
  waiting for transfers between devices: 13.9 us -> 13.5 us
    ppermute x7, waiting for transfers between devices: 10.6 us -> 10.2 us  [exchange(): return lax.ppermute(x, ('col', 'row', 'sub'), pairs)]
where the time goes in v6:
time: 32 us; the launch traced here: 31.9 us
  waiting for transfers between devices  13.5 us (42%)
  starting transfers between devices  12.8 us (40%)
  Pallas kernels  4.92 us (15%)
  between operations  0.67 us (2%)
    ppermute x7, waiting for transfers between devices, exchange(): return lax.ppermute(x, ('col', 'row', 'sub'), pairs)  10.2 us
    ppermute x7, starting transfers between devices, exchange(): return lax.ppermute(x, ('col', 'row', 'sub'), pairs)  9.44 us
    ppermute x5, starting transfers between devices, partner(): return lax.ppermute(x, axes, [(i, i ^ k) for i in range(n)])  3.32 us
    ppermute x5, waiting for transfers between devices, partner(): return lax.ppermute(x, axes, [(i, i ^ k) for i in range(n)])  3.29 us
    pallas_call x1, Pallas kernels, split_blocks(): pl.pallas_call(split_kernel, out_shape=(pltpu.VMEM(blocks.shape, jnp.bflo...  2.56 us
    pallas_call x1, Pallas kernels, rows_product(): pl.pallas_call(lambda *refs: rows_kernel(steps, *refs), out_shape=jax.Sha...  1 us
    pallas_call x1, Pallas kernels, cols_product(): pl.pallas_call(lambda *refs: cols_kernel(column_count, *refs), out_shape=...  0.73 us
  transfers between devices with their start and end apart: 12, of which 9 were waited for; matrix products, arithmetic and copies ran while one was open for 0% of the time, Pallas kernels for 8%

profile of v6, /device:TPU:0, one launch (start us, length us, event | category | flops | bytes accessed | tf_op | source)
XLA Modules:
  0.0 31.9 jit_solution(4525210793031568378)
XLA Ops:
  0.6 2.4 %collective-permute-start = (f32[16,512]{1,0:T(8,128)}, f32[16,512]{1,0:T(8,128)S(1)}, u32[]{:S(2)}, u32[]{:S(2)}) collective-permute-start(f32[16,512]{1,0:T(8,128)} %refs_3_.1), channel_id=1, source_target_pairs={{0,3},{1,2},{2,1},{3,0},{4,7},{5,6},{6,5},{7,4},{8,11},{9,10},{10,... | collective-permute-start | bytes 98312 | tf_op jit(solution)/shard_map/ppermute | solution.py:272
  3.1 0.6 %collective-permute-start.1 = (f32[16,512]{1,0:T(8,128)}, f32[16,512]{1,0:T(8,128)S(1)}, u32[]{:S(2)}, u32[]{:S(2)}) collective-permute-start(f32[16,512]{1,0:T(8,128)} %refs_3_.1), channel_id=1, source_target_pairs={{0,2},{1,3},{2,0},{3,1},{4,6},{5,7},{6,4},{7,5},{8,10},{9,11},{10,... | collective-permute-start | bytes 98312 | tf_op jit(solution)/shard_map/ppermute | solution.py:272
  3.7 0.0 collective-permute-start.2
  3.8 0.0 copy-start
  3.8 2.6 %shard_map.50 = (bf16[16,256,256]{2,1,0:T(8,128)(2,1)S(1)}, bf16[16,256,256]{2,1,0:T(8,128)(2,1)S(1)}, bf16[16,256,256]{2,1,0:T(8,128)(2,1)S(1)}, s32[16]{0:T(128)S(4)}) custom-call(f32[16,256,256]{2,1,0:T(8,128)} %bitcast.2, s32[16]{0:T(128)} %bitcast.3), custom_call_target="tpu_custom_call" | custom-call | flops 3145728 | bytes 8388608 | tf_op jit(solution)/shard_map/pallas_call | solution.py:58
  6.3 0.0 collective-permute-done.refs_4_
  6.3 0.9 %collective-permute-done.1.refs_5_ = f32[16,512]{1,0:T(8,128)S(1)} collective-permute-done((f32[16,512]{1,0:T(8,128)}, f32[16,512]{1,0:T(8,128)S(1)}, u32[]{:S(2)}, u32[]{:S(2)}) %collective-permute-start.1) | collective-permute-done | bytes 32800 | tf_op jit(solution)/shard_map/ppermute | solution.py:272
  7.3 0.0 collective-permute-done.2.refs_6_
  7.3 0.0 copy-done
  7.3 1.0 %shard_map.51.refs_3_ = f32[4,16,256]{2,1,0:T(8,128)S(1)} custom-call(s32[16]{0:T(128)S(4)} %get-tuple-element.11.refs_0_, bf16[16,256,256]{2,1,0:T(8,128)(2,1)S(1)} %get-tuple-element.14.refs_1_, bf16[16,256,256]{2,1,0:T(8,128)(2,1)S(1)} %get-tuple-element.13.refs_2_, f32[16,512]{1,0:T(8,128)S(1)} %copy-done, f32[16,512]{1,0:T(8,128)S(1)} %collective-permute-done.refs_4_, ...), custom_call_target="tpu_custom_call" | custom-call | tf_op jit(solution)/shard_map/pallas_call | solution.py:112
  8.3 3.6 %collective-permute-start.3 = (f32[4,16,256]{2,1,0:T(8,128)S(1)}, f32[4,16,256]{2,1,0:T(8,128)S(1)}, u32[]{:S(2)}, u32[]{:S(2)}) collective-permute-start(f32[4,16,256]{2,1,0:T(8,128)S(1)} %shard_map.51.refs_3_), channel_id=1, source_target_pairs={{0,12},{1,9},{2,14},{3,11},{4,8},{5,13},{6,10},{7,15},{8,4},{9,1},... | collective-permute-start | bytes 196616 | tf_op jit(solution)/shard_map/ppermute | solution.py:292
  11.9 0.0 collective-permute-start.4
  11.9 0.8 %collective-permute-start.5 = (f32[4,16,256]{2,1,0:T(8,128)S(1)}, f32[4,16,256]{2,1,0:T(8,128)S(1)}, u32[]{:S(2)}, u32[]{:S(2)}) collective-permute-start(f32[4,16,256]{2,1,0:T(8,128)S(1)} %shard_map.51.refs_3_), channel_id=1, source_target_pairs={{0,8},{1,5},{2,10},{3,7},{4,12},{5,1},{6,14},{7,3},{8,0},{9,13},{1... | collective-permute-start | bytes 196616 | tf_op jit(solution)/shard_map/ppermute | solution.py:292
  12.7 1.8 %collective-permute-done.3.refs_4_ = f32[4,16,256]{2,1,0:T(8,128)S(1)} collective-permute-done((f32[4,16,256]{2,1,0:T(8,128)S(1)}, f32[4,16,256]{2,1,0:T(8,128)S(1)}, u32[]{:S(2)}, u32[]{:S(2)}) %collective-permute-start.3) | collective-permute-done | bytes 65568 | tf_op jit(solution)/shard_map/ppermute | solution.py:292
  14.5 2.7 %collective-permute-done.4.refs_5_ = f32[4,16,256]{2,1,0:T(8,128)S(1)} collective-permute-done((f32[4,16,256]{2,1,0:T(8,128)S(1)}, f32[4,16,256]{2,1,0:T(8,128)S(1)}, u32[]{:S(2)}, u32[]{:S(2)}) %collective-permute-start.4) | collective-permute-done | bytes 65568 | tf_op jit(solution)/shard_map/ppermute | solution.py:292
  17.2 0.0 collective-permute-done.5.refs_6_
  17.2 0.7 %shard_map.52 = f32[8,16,256]{2,1,0:T(8,128)S(1)} custom-call(s32[16]{0:T(128)S(4)} %get-tuple-element.11.refs_0_, bf16[16,256,256]{2,1,0:T(8,128)(2,1)S(1)} %get-tuple-element.12.refs_1_, bf16[16,256,256]{2,1,0:T(8,128)(2,1)S(1)} %get-tuple-element.13.refs_2_, f32[4,16,256]{2,1,0:T(8,128)S(1)} %shard_map.51.refs_3_, ...), custom_call_target="tpu_custom_call" | custom-call | tf_op jit(solution)/shard_map/pallas_call | solution.py:139
  17.9 0.0 collective-permute-start.6
  17.9 1.3 %collective-permute-done.6 = f32[8,16,256]{2,1,0:T(8,128)S(1)} collective-permute-done((f32[8,16,256]{2,1,0:T(8,128)S(1)}, f32[8,16,256]{2,1,0:T(8,128)S(1)}, u32[]{:S(2)}, u32[]{:S(2)}) %collective-permute-start.6) | collective-permute-done | bytes 131104 | tf_op jit(solution)/shard_map/ppermute | solution.py:272
  19.3 1.9 %collective-permute-start.7 = (f32[8,16,256]{2,1,0:T(8,128)S(1)}, f32[8,16,256]{2,1,0:T(8,128)S(1)}, u32[]{:S(2)}, u32[]{:S(2)}) collective-permute-start(f32[8,16,256]{2,1,0:T(8,128)S(1)} %add.3.refs_0_), channel_id=1, source_target_pairs={{0,4},{1,3},{2,6},{3,1},{4,0},{5,7},{6,2},{7,5},{8,12},{9,11},{10,... | collective-permute-start | bytes 393224 | tf_op jit(solution)/shard_map/ppermute | solution.py:292
  21.2 3.1 %collective-permute-done.7.refs_1_ = f32[8,16,256]{2,1,0:T(8,128)S(1)} collective-permute-done((f32[8,16,256]{2,1,0:T(8,128)S(1)}, f32[8,16,256]{2,1,0:T(8,128)S(1)}, u32[]{:S(2)}, u32[]{:S(2)}) %collective-permute-start.7) | collective-permute-done | bytes 131104 | tf_op jit(solution)/shard_map/ppermute | solution.py:292
  24.3 1.1 %collective-permute-start.8 = (f32[16,16]{1,0:T(8,128)S(1)}, f32[16,16]{1,0:T(8,128)S(1)}, u32[]{:S(2)}, u32[]{:S(2)}) collective-permute-start(f32[16,16]{1,0:T(8,128)S(1)} %get-tuple-element.17.refs_2_), channel_id=1, source_target_pairs={{0,2},{1,5},{2,0},{3,7},{4,6},{5,13},{6,4},{7,15},{8,10},{9,1},{10... | collective-permute-start | bytes 3080 | tf_op jit(solution)/shard_map/ppermute | solution.py:292
  25.4 0.9 %collective-permute-start.9 = (f32[16,16]{1,0:T(8,128)S(1)}, f32[16,16]{1,0:T(8,128)S(1)}, u32[]{:S(2)}, u32[]{:S(2)}) collective-permute-start(f32[16,16]{1,0:T(8,128)S(1)} %get-tuple-element.17.refs_2_), channel_id=1, source_target_pairs={{0,2},{1,13},{2,0},{3,15},{4,6},{5,9},{6,4},{7,11},{8,10},{9,5},{1... | collective-permute-start | bytes 3080 | tf_op jit(solution)/shard_map/ppermute | solution.py:292
  26.4 1.1 %collective-permute-start.10 = (f32[16,16]{1,0:T(8,128)S(1)}, f32[16,16]{1,0:T(8,128)S(1)}, u32[]{:S(2)}, u32[]{:S(2)}) collective-permute-start(f32[16,16]{1,0:T(8,128)S(1)} %get-tuple-element.17.refs_2_), channel_id=1, source_target_pairs={{0,2},{1,9},{2,0},{3,11},{4,6},{5,1},{6,4},{7,3},{8,10},{9,13},{10... | collective-permute-start | bytes 3080 | tf_op jit(solution)/shard_map/ppermute | solution.py:292
  27.4 0.5 %collective-permute-done.8.refs_3_ = f32[16,16]{1,0:T(8,128)S(1)} collective-permute-done((f32[16,16]{1,0:T(8,128)S(1)}, f32[16,16]{1,0:T(8,128)S(1)}, u32[]{:S(2)}, u32[]{:S(2)}) %collective-permute-start.8) | collective-permute-done | bytes 1056 | tf_op jit(solution)/shard_map/ppermute | solution.py:292
  28.0 1.1 %collective-permute-done.9.refs_4_ = f32[16,16]{1,0:T(8,128)S(1)} collective-permute-done((f32[16,16]{1,0:T(8,128)S(1)}, f32[16,16]{1,0:T(8,128)S(1)}, u32[]{:S(2)}, u32[]{:S(2)}) %collective-permute-start.9) | collective-permute-done | bytes 1056 | tf_op jit(solution)/shard_map/ppermute | solution.py:292
  29.1 0.9 %collective-permute-done.10.refs_5_ = f32[16,16]{1,0:T(8,128)S(1)} collective-permute-done((f32[16,16]{1,0:T(8,128)S(1)}, f32[16,16]{1,0:T(8,128)S(1)}, u32[]{:S(2)}, u32[]{:S(2)}) %collective-permute-start.10) | collective-permute-done | bytes 1056 | tf_op jit(solution)/shard_map/ppermute | solution.py:292
  30.0 0.2 collective-permute-start.11
  30.2 1.0 %collective-permute-done.11.far_ref = f32[16,640]{1,0:T(8,128)S(1)} collective-permute-done((f32[16,640]{1,0:T(8,128)S(1)}, f32[16,640]{1,0:T(8,128)S(1)}, u32[]{:S(2)}, u32[]{:S(2)}) %collective-permute-start.11) | collective-permute-done | bytes 40992 | tf_op jit(solution)/shard_map/ppermute | solution.py:272
  31.2 0.6 %shard_map.55 = (f32[16,512]{1,0:T(8,128)}, f32[16,16]{1,0:T(8,128)}) custom-call(f32[16,512]{1,0:T(8,128)S(1)} %get-tuple-element.18.mine_ref, f32[16,640]{1,0:T(8,128)S(1)} %get-tuple-element.19.other_ref, f32[16,640]{1,0:T(8,128)S(1)} %collective-permute-done.11.far_ref), custom_call_target="tpu_custom_call" | custom-call | tf_op jit(solution)/shard_map/pallas_call | solution.py:258
  (3 shorter events, 0.0 us)
Async XLA Ops:
  0.6 5.7 %collective-permute-start = (f32[16,512]{1,0:T(8,128)}, f32[16,512]{1,0:T(8,128)S(1)}, u32[]{:S(2)}, u32[]{:S(2)}) collective-permute-start(f32[16,512]{1,0:T(8,128)} %refs_3_.1), channel_id=1, source_target_pairs={{0,3},{1,2},{2,1},{3,0},{4,7},{5,6},{6,5},{7,4},{8,11},{9,10},{10,... | collective-permute-start | bytes 98312 | tf_op jit(solution)/shard_map/ppermute | solution.py:272
  3.1 4.2 %collective-permute-start.1 = (f32[16,512]{1,0:T(8,128)}, f32[16,512]{1,0:T(8,128)S(1)}, u32[]{:S(2)}, u32[]{:S(2)}) collective-permute-start(f32[16,512]{1,0:T(8,128)} %refs_3_.1), channel_id=1, source_target_pairs={{0,2},{1,3},{2,0},{3,1},{4,6},{5,7},{6,4},{7,5},{8,10},{9,11},{10,... | collective-permute-start | bytes 98312 | tf_op jit(solution)/shard_map/ppermute | solution.py:272
  3.7 3.5 %collective-permute-start.2 = (f32[16,512]{1,0:T(8,128)}, f32[16,512]{1,0:T(8,128)S(1)}, u32[]{:S(2)}, u32[]{:S(2)}) collective-permute-start(f32[16,512]{1,0:T(8,128)} %refs_3_.1), channel_id=1, source_target_pairs={{0,1},{1,0},{2,3},{3,2},{4,5},{5,4},{6,7},{7,6},{8,9},{9,8},{10,11... | collective-permute-start | bytes 98312 | tf_op jit(solution)/shard_map/ppermute | solution.py:272
  3.8 3.5 %copy-start = (f32[16,512]{1,0:T(8,128)S(1)}, f32[16,512]{1,0:T(8,128)}, u32[]{:S(2)}) copy-start(f32[16,512]{1,0:T(8,128)} %refs_3_.1) | copy-start | bytes 98308
  8.3 6.2 %collective-permute-start.3 = (f32[4,16,256]{2,1,0:T(8,128)S(1)}, f32[4,16,256]{2,1,0:T(8,128)S(1)}, u32[]{:S(2)}, u32[]{:S(2)}) collective-permute-start(f32[4,16,256]{2,1,0:T(8,128)S(1)} %shard_map.51.refs_3_), channel_id=1, source_target_pairs={{0,12},{1,9},{2,14},{3,11},{4,8},{5,13},{6,10},{7,15},{8,4},{9,1},... | collective-permute-start | bytes 196616 | tf_op jit(solution)/shard_map/ppermute | solution.py:292
  11.9 5.3 %collective-permute-start.4 = (f32[4,16,256]{2,1,0:T(8,128)S(1)}, f32[4,16,256]{2,1,0:T(8,128)S(1)}, u32[]{:S(2)}, u32[]{:S(2)}) collective-permute-start(f32[4,16,256]{2,1,0:T(8,128)S(1)} %shard_map.51.refs_3_), channel_id=1, source_target_pairs={{0,4},{1,13},{2,6},{3,15},{4,0},{5,9},{6,2},{7,11},{8,12},{9,5},{1... | collective-permute-start | bytes 196616 | tf_op jit(solution)/shard_map/ppermute | solution.py:292
  11.9 5.3 %collective-permute-start.5 = (f32[4,16,256]{2,1,0:T(8,128)S(1)}, f32[4,16,256]{2,1,0:T(8,128)S(1)}, u32[]{:S(2)}, u32[]{:S(2)}) collective-permute-start(f32[4,16,256]{2,1,0:T(8,128)S(1)} %shard_map.51.refs_3_), channel_id=1, source_target_pairs={{0,8},{1,5},{2,10},{3,7},{4,12},{5,1},{6,14},{7,3},{8,0},{9,13},{1... | collective-permute-start | bytes 196616 | tf_op jit(solution)/shard_map/ppermute | solution.py:292
  17.9 1.4 %collective-permute-start.6 = (f32[8,16,256]{2,1,0:T(8,128)S(1)}, f32[8,16,256]{2,1,0:T(8,128)S(1)}, u32[]{:S(2)}, u32[]{:S(2)}) collective-permute-start(f32[8,16,256]{2,1,0:T(8,128)S(1)} %shard_map.52), channel_id=1, source_target_pairs={{0,1},{1,0},{2,3},{3,2},{4,5},{5,4},{6,7},{7,6},{8,9},{9,8},{10,11... | collective-permute-start | bytes 393224 | tf_op jit(solution)/shard_map/ppermute | solution.py:272
  19.3 5.0 %collective-permute-start.7 = (f32[8,16,256]{2,1,0:T(8,128)S(1)}, f32[8,16,256]{2,1,0:T(8,128)S(1)}, u32[]{:S(2)}, u32[]{:S(2)}) collective-permute-start(f32[8,16,256]{2,1,0:T(8,128)S(1)} %add.3.refs_0_), channel_id=1, source_target_pairs={{0,4},{1,3},{2,6},{3,1},{4,0},{5,7},{6,2},{7,5},{8,12},{9,11},{10,... | collective-permute-start | bytes 393224 | tf_op jit(solution)/shard_map/ppermute | solution.py:292
  24.3 3.7 %collective-permute-start.8 = (f32[16,16]{1,0:T(8,128)S(1)}, f32[16,16]{1,0:T(8,128)S(1)}, u32[]{:S(2)}, u32[]{:S(2)}) collective-permute-start(f32[16,16]{1,0:T(8,128)S(1)} %get-tuple-element.17.refs_2_), channel_id=1, source_target_pairs={{0,2},{1,5},{2,0},{3,7},{4,6},{5,13},{6,4},{7,15},{8,10},{9,1},{10... | collective-permute-start | bytes 3080 | tf_op jit(solution)/shard_map/ppermute | solution.py:292
  25.4 3.7 %collective-permute-start.9 = (f32[16,16]{1,0:T(8,128)S(1)}, f32[16,16]{1,0:T(8,128)S(1)}, u32[]{:S(2)}, u32[]{:S(2)}) collective-permute-start(f32[16,16]{1,0:T(8,128)S(1)} %get-tuple-element.17.refs_2_), channel_id=1, source_target_pairs={{0,2},{1,13},{2,0},{3,15},{4,6},{5,9},{6,4},{7,11},{8,10},{9,5},{1... | collective-permute-start | bytes 3080 | tf_op jit(solution)/shard_map/ppermute | solution.py:292
  26.4 3.7 %collective-permute-start.10 = (f32[16,16]{1,0:T(8,128)S(1)}, f32[16,16]{1,0:T(8,128)S(1)}, u32[]{:S(2)}, u32[]{:S(2)}) collective-permute-start(f32[16,16]{1,0:T(8,128)S(1)} %get-tuple-element.17.refs_2_), channel_id=1, source_target_pairs={{0,2},{1,9},{2,0},{3,11},{4,6},{5,1},{6,4},{7,3},{8,10},{9,13},{10... | collective-permute-start | bytes 3080 | tf_op jit(solution)/shard_map/ppermute | solution.py:292
  30.0 1.2 %collective-permute-start.11 = (f32[16,640]{1,0:T(8,128)S(1)}, f32[16,640]{1,0:T(8,128)S(1)}, u32[]{:S(2)}, u32[]{:S(2)}) collective-permute-start(f32[16,640]{1,0:T(8,128)S(1)} %get-tuple-element.19.other_ref), channel_id=1, source_target_pairs={{0,1},{1,0},{2,3},{3,2},{4,5},{5,4},{6,7},{7,6},{8,9},{9,8},{10,11... | collective-permute-start | bytes 122888 | tf_op jit(solution)/shard_map/ppermute | solution.py:272

commit v7 on v6

--- a/solution.py
+++ b/solution.py
@@ -9,6 +9,7 @@
 
 RBL = 4
 LANES = 128
+LOW_T = 5
 GROUP = ("row", "sub")
 LEAD = 1
 COLS = ((0, 1, 2, 3), (1, 0, 3, 2), (2, 3, 0, 1), (3, 2, 1, 0), (1, 3, 0, 2), (2, 0, 3, 1))
@@ -38,7 +39,7 @@
     return high, low
 
 
-def split_kernel(blocks_ref, slot_ref, high_ref, low_ref, high_t_ref, place_ref, held_ref, sems, slot_sem):
+def split_kernel(blocks_ref, slot_ref, high_ref, low_ref, high_t_ref, low_t_ref, place_ref, held_ref, sems, slot_sem):
     count = blocks_ref.shape[0]
     place = pltpu.make_async_copy(slot_ref, place_ref, slot_sem)
     place.start()
@@ -50,6 +51,8 @@
         high, low = halves(held_ref[i])
         high_ref[i], low_ref[i] = high, low
         high_t_ref[i] = high.T
+        if i < LOW_T:
+            low_t_ref[i] = low.T
     place.wait()
 
 
@@ -61,10 +64,11 @@
             pltpu.VMEM(blocks.shape, jnp.bfloat16),
             pltpu.VMEM(blocks.shape, jnp.bfloat16),
             pltpu.VMEM(blocks.shape, jnp.bfloat16),
+            pltpu.VMEM((LOW_T, cols, rows), jnp.bfloat16),
             pltpu.SMEM(slot.shape, jnp.int32),
         ),
         in_specs=[pl.BlockSpec(memory_space=pltpu.HBM)] * 2,
-        out_specs=(vmem(), vmem(), vmem(), smem()),
+        out_specs=(vmem(), vmem(), vmem(), vmem(), smem()),
         scratch_shapes=[
             pltpu.VMEM(blocks.shape, jnp.float32),
             pltpu.SemaphoreType.DMA((n,)),
@@ -89,7 +93,7 @@
     return first[:count] + first[count:] + second
 
 
-def rows_kernel(steps, slot_ref, high_ref, low_ref, *refs):
+def rows_kernel(steps, slot_ref, high_ref, low_ref, low_t_ref, *refs):
     pieces, out_ref, pair_ref = refs[:-2], refs[-2], refs[-1]
     nblk, edge = high_ref.shape[0], high_ref.shape[1]
     per_piece = pieces[0].shape[1] // edge
@@ -102,21 +106,21 @@
     for b in range(nblk):
         slot = slot_ref[b]
         r, c = lax.div(slot, column_count), lax.rem(slot, column_count)
-        out_ref[r] += product(pair_ref[c], high_ref[b], low_ref[b], NN, NT)
-
-
-def rows_product(slot, high, low, pieces, steps):
+        out_ref[r] += product(pair_ref[c], high_ref[b], *((low_t_ref[b], NN, NN) if b < LOW_T else (low_ref[b], NN, NT)))
+
+
+def rows_product(slot, high, low, low_t, pieces, steps):
     count = pieces[0].shape[0]
     nblk, edge = high.shape[0], high.shape[1]
     column_count = len(pieces) * pieces[0].shape[1] // edge
     return pl.pallas_call(
         lambda *refs: rows_kernel(steps, *refs),
         out_shape=jax.ShapeDtypeStruct((RBL, count, edge), jnp.float32),
-        in_specs=[smem()] + [vmem()] * (2 + len(pieces)),
+        in_specs=[smem()] + [vmem()] * (3 + len(pieces)),
         out_specs=vmem(),
         scratch_shapes=[pltpu.VMEM((column_count, 2 * count, edge), jnp.bfloat16)],
         compiler_params=params(),
-    )(slot, high, low, *pieces)
+    )(slot, high, low, low_t, *pieces)
 
 
 def cols_kernel(column_count, slot_ref, high_ref, low_ref, *refs):
@@ -323,10 +327,10 @@
     column_count = share * lax.axis_size(GROUP) // edge
     slot = block_slot.reshape(nblk)
     *split, slot = split_blocks(blocks.reshape(nblk, edge, edge), slot)
-    high, low, high_t = [pltpu.with_memory_space_constraint(x, pltpu.VMEM) for x in split]
+    high, low, high_t, low_t = [pltpu.with_memory_space_constraint(x, pltpu.VMEM) for x in split]
     slot = pltpu.with_memory_space_constraint(slot, pltpu.SMEM)
     steps = (3, 2, 1) if lax.axis_size(GROUP) == 4 else tuple(range(1, lax.axis_size(GROUP)))
-    ypart = rows_product(slot, high_t, low, gather(basis_in, GROUP, steps), (0,) + steps)
+    ypart = rows_product(slot, high_t, low, low_t, gather(basis_in, GROUP, steps), (0,) + steps)
     scale = math.sqrt(share * lax.axis_size(("col",) + GROUP))
     sizes = tuple(lax.axis_size(a) for a in ("col", "row", "sub"))
     finish = four_by_two if sizes == (4, 2, 2) else general

time: 32 us -> 31.9 us (level)
  transfers between devices with their start and end apart: 12 -> 12, of which waited for: 9 -> 9; matrix products, arithmetic and copies ran while one was open for 0% -> 0% of each run, Pallas kernels for 8% -> 9%
where the time goes in v7:
time: 31.9 us; the launch traced here: 31.8 us
  waiting for transfers between devices  13.2 us (41%)
  starting transfers between devices  12.8 us (40%)
  Pallas kernels  5 us (16%)
  between operations  0.67 us (2%)
    ppermute x7, waiting for transfers between devices, exchange(): return lax.ppermute(x, ('col', 'row', 'sub'), pairs)  10.1 us
    ppermute x7, starting transfers between devices, exchange(): return lax.ppermute(x, ('col', 'row', 'sub'), pairs)  9.51 us
    ppermute x5, starting transfers between devices, partner(): return lax.ppermute(x, axes, [(i, i ^ k) for i in range(n)])  3.32 us
    ppermute x5, waiting for transfers between devices, partner(): return lax.ppermute(x, axes, [(i, i ^ k) for i in range(n)])  3.11 us
    pallas_call x1, Pallas kernels, split_blocks(): pl.pallas_call(split_kernel, out_shape=(pltpu.VMEM(blocks.shape, jnp.bflo...  2.75 us
    pallas_call x1, Pallas kernels, rows_product(): pl.pallas_call(lambda *refs: rows_kernel(steps, *refs), out_shape=jax.Sha...  0.89 us
    pallas_call x1, Pallas kernels, cols_product(): pl.pallas_call(lambda *refs: cols_kernel(column_count, *refs), out_shape=...  0.73 us
  transfers between devices with their start and end apart: 12, of which 9 were waited for; matrix products, arithmetic and copies ran while one was open for 0% of the time, Pallas kernels for 9%

profile of v7, /device:TPU:0, one launch (start us, length us, event | category | flops | bytes accessed | tf_op | source)
XLA Modules:
  0.0 31.8 jit_solution(14418802699914091171)
XLA Ops:
  0.6 2.4 %collective-permute-start = (f32[16,512]{1,0:T(8,128)}, f32[16,512]{1,0:T(8,128)S(1)}, u32[]{:S(2)}, u32[]{:S(2)}) collective-permute-start(f32[16,512]{1,0:T(8,128)} %refs_4_.1), channel_id=1, source_target_pairs={{0,3},{1,2},{2,1},{3,0},{4,7},{5,6},{6,5},{7,4},{8,11},{9,10},{10,... | collective-permute-start | bytes 98312 | tf_op jit(solution)/shard_map/ppermute | solution.py:276
  3.1 0.6 %collective-permute-start.1 = (f32[16,512]{1,0:T(8,128)}, f32[16,512]{1,0:T(8,128)S(1)}, u32[]{:S(2)}, u32[]{:S(2)}) collective-permute-start(f32[16,512]{1,0:T(8,128)} %refs_4_.1), channel_id=1, source_target_pairs={{0,2},{1,3},{2,0},{3,1},{4,6},{5,7},{6,4},{7,5},{8,10},{9,11},{10,... | collective-permute-start | bytes 98312 | tf_op jit(solution)/shard_map/ppermute | solution.py:276
  3.7 0.0 collective-permute-start.2
  3.8 0.0 copy-start
  3.8 2.7 %shard_map.50 = (bf16[16,256,256]{2,1,0:T(8,128)(2,1)S(1)}, bf16[16,256,256]{2,1,0:T(8,128)(2,1)S(1)}, bf16[16,256,256]{2,1,0:T(8,128)(2,1)S(1)}, bf16[5,256,256]{2,1,0:T(8,128)(2,1)S(1)}, s32[16]{0:T(128)S(4)}) custom-call(f32[16,256,256]{2,1,0:T(8,128)} %bitcast.2, s32[16]{0:T(128)} %bitcast.3), custom_call_target="tpu_custom_call" | custom-call | flops 3145728 | bytes 8388608 | tf_op jit(solution)/shard_map/pallas_call | solution.py:61
  6.5 0.0 collective-permute-done.refs_5_
  6.5 0.7 %collective-permute-done.1.refs_6_ = f32[16,512]{1,0:T(8,128)S(1)} collective-permute-done((f32[16,512]{1,0:T(8,128)}, f32[16,512]{1,0:T(8,128)S(1)}, u32[]{:S(2)}, u32[]{:S(2)}) %collective-permute-start.1) | collective-permute-done | bytes 32800 | tf_op jit(solution)/shard_map/ppermute | solution.py:276
  7.3 0.0 collective-permute-done.2.refs_7_
  7.3 0.0 copy-done
  7.3 0.9 %shard_map.51.refs_3_ = f32[4,16,256]{2,1,0:T(8,128)S(1)} custom-call(s32[16]{0:T(128)S(4)} %get-tuple-element.12.refs_0_, bf16[16,256,256]{2,1,0:T(8,128)(2,1)S(1)} %get-tuple-element.15.refs_1_, bf16[16,256,256]{2,1,0:T(8,128)(2,1)S(1)} %get-tuple-element.14.refs_2_, bf16[5,256,256]{2,1,0:T(8,128)(2,1)S(1)} %get-tuple-element.16.refs_3_, ...), custom_call_target="tpu_custom_call" | custom-call | tf_op jit(solution)/shard_map/pallas_call | solution.py:116
  8.2 3.6 %collective-permute-start.3 = (f32[4,16,256]{2,1,0:T(8,128)S(1)}, f32[4,16,256]{2,1,0:T(8,128)S(1)}, u32[]{:S(2)}, u32[]{:S(2)}) collective-permute-start(f32[4,16,256]{2,1,0:T(8,128)S(1)} %shard_map.51.refs_3_), channel_id=1, source_target_pairs={{0,12},{1,9},{2,14},{3,11},{4,8},{5,13},{6,10},{7,15},{8,4},{9,1},... | collective-permute-start | bytes 196616 | tf_op jit(solution)/shard_map/ppermute | solution.py:296
  11.8 0.0 collective-permute-start.4
  11.8 0.8 %collective-permute-start.5 = (f32[4,16,256]{2,1,0:T(8,128)S(1)}, f32[4,16,256]{2,1,0:T(8,128)S(1)}, u32[]{:S(2)}, u32[]{:S(2)}) collective-permute-start(f32[4,16,256]{2,1,0:T(8,128)S(1)} %shard_map.51.refs_3_), channel_id=1, source_target_pairs={{0,8},{1,5},{2,10},{3,7},{4,12},{5,1},{6,14},{7,3},{8,0},{9,13},{1... | collective-permute-start | bytes 196616 | tf_op jit(solution)/shard_map/ppermute | solution.py:296
  12.6 1.8 %collective-permute-done.3.refs_4_ = f32[4,16,256]{2,1,0:T(8,128)S(1)} collective-permute-done((f32[4,16,256]{2,1,0:T(8,128)S(1)}, f32[4,16,256]{2,1,0:T(8,128)S(1)}, u32[]{:S(2)}, u32[]{:S(2)}) %collective-permute-start.3) | collective-permute-done | bytes 65568 | tf_op jit(solution)/shard_map/ppermute | solution.py:296
  14.3 2.8 %collective-permute-done.4.refs_5_ = f32[4,16,256]{2,1,0:T(8,128)S(1)} collective-permute-done((f32[4,16,256]{2,1,0:T(8,128)S(1)}, f32[4,16,256]{2,1,0:T(8,128)S(1)}, u32[]{:S(2)}, u32[]{:S(2)}) %collective-permute-start.4) | collective-permute-done | bytes 65568 | tf_op jit(solution)/shard_map/ppermute | solution.py:296
  17.1 0.0 collective-permute-done.5.refs_6_
  17.1 0.7 %shard_map.52 = f32[8,16,256]{2,1,0:T(8,128)S(1)} custom-call(s32[16]{0:T(128)S(4)} %get-tuple-element.12.refs_0_, bf16[16,256,256]{2,1,0:T(8,128)(2,1)S(1)} %get-tuple-element.13.refs_1_, bf16[16,256,256]{2,1,0:T(8,128)(2,1)S(1)} %get-tuple-element.14.refs_2_, f32[4,16,256]{2,1,0:T(8,128)S(1)} %shard_map.51.refs_3_, ...), custom_call_target="tpu_custom_call" | custom-call | tf_op jit(solution)/shard_map/pallas_call | solution.py:143
  17.8 0.0 collective-permute-start.6
  17.8 1.3 %collective-permute-done.6 = f32[8,16,256]{2,1,0:T(8,128)S(1)} collective-permute-done((f32[8,16,256]{2,1,0:T(8,128)S(1)}, f32[8,16,256]{2,1,0:T(8,128)S(1)}, u32[]{:S(2)}, u32[]{:S(2)}) %collective-permute-start.6) | collective-permute-done | bytes 131104 | tf_op jit(solution)/shard_map/ppermute | solution.py:276
  19.2 1.9 %collective-permute-start.7 = (f32[8,16,256]{2,1,0:T(8,128)S(1)}, f32[8,16,256]{2,1,0:T(8,128)S(1)}, u32[]{:S(2)}, u32[]{:S(2)}) collective-permute-start(f32[8,16,256]{2,1,0:T(8,128)S(1)} %add.3.refs_0_), channel_id=1, source_target_pairs={{0,4},{1,3},{2,6},{3,1},{4,0},{5,7},{6,2},{7,5},{8,12},{9,11},{10,... | collective-permute-start | bytes 393224 | tf_op jit(solution)/shard_map/ppermute | solution.py:296
  21.1 3.1 %collective-permute-done.7.refs_1_ = f32[8,16,256]{2,1,0:T(8,128)S(1)} collective-permute-done((f32[8,16,256]{2,1,0:T(8,128)S(1)}, f32[8,16,256]{2,1,0:T(8,128)S(1)}, u32[]{:S(2)}, u32[]{:S(2)}) %collective-permute-start.7) | collective-permute-done | bytes 131104 | tf_op jit(solution)/shard_map/ppermute | solution.py:296
  24.2 1.1 %collective-permute-start.8 = (f32[16,16]{1,0:T(8,128)S(1)}, f32[16,16]{1,0:T(8,128)S(1)}, u32[]{:S(2)}, u32[]{:S(2)}) collective-permute-start(f32[16,16]{1,0:T(8,128)S(1)} %get-tuple-element.19.refs_2_), channel_id=1, source_target_pairs={{0,2},{1,5},{2,0},{3,7},{4,6},{5,13},{6,4},{7,15},{8,10},{9,1},{10... | collective-permute-start | bytes 3080 | tf_op jit(solution)/shard_map/ppermute | solution.py:296
  25.4 0.9 %collective-permute-start.9 = (f32[16,16]{1,0:T(8,128)S(1)}, f32[16,16]{1,0:T(8,128)S(1)}, u32[]{:S(2)}, u32[]{:S(2)}) collective-permute-start(f32[16,16]{1,0:T(8,128)S(1)} %get-tuple-element.19.refs_2_), channel_id=1, source_target_pairs={{0,2},{1,13},{2,0},{3,15},{4,6},{5,9},{6,4},{7,11},{8,10},{9,5},{1... | collective-permute-start | bytes 3080 | tf_op jit(solution)/shard_map/ppermute | solution.py:296
  26.3 1.1 %collective-permute-start.10 = (f32[16,16]{1,0:T(8,128)S(1)}, f32[16,16]{1,0:T(8,128)S(1)}, u32[]{:S(2)}, u32[]{:S(2)}) collective-permute-start(f32[16,16]{1,0:T(8,128)S(1)} %get-tuple-element.19.refs_2_), channel_id=1, source_target_pairs={{0,2},{1,9},{2,0},{3,11},{4,6},{5,1},{6,4},{7,3},{8,10},{9,13},{10... | collective-permute-start | bytes 3080 | tf_op jit(solution)/shard_map/ppermute | solution.py:296
  27.4 0.5 %collective-permute-done.8.refs_3_ = f32[16,16]{1,0:T(8,128)S(1)} collective-permute-done((f32[16,16]{1,0:T(8,128)S(1)}, f32[16,16]{1,0:T(8,128)S(1)}, u32[]{:S(2)}, u32[]{:S(2)}) %collective-permute-start.8) | collective-permute-done | bytes 1056 | tf_op jit(solution)/shard_map/ppermute | solution.py:296
  27.9 1.1 %collective-permute-done.9.refs_4_ = f32[16,16]{1,0:T(8,128)S(1)} collective-permute-done((f32[16,16]{1,0:T(8,128)S(1)}, f32[16,16]{1,0:T(8,128)S(1)}, u32[]{:S(2)}, u32[]{:S(2)}) %collective-permute-start.9) | collective-permute-done | bytes 1056 | tf_op jit(solution)/shard_map/ppermute | solution.py:296
  29.0 0.9 %collective-permute-done.10.refs_5_ = f32[16,16]{1,0:T(8,128)S(1)} collective-permute-done((f32[16,16]{1,0:T(8,128)S(1)}, f32[16,16]{1,0:T(8,128)S(1)}, u32[]{:S(2)}, u32[]{:S(2)}) %collective-permute-start.10) | collective-permute-done | bytes 1056 | tf_op jit(solution)/shard_map/ppermute | solution.py:296
  29.9 0.2 collective-permute-start.11
  30.1 1.0 %collective-permute-done.11.far_ref = f32[16,640]{1,0:T(8,128)S(1)} collective-permute-done((f32[16,640]{1,0:T(8,128)S(1)}, f32[16,640]{1,0:T(8,128)S(1)}, u32[]{:S(2)}, u32[]{:S(2)}) %collective-permute-start.11) | collective-permute-done | bytes 40992 | tf_op jit(solution)/shard_map/ppermute | solution.py:276
  31.1 0.6 %shard_map.55 = (f32[16,512]{1,0:T(8,128)}, f32[16,16]{1,0:T(8,128)}) custom-call(f32[16,512]{1,0:T(8,128)S(1)} %get-tuple-element.20.mine_ref, f32[16,640]{1,0:T(8,128)S(1)} %get-tuple-element.21.other_ref, f32[16,640]{1,0:T(8,128)S(1)} %collective-permute-done.11.far_ref), custom_call_target="tpu_custom_call" | custom-call | tf_op jit(solution)/shard_map/pallas_call | solution.py:262
  (3 shorter events, 0.0 us)
Async XLA Ops:
  0.6 5.9 %collective-permute-start = (f32[16,512]{1,0:T(8,128)}, f32[16,512]{1,0:T(8,128)S(1)}, u32[]{:S(2)}, u32[]{:S(2)}) collective-permute-start(f32[16,512]{1,0:T(8,128)} %refs_4_.1), channel_id=1, source_target_pairs={{0,3},{1,2},{2,1},{3,0},{4,7},{5,6},{6,5},{7,4},{8,11},{9,10},{10,... | collective-permute-start | bytes 98312 | tf_op jit(solution)/shard_map/ppermute | solution.py:276
  3.1 4.2 %collective-permute-start.1 = (f32[16,512]{1,0:T(8,128)}, f32[16,512]{1,0:T(8,128)S(1)}, u32[]{:S(2)}, u32[]{:S(2)}) collective-permute-start(f32[16,512]{1,0:T(8,128)} %refs_4_.1), channel_id=1, source_target_pairs={{0,2},{1,3},{2,0},{3,1},{4,6},{5,7},{6,4},{7,5},{8,10},{9,11},{10,... | collective-permute-start | bytes 98312 | tf_op jit(solution)/shard_map/ppermute | solution.py:276
  3.7 3.5 %collective-permute-start.2 = (f32[16,512]{1,0:T(8,128)}, f32[16,512]{1,0:T(8,128)S(1)}, u32[]{:S(2)}, u32[]{:S(2)}) collective-permute-start(f32[16,512]{1,0:T(8,128)} %refs_4_.1), channel_id=1, source_target_pairs={{0,1},{1,0},{2,3},{3,2},{4,5},{5,4},{6,7},{7,6},{8,9},{9,8},{10,11... | collective-permute-start | bytes 98312 | tf_op jit(solution)/shard_map/ppermute | solution.py:276
  3.8 3.5 %copy-start = (f32[16,512]{1,0:T(8,128)S(1)}, f32[16,512]{1,0:T(8,128)}, u32[]{:S(2)}) copy-start(f32[16,512]{1,0:T(8,128)} %refs_4_.1) | copy-start | bytes 98308
  8.2 6.2 %collective-permute-start.3 = (f32[4,16,256]{2,1,0:T(8,128)S(1)}, f32[4,16,256]{2,1,0:T(8,128)S(1)}, u32[]{:S(2)}, u32[]{:S(2)}) collective-permute-start(f32[4,16,256]{2,1,0:T(8,128)S(1)} %shard_map.51.refs_3_), channel_id=1, source_target_pairs={{0,12},{1,9},{2,14},{3,11},{4,8},{5,13},{6,10},{7,15},{8,4},{9,1},... | collective-permute-start | bytes 196616 | tf_op jit(solution)/shard_map/ppermute | solution.py:296
  11.8 5.3 %collective-permute-start.4 = (f32[4,16,256]{2,1,0:T(8,128)S(1)}, f32[4,16,256]{2,1,0:T(8,128)S(1)}, u32[]{:S(2)}, u32[]{:S(2)}) collective-permute-start(f32[4,16,256]{2,1,0:T(8,128)S(1)} %shard_map.51.refs_3_), channel_id=1, source_target_pairs={{0,4},{1,13},{2,6},{3,15},{4,0},{5,9},{6,2},{7,11},{8,12},{9,5},{1... | collective-permute-start | bytes 196616 | tf_op jit(solution)/shard_map/ppermute | solution.py:296
  11.8 5.3 %collective-permute-start.5 = (f32[4,16,256]{2,1,0:T(8,128)S(1)}, f32[4,16,256]{2,1,0:T(8,128)S(1)}, u32[]{:S(2)}, u32[]{:S(2)}) collective-permute-start(f32[4,16,256]{2,1,0:T(8,128)S(1)} %shard_map.51.refs_3_), channel_id=1, source_target_pairs={{0,8},{1,5},{2,10},{3,7},{4,12},{5,1},{6,14},{7,3},{8,0},{9,13},{1... | collective-permute-start | bytes 196616 | tf_op jit(solution)/shard_map/ppermute | solution.py:296
  17.8 1.4 %collective-permute-start.6 = (f32[8,16,256]{2,1,0:T(8,128)S(1)}, f32[8,16,256]{2,1,0:T(8,128)S(1)}, u32[]{:S(2)}, u32[]{:S(2)}) collective-permute-start(f32[8,16,256]{2,1,0:T(8,128)S(1)} %shard_map.52), channel_id=1, source_target_pairs={{0,1},{1,0},{2,3},{3,2},{4,5},{5,4},{6,7},{7,6},{8,9},{9,8},{10,11... | collective-permute-start | bytes 393224 | tf_op jit(solution)/shard_map/ppermute | solution.py:276
  19.2 5.0 %collective-permute-start.7 = (f32[8,16,256]{2,1,0:T(8,128)S(1)}, f32[8,16,256]{2,1,0:T(8,128)S(1)}, u32[]{:S(2)}, u32[]{:S(2)}) collective-permute-start(f32[8,16,256]{2,1,0:T(8,128)S(1)} %add.3.refs_0_), channel_id=1, source_target_pairs={{0,4},{1,3},{2,6},{3,1},{4,0},{5,7},{6,2},{7,5},{8,12},{9,11},{10,... | collective-permute-start | bytes 393224 | tf_op jit(solution)/shard_map/ppermute | solution.py:296
  24.2 3.7 %collective-permute-start.8 = (f32[16,16]{1,0:T(8,128)S(1)}, f32[16,16]{1,0:T(8,128)S(1)}, u32[]{:S(2)}, u32[]{:S(2)}) collective-permute-start(f32[16,16]{1,0:T(8,128)S(1)} %get-tuple-element.19.refs_2_), channel_id=1, source_target_pairs={{0,2},{1,5},{2,0},{3,7},{4,6},{5,13},{6,4},{7,15},{8,10},{9,1},{10... | collective-permute-start | bytes 3080 | tf_op jit(solution)/shard_map/ppermute | solution.py:296
  25.4 3.7 %collective-permute-start.9 = (f32[16,16]{1,0:T(8,128)S(1)}, f32[16,16]{1,0:T(8,128)S(1)}, u32[]{:S(2)}, u32[]{:S(2)}) collective-permute-start(f32[16,16]{1,0:T(8,128)S(1)} %get-tuple-element.19.refs_2_), channel_id=1, source_target_pairs={{0,2},{1,13},{2,0},{3,15},{4,6},{5,9},{6,4},{7,11},{8,10},{9,5},{1... | collective-permute-start | bytes 3080 | tf_op jit(solution)/shard_map/ppermute | solution.py:296
  26.3 3.7 %collective-permute-start.10 = (f32[16,16]{1,0:T(8,128)S(1)}, f32[16,16]{1,0:T(8,128)S(1)}, u32[]{:S(2)}, u32[]{:S(2)}) collective-permute-start(f32[16,16]{1,0:T(8,128)S(1)} %get-tuple-element.19.refs_2_), channel_id=1, source_target_pairs={{0,2},{1,9},{2,0},{3,11},{4,6},{5,1},{6,4},{7,3},{8,10},{9,13},{10... | collective-permute-start | bytes 3080 | tf_op jit(solution)/shard_map/ppermute | solution.py:296
  29.9 1.2 %collective-permute-start.11 = (f32[16,640]{1,0:T(8,128)S(1)}, f32[16,640]{1,0:T(8,128)S(1)}, u32[]{:S(2)}, u32[]{:S(2)}) collective-permute-start(f32[16,640]{1,0:T(8,128)S(1)} %get-tuple-element.21.other_ref), channel_id=1, source_target_pairs={{0,1},{1,0},{2,3},{3,2},{4,5},{5,4},{6,7},{7,6},{8,9},{9,8},{10,11... | collective-permute-start | bytes 122888 | tf_op jit(solution)/shard_map/ppermute | solution.py:276

commit v8 on v7

--- a/solution.py
+++ b/solution.py
@@ -159,9 +159,11 @@
         for c in range(a_ref.shape[0]):
             z = a_ref[c] + b_ref[c]
             z_ref[c] = z
-            g = lax.dot_general(z, z, NT, precision=lax.Precision.HIGHEST, preferred_element_type=jnp.float32)
+            both = jnp.concatenate(halves(z), axis=0)
+            g = lax.dot_general(both, both, NT, preferred_element_type=jnp.float32)
             total = g if total is None else total + g
-        gram_ref[...] = total
+        n = gram_ref.shape[0]
+        gram_ref[...] = total[:n, :n] + total[:n, n:] + total[n:, :n] + total[n:, n:]
         me = lax.axis_index(GROUP)
         count = mine_ref.shape[0]
         for h in range(count):

time: 31.9 us -> 31.9 us (level)
  no operation moved by 1% of the time
where the time goes in v8:
time: 31.9 us; the launch traced here: 31.8 us
  waiting for transfers between devices  13.3 us (42%)
  starting transfers between devices  12.8 us (40%)
  Pallas kernels  5 us (16%)
  between operations  0.67 us (2%)
    ppermute x7, waiting for transfers between devices, exchange(): return lax.ppermute(x, ('col', 'row', 'sub'), pairs)  10.1 us
    ppermute x7, starting transfers between devices, exchange(): return lax.ppermute(x, ('col', 'row', 'sub'), pairs)  9.51 us
    ppermute x5, starting transfers between devices, partner(): return lax.ppermute(x, axes, [(i, i ^ k) for i in range(n)])  3.27 us
    ppermute x5, waiting for transfers between devices, partner(): return lax.ppermute(x, axes, [(i, i ^ k) for i in range(n)])  3.16 us
    pallas_call x1, Pallas kernels, split_blocks(): pl.pallas_call(split_kernel, out_shape=(pltpu.VMEM(blocks.shape, jnp.bflo...  2.75 us
    pallas_call x1, Pallas kernels, rows_product(): pl.pallas_call(lambda *refs: rows_kernel(steps, *refs), out_shape=jax.Sha...  0.89 us
    pallas_call x1, Pallas kernels, cols_product(): pl.pallas_call(lambda *refs: cols_kernel(column_count, *refs), out_shape=...  0.73 us
  transfers between devices with their start and end apart: 12, of which 9 were waited for; matrix products, arithmetic and copies ran while one was open for 0% of the time, Pallas kernels for 9%

profile of v8, /device:TPU:0, one launch (start us, length us, event | category | flops | bytes accessed | tf_op | source)
XLA Modules:
  0.0 31.8 jit_solution(5165495240948827532)
XLA Ops:
  0.6 2.4 %collective-permute-start = (f32[16,512]{1,0:T(8,128)}, f32[16,512]{1,0:T(8,128)S(1)}, u32[]{:S(2)}, u32[]{:S(2)}) collective-permute-start(f32[16,512]{1,0:T(8,128)} %refs_4_.1), channel_id=1, source_target_pairs={{0,3},{1,2},{2,1},{3,0},{4,7},{5,6},{6,5},{7,4},{8,11},{9,10},{10,... | collective-permute-start | bytes 98312 | tf_op jit(solution)/shard_map/ppermute | solution.py:278
  3.1 0.6 %collective-permute-start.1 = (f32[16,512]{1,0:T(8,128)}, f32[16,512]{1,0:T(8,128)S(1)}, u32[]{:S(2)}, u32[]{:S(2)}) collective-permute-start(f32[16,512]{1,0:T(8,128)} %refs_4_.1), channel_id=1, source_target_pairs={{0,2},{1,3},{2,0},{3,1},{4,6},{5,7},{6,4},{7,5},{8,10},{9,11},{10,... | collective-permute-start | bytes 98312 | tf_op jit(solution)/shard_map/ppermute | solution.py:278
  3.7 0.0 collective-permute-start.2
  3.8 0.0 copy-start
  3.8 2.7 %shard_map.50 = (bf16[16,256,256]{2,1,0:T(8,128)(2,1)S(1)}, bf16[16,256,256]{2,1,0:T(8,128)(2,1)S(1)}, bf16[16,256,256]{2,1,0:T(8,128)(2,1)S(1)}, bf16[5,256,256]{2,1,0:T(8,128)(2,1)S(1)}, s32[16]{0:T(128)S(4)}) custom-call(f32[16,256,256]{2,1,0:T(8,128)} %bitcast.2, s32[16]{0:T(128)} %bitcast.3), custom_call_target="tpu_custom_call" | custom-call | flops 3145728 | bytes 8388608 | tf_op jit(solution)/shard_map/pallas_call | solution.py:61
  6.5 0.0 collective-permute-done.refs_5_
  6.5 0.7 %collective-permute-done.1.refs_6_ = f32[16,512]{1,0:T(8,128)S(1)} collective-permute-done((f32[16,512]{1,0:T(8,128)}, f32[16,512]{1,0:T(8,128)S(1)}, u32[]{:S(2)}, u32[]{:S(2)}) %collective-permute-start.1) | collective-permute-done | bytes 32800 | tf_op jit(solution)/shard_map/ppermute | solution.py:278
  7.3 0.0 collective-permute-done.2.refs_7_
  7.3 0.0 copy-done
  7.3 0.9 %shard_map.51.refs_3_ = f32[4,16,256]{2,1,0:T(8,128)S(1)} custom-call(s32[16]{0:T(128)S(4)} %get-tuple-element.12.refs_0_, bf16[16,256,256]{2,1,0:T(8,128)(2,1)S(1)} %get-tuple-element.15.refs_1_, bf16[16,256,256]{2,1,0:T(8,128)(2,1)S(1)} %get-tuple-element.14.refs_2_, bf16[5,256,256]{2,1,0:T(8,128)(2,1)S(1)} %get-tuple-element.16.refs_3_, ...), custom_call_target="tpu_custom_call" | custom-call | tf_op jit(solution)/shard_map/pallas_call | solution.py:116
  8.1 3.6 %collective-permute-start.3 = (f32[4,16,256]{2,1,0:T(8,128)S(1)}, f32[4,16,256]{2,1,0:T(8,128)S(1)}, u32[]{:S(2)}, u32[]{:S(2)}) collective-permute-start(f32[4,16,256]{2,1,0:T(8,128)S(1)} %shard_map.51.refs_3_), channel_id=1, source_target_pairs={{0,12},{1,9},{2,14},{3,11},{4,8},{5,13},{6,10},{7,15},{8,4},{9,1},... | collective-permute-start | bytes 196616 | tf_op jit(solution)/shard_map/ppermute | solution.py:298
  11.8 0.0 collective-permute-start.4
  11.8 0.8 %collective-permute-start.5 = (f32[4,16,256]{2,1,0:T(8,128)S(1)}, f32[4,16,256]{2,1,0:T(8,128)S(1)}, u32[]{:S(2)}, u32[]{:S(2)}) collective-permute-start(f32[4,16,256]{2,1,0:T(8,128)S(1)} %shard_map.51.refs_3_), channel_id=1, source_target_pairs={{0,8},{1,5},{2,10},{3,7},{4,12},{5,1},{6,14},{7,3},{8,0},{9,13},{1... | collective-permute-start | bytes 196616 | tf_op jit(solution)/shard_map/ppermute | solution.py:298
  12.6 1.8 %collective-permute-done.3.refs_4_ = f32[4,16,256]{2,1,0:T(8,128)S(1)} collective-permute-done((f32[4,16,256]{2,1,0:T(8,128)S(1)}, f32[4,16,256]{2,1,0:T(8,128)S(1)}, u32[]{:S(2)}, u32[]{:S(2)}) %collective-permute-start.3) | collective-permute-done | bytes 65568 | tf_op jit(solution)/shard_map/ppermute | solution.py:298
  14.3 2.8 %collective-permute-done.4.refs_5_ = f32[4,16,256]{2,1,0:T(8,128)S(1)} collective-permute-done((f32[4,16,256]{2,1,0:T(8,128)S(1)}, f32[4,16,256]{2,1,0:T(8,128)S(1)}, u32[]{:S(2)}, u32[]{:S(2)}) %collective-permute-start.4) | collective-permute-done | bytes 65568 | tf_op jit(solution)/shard_map/ppermute | solution.py:298
  17.1 0.0 collective-permute-done.5.refs_6_
  17.1 0.7 %shard_map.52 = f32[8,16,256]{2,1,0:T(8,128)S(1)} custom-call(s32[16]{0:T(128)S(4)} %get-tuple-element.12.refs_0_, bf16[16,256,256]{2,1,0:T(8,128)(2,1)S(1)} %get-tuple-element.13.refs_1_, bf16[16,256,256]{2,1,0:T(8,128)(2,1)S(1)} %get-tuple-element.14.refs_2_, f32[4,16,256]{2,1,0:T(8,128)S(1)} %shard_map.51.refs_3_, ...), custom_call_target="tpu_custom_call" | custom-call | tf_op jit(solution)/shard_map/pallas_call | solution.py:143
  17.8 0.0 collective-permute-start.6
  17.8 1.3 %collective-permute-done.6 = f32[8,16,256]{2,1,0:T(8,128)S(1)} collective-permute-done((f32[8,16,256]{2,1,0:T(8,128)S(1)}, f32[8,16,256]{2,1,0:T(8,128)S(1)}, u32[]{:S(2)}, u32[]{:S(2)}) %collective-permute-start.6) | collective-permute-done | bytes 131104 | tf_op jit(solution)/shard_map/ppermute | solution.py:278
  19.2 1.9 %collective-permute-start.7 = (f32[8,16,256]{2,1,0:T(8,128)S(1)}, f32[8,16,256]{2,1,0:T(8,128)S(1)}, u32[]{:S(2)}, u32[]{:S(2)}) collective-permute-start(f32[8,16,256]{2,1,0:T(8,128)S(1)} %add.3.refs_0_), channel_id=1, source_target_pairs={{0,4},{1,3},{2,6},{3,1},{4,0},{5,7},{6,2},{7,5},{8,12},{9,11},{10,... | collective-permute-start | bytes 393224 | tf_op jit(solution)/shard_map/ppermute | solution.py:298
  21.1 3.1 %collective-permute-done.7.refs_1_ = f32[8,16,256]{2,1,0:T(8,128)S(1)} collective-permute-done((f32[8,16,256]{2,1,0:T(8,128)S(1)}, f32[8,16,256]{2,1,0:T(8,128)S(1)}, u32[]{:S(2)}, u32[]{:S(2)}) %collective-permute-start.7) | collective-permute-done | bytes 131104 | tf_op jit(solution)/shard_map/ppermute | solution.py:298
  24.2 1.1 %collective-permute-start.8 = (f32[16,16]{1,0:T(8,128)S(1)}, f32[16,16]{1,0:T(8,128)S(1)}, u32[]{:S(2)}, u32[]{:S(2)}) collective-permute-start(f32[16,16]{1,0:T(8,128)S(1)} %get-tuple-element.19.refs_2_), channel_id=1, source_target_pairs={{0,2},{1,5},{2,0},{3,7},{4,6},{5,13},{6,4},{7,15},{8,10},{9,1},{10... | collective-permute-start | bytes 3080 | tf_op jit(solution)/shard_map/ppermute | solution.py:298
  25.4 0.9 %collective-permute-start.9 = (f32[16,16]{1,0:T(8,128)S(1)}, f32[16,16]{1,0:T(8,128)S(1)}, u32[]{:S(2)}, u32[]{:S(2)}) collective-permute-start(f32[16,16]{1,0:T(8,128)S(1)} %get-tuple-element.19.refs_2_), channel_id=1, source_target_pairs={{0,2},{1,13},{2,0},{3,15},{4,6},{5,9},{6,4},{7,11},{8,10},{9,5},{1... | collective-permute-start | bytes 3080 | tf_op jit(solution)/shard_map/ppermute | solution.py:298
  26.3 1.1 %collective-permute-start.10 = (f32[16,16]{1,0:T(8,128)S(1)}, f32[16,16]{1,0:T(8,128)S(1)}, u32[]{:S(2)}, u32[]{:S(2)}) collective-permute-start(f32[16,16]{1,0:T(8,128)S(1)} %get-tuple-element.19.refs_2_), channel_id=1, source_target_pairs={{0,2},{1,9},{2,0},{3,11},{4,6},{5,1},{6,4},{7,3},{8,10},{9,13},{10... | collective-permute-start | bytes 3080 | tf_op jit(solution)/shard_map/ppermute | solution.py:298
  27.4 0.5 %collective-permute-done.8.refs_3_ = f32[16,16]{1,0:T(8,128)S(1)} collective-permute-done((f32[16,16]{1,0:T(8,128)S(1)}, f32[16,16]{1,0:T(8,128)S(1)}, u32[]{:S(2)}, u32[]{:S(2)}) %collective-permute-start.8) | collective-permute-done | bytes 1056 | tf_op jit(solution)/shard_map/ppermute | solution.py:298
  27.9 1.1 %collective-permute-done.9.refs_4_ = f32[16,16]{1,0:T(8,128)S(1)} collective-permute-done((f32[16,16]{1,0:T(8,128)S(1)}, f32[16,16]{1,0:T(8,128)S(1)}, u32[]{:S(2)}, u32[]{:S(2)}) %collective-permute-start.9) | collective-permute-done | bytes 1056 | tf_op jit(solution)/shard_map/ppermute | solution.py:298
  29.0 0.9 %collective-permute-done.10.refs_5_ = f32[16,16]{1,0:T(8,128)S(1)} collective-permute-done((f32[16,16]{1,0:T(8,128)S(1)}, f32[16,16]{1,0:T(8,128)S(1)}, u32[]{:S(2)}, u32[]{:S(2)}) %collective-permute-start.10) | collective-permute-done | bytes 1056 | tf_op jit(solution)/shard_map/ppermute | solution.py:298
  29.9 0.1 collective-permute-start.11
  30.1 1.1 %collective-permute-done.11.far_ref = f32[16,640]{1,0:T(8,128)S(1)} collective-permute-done((f32[16,640]{1,0:T(8,128)S(1)}, f32[16,640]{1,0:T(8,128)S(1)}, u32[]{:S(2)}, u32[]{:S(2)}) %collective-permute-start.11) | collective-permute-done | bytes 40992 | tf_op jit(solution)/shard_map/ppermute | solution.py:278
  31.1 0.6 %shard_map.55 = (f32[16,512]{1,0:T(8,128)}, f32[16,16]{1,0:T(8,128)}) custom-call(f32[16,512]{1,0:T(8,128)S(1)} %get-tuple-element.20.mine_ref, f32[16,640]{1,0:T(8,128)S(1)} %get-tuple-element.21.other_ref, f32[16,640]{1,0:T(8,128)S(1)} %collective-permute-done.11.far_ref), custom_call_target="tpu_custom_call" | custom-call | tf_op jit(solution)/shard_map/pallas_call | solution.py:264
  (3 shorter events, 0.0 us)
Async XLA Ops:
  0.6 5.9 %collective-permute-start = (f32[16,512]{1,0:T(8,128)}, f32[16,512]{1,0:T(8,128)S(1)}, u32[]{:S(2)}, u32[]{:S(2)}) collective-permute-start(f32[16,512]{1,0:T(8,128)} %refs_4_.1), channel_id=1, source_target_pairs={{0,3},{1,2},{2,1},{3,0},{4,7},{5,6},{6,5},{7,4},{8,11},{9,10},{10,... | collective-permute-start | bytes 98312 | tf_op jit(solution)/shard_map/ppermute | solution.py:278
  3.1 4.2 %collective-permute-start.1 = (f32[16,512]{1,0:T(8,128)}, f32[16,512]{1,0:T(8,128)S(1)}, u32[]{:S(2)}, u32[]{:S(2)}) collective-permute-start(f32[16,512]{1,0:T(8,128)} %refs_4_.1), channel_id=1, source_target_pairs={{0,2},{1,3},{2,0},{3,1},{4,6},{5,7},{6,4},{7,5},{8,10},{9,11},{10,... | collective-permute-start | bytes 98312 | tf_op jit(solution)/shard_map/ppermute | solution.py:278
  3.7 3.5 %collective-permute-start.2 = (f32[16,512]{1,0:T(8,128)}, f32[16,512]{1,0:T(8,128)S(1)}, u32[]{:S(2)}, u32[]{:S(2)}) collective-permute-start(f32[16,512]{1,0:T(8,128)} %refs_4_.1), channel_id=1, source_target_pairs={{0,1},{1,0},{2,3},{3,2},{4,5},{5,4},{6,7},{7,6},{8,9},{9,8},{10,11... | collective-permute-start | bytes 98312 | tf_op jit(solution)/shard_map/ppermute | solution.py:278
  3.8 3.5 %copy-start = (f32[16,512]{1,0:T(8,128)S(1)}, f32[16,512]{1,0:T(8,128)}, u32[]{:S(2)}) copy-start(f32[16,512]{1,0:T(8,128)} %refs_4_.1) | copy-start | bytes 98308
  8.1 6.2 %collective-permute-start.3 = (f32[4,16,256]{2,1,0:T(8,128)S(1)}, f32[4,16,256]{2,1,0:T(8,128)S(1)}, u32[]{:S(2)}, u32[]{:S(2)}) collective-permute-start(f32[4,16,256]{2,1,0:T(8,128)S(1)} %shard_map.51.refs_3_), channel_id=1, source_target_pairs={{0,12},{1,9},{2,14},{3,11},{4,8},{5,13},{6,10},{7,15},{8,4},{9,1},... | collective-permute-start | bytes 196616 | tf_op jit(solution)/shard_map/ppermute | solution.py:298
  11.8 5.3 %collective-permute-start.4 = (f32[4,16,256]{2,1,0:T(8,128)S(1)}, f32[4,16,256]{2,1,0:T(8,128)S(1)}, u32[]{:S(2)}, u32[]{:S(2)}) collective-permute-start(f32[4,16,256]{2,1,0:T(8,128)S(1)} %shard_map.51.refs_3_), channel_id=1, source_target_pairs={{0,4},{1,13},{2,6},{3,15},{4,0},{5,9},{6,2},{7,11},{8,12},{9,5},{1... | collective-permute-start | bytes 196616 | tf_op jit(solution)/shard_map/ppermute | solution.py:298
  11.8 5.3 %collective-permute-start.5 = (f32[4,16,256]{2,1,0:T(8,128)S(1)}, f32[4,16,256]{2,1,0:T(8,128)S(1)}, u32[]{:S(2)}, u32[]{:S(2)}) collective-permute-start(f32[4,16,256]{2,1,0:T(8,128)S(1)} %shard_map.51.refs_3_), channel_id=1, source_target_pairs={{0,8},{1,5},{2,10},{3,7},{4,12},{5,1},{6,14},{7,3},{8,0},{9,13},{1... | collective-permute-start | bytes 196616 | tf_op jit(solution)/shard_map/ppermute | solution.py:298
  17.8 1.4 %collective-permute-start.6 = (f32[8,16,256]{2,1,0:T(8,128)S(1)}, f32[8,16,256]{2,1,0:T(8,128)S(1)}, u32[]{:S(2)}, u32[]{:S(2)}) collective-permute-start(f32[8,16,256]{2,1,0:T(8,128)S(1)} %shard_map.52), channel_id=1, source_target_pairs={{0,1},{1,0},{2,3},{3,2},{4,5},{5,4},{6,7},{7,6},{8,9},{9,8},{10,11... | collective-permute-start | bytes 393224 | tf_op jit(solution)/shard_map/ppermute | solution.py:278
  19.2 5.0 %collective-permute-start.7 = (f32[8,16,256]{2,1,0:T(8,128)S(1)}, f32[8,16,256]{2,1,0:T(8,128)S(1)}, u32[]{:S(2)}, u32[]{:S(2)}) collective-permute-start(f32[8,16,256]{2,1,0:T(8,128)S(1)} %add.3.refs_0_), channel_id=1, source_target_pairs={{0,4},{1,3},{2,6},{3,1},{4,0},{5,7},{6,2},{7,5},{8,12},{9,11},{10,... | collective-permute-start | bytes 393224 | tf_op jit(solution)/shard_map/ppermute | solution.py:298
  24.2 3.7 %collective-permute-start.8 = (f32[16,16]{1,0:T(8,128)S(1)}, f32[16,16]{1,0:T(8,128)S(1)}, u32[]{:S(2)}, u32[]{:S(2)}) collective-permute-start(f32[16,16]{1,0:T(8,128)S(1)} %get-tuple-element.19.refs_2_), channel_id=1, source_target_pairs={{0,2},{1,5},{2,0},{3,7},{4,6},{5,13},{6,4},{7,15},{8,10},{9,1},{10... | collective-permute-start | bytes 3080 | tf_op jit(solution)/shard_map/ppermute | solution.py:298
  25.4 3.7 %collective-permute-start.9 = (f32[16,16]{1,0:T(8,128)S(1)}, f32[16,16]{1,0:T(8,128)S(1)}, u32[]{:S(2)}, u32[]{:S(2)}) collective-permute-start(f32[16,16]{1,0:T(8,128)S(1)} %get-tuple-element.19.refs_2_), channel_id=1, source_target_pairs={{0,2},{1,13},{2,0},{3,15},{4,6},{5,9},{6,4},{7,11},{8,10},{9,5},{1... | collective-permute-start | bytes 3080 | tf_op jit(solution)/shard_map/ppermute | solution.py:298
  26.3 3.7 %collective-permute-start.10 = (f32[16,16]{1,0:T(8,128)S(1)}, f32[16,16]{1,0:T(8,128)S(1)}, u32[]{:S(2)}, u32[]{:S(2)}) collective-permute-start(f32[16,16]{1,0:T(8,128)S(1)} %get-tuple-element.19.refs_2_), channel_id=1, source_target_pairs={{0,2},{1,9},{2,0},{3,11},{4,6},{5,1},{6,4},{7,3},{8,10},{9,13},{10... | collective-permute-start | bytes 3080 | tf_op jit(solution)/shard_map/ppermute | solution.py:298
  29.9 1.2 %collective-permute-start.11 = (f32[16,640]{1,0:T(8,128)S(1)}, f32[16,640]{1,0:T(8,128)S(1)}, u32[]{:S(2)}, u32[]{:S(2)}) collective-permute-start(f32[16,640]{1,0:T(8,128)S(1)} %get-tuple-element.21.other_ref), channel_id=1, source_target_pairs={{0,1},{1,0},{2,3},{3,2},{4,5},{5,4},{6,7},{7,6},{8,9},{9,8},{10,11... | collective-permute-start | bytes 122888 | tf_op jit(solution)/shard_map/ppermute | solution.py:278
